TPU v7x, 32 devices: a whole 2x2x4 slice. The times are simulated.
32 devices in a mesh: mp: 4 (over x, core), fsdp: 8 (over z, y).
Axes of the slice: x: 2, y: 2, z: 4, core: 2. Of those that a mesh axis runs over, the one named last changes fastest.
Arguments:
- activations: bfloat16 [4, 1024, 8192], P('mp', 'fsdp'), may hold values from -6 to 6
- out_grads: bfloat16 [4, 1024, 7168], P('mp', 'fsdp'), may hold values from -0.29882812 to 0.29882812
- seq_ids: int32 [4, 1024], P('mp', 'fsdp'), may hold values from 0 to 1, as said below
- weights: bfloat16 [4, 32768, 1792], P('mp', 'fsdp'), may hold values from -6 to 6
Outputs:
- merged: bfloat16 [32768, 1792], P('fsdp')
Inputs may be any that keep to these rules, and one draw needn't show every extreme that they name: `seq_ids`: sequence ids never fall along the tokens of a copy; in every copy one of the 2 sequences holds exactly 768 neighbouring tokens and the other the remaining 1024 - 768, in either order.
All inputs are finite; a program needn't handle non-finite values.
Results may differ from a plain program's by a relative error of at most 0.001.
Values may be sent and summed in bfloat16 or wider, within the bound.
No kernel may reach another device: no remote copies, remote signals or barrier semaphores. Data moves between devices by JAX's collectives and lax.ppermute only.
A program may use at most 192 MiB of HBM per device.

v0:
```python
import jax
import jax.numpy as jnp
from jax import lax
from jax.sharding import PartitionSpec as P

F = 7168
SEQS = 2


smoothing = 0.05


def per_device(activations, out_grads, seq_ids, weights):
    devices = lax.axis_size("fsdp")
    col_width = weights.shape[2]
    row_width = weights.shape[1]
    blocks = F // col_width
    row_blocks = devices // blocks
    tok_local = activations.shape[1]
    act_blocks = activations[0].reshape(tok_local, row_blocks, row_width).transpose(1, 0, 2)
    act_send = jnp.tile(act_blocks, (blocks, 1, 1))
    grad_blocks = out_grads[0].reshape(tok_local, blocks, col_width).transpose(1, 0, 2)
    grad_send = jnp.repeat(grad_blocks, row_blocks, axis=0)
    act_all = lax.all_to_all(act_send, "fsdp", split_axis=0, concat_axis=1, tiled=True)[0]
    grad_all = lax.all_to_all(grad_send, "fsdp", split_axis=0, concat_axis=1, tiled=True)[0]
    owners = lax.all_gather(seq_ids[0], "fsdp", axis=0, tiled=True)
    total = owners.shape[0]
    longest = total // SEQS * 3 // 2

    def per_sequence(seq, fisher):
        first = jnp.sum((owners < seq).astype(jnp.int32))
        first = jnp.minimum(first, jnp.int32(total - longest))
        act_window = lax.dynamic_slice_in_dim(act_all, first, longest, 0)
        grad_window = lax.dynamic_slice_in_dim(grad_all, first, longest, 0)
        owner_window = lax.dynamic_slice_in_dim(owners, first, longest, 0)
        masked = jnp.where((owner_window == seq)[:, None], grad_window, jnp.zeros_like(grad_window))
        grad = lax.dot_general(
            act_window, masked, (((0,), (0,)), ((), ())), preferred_element_type=jnp.float32
        )
        return fisher + grad * grad

    fisher = lax.fori_loop(0, SEQS, per_sequence, jnp.zeros((row_width, col_width), jnp.float32))
    prior = fisher / SEQS + smoothing
    numer = prior * weights[0].astype(jnp.float32)
    numer_part, denom_part = (
        lax.psum_scatter(numer, "mp", scatter_dimension=0, tiled=True),
        lax.psum_scatter(prior, "mp", scatter_dimension=0, tiled=True),
    )
    share = (numer_part / denom_part).astype(jnp.bfloat16)
    merged = lax.all_gather(share, "mp", axis=0, tiled=True)
    return merged


def solution(mesh):
    placed = (P("mp", "fsdp", None), P("mp", "fsdp", None), P("mp", "fsdp"), P("mp", "fsdp", None))
    return jax.shard_map(
        per_device, mesh=mesh, in_specs=placed, out_specs=P("fsdp", None), check_vma=False
    )
```

profile of v0, /device:TPU:0, one launch (start us, length us, event | category | flops | bytes accessed | tf_op | source)
XLA Modules:
  0.0 927.6 jit_solution(647836909805855970)
XLA Ops:
  6.5 3.6 reshape_squeeze.7
  10.2 0.2 copy.6
  10.4 2.1 broadcast_in_dim.26
  12.5 7.3 all-to-all-start.1
  19.7 2.8 reshape_squeeze.6
  22.5 2.9 copy.5
  25.4 76.4 %all-to-all-done.1 = bf16[8,128,1792]{2,1,0:T(8,128)(2,1)} async-done(((bf16[8,128,1792]{2,1,0:T(8,128)(2,1)}), bf16[8,128,1792]{2,1,0:T(8,128)(2,1)}, u32[]{:S(2)}, u32[]{:S(2)}) %all-to-all-start.1) | async-done | bytes 3670048 | tf_op jit(solution)/shard_map/all_to_all | solution.py:25
  101.8 4.4 tile.4
  106.2 5.1 all-to-all-start
  111.4 149.2 %all-gather = s32[1,1024]{1,0:T(1,128)S(1)} all-gather(s32[1,128]{1,0:T(1,128)S(1)} %copy-done.1), channel_id=2, replica_groups=mesh['mp'=4,'fsdp'=8] {'fsdp'}, dimensions={1}, use_global_device_ids=true | all-gather | bytes 4608 | tf_op jit(solution)/shard_map/all_gather | solution.py:26
  260.6 32.9 %all-to-all-done = bf16[8,128,4096]{2,1,0:T(8,128)(2,1)} async-done(((bf16[8,128,4096]{2,1,0:T(8,128)(2,1)}), bf16[8,128,4096]{2,1,0:T(8,128)(2,1)}, u32[]{:S(2)}, u32[]{:S(2)}) %all-to-all-start) | async-done | bytes 8388640 | tf_op jit(solution)/shard_map/all_to_all | solution.py:24
  293.5 52.9 %while.14 = (s32[]{:T(128)}, f32[4096,1792]{1,0:T(8,128)}, s32[1024]{0:T(1024)S(1)}, bf16[1024,4096]{1,0:T(8,128)(2,1)}, bf16[1024,1792]{1,0:T(8,128)(2,1)}, /*index=5*/s32[]{:T(128)}, s32[]{:T(128)}, s32[]{:T(128)}, s32[]{:T(128)}) while((s32[]{:T(128)}, f32[4096,1792]{1,0:T(8,128)}, s32[1024]{0:T(1024)S(1)}, ...), condition=%wide.region_2.3_spmd.clone, body=%wide.region_0.2_spmd.clone.sunk | while | flops 11297689600 | bytes 67774632 | solution.py:42
  293.5 0.6 convert_reduce_fusion.2
  294.8 0.1 dynamic-slice_compare_fusion.2
  294.9 20.3 %select_add_fusion.2 = f32[4096,1792]{1,0:T(8,128)} fusion(f32[4096,1792]{1,0:T(8,128)} %get-tuple-element.171, pred[]{:T(512)S(6)} %compare.3, bf16[1024,4096]{1,0:T(8,128)(2,1)} %get-tuple-element.182, s32[]{:T(128)S(6)} %select_n.24, bf16[1024,1792]{1,0:T(8,128)(2,1)} %get-tuple-element.183, pred[768]{0:T(1024)(128)(4,1)S(1)} %dynamic-slice_compare_fusion.2), kind=kOutput, calls=%fused_computation.clone.1 | convolution fusion | flops 11297685504 | bytes 67766528 | tf_op jit(solution)/shard_map/while/body/eval_jaxpr/dot_general | solution.py:37
  315.2 0.6 convert_reduce_fusion.2
  316.6 29.9 %select_add_fusion.2 = f32[4096,1792]{1,0:T(8,128)} fusion(f32[4096,1792]{1,0:T(8,128)} %get-tuple-element.171, pred[]{:T(512)S(6)} %compare.3, bf16[1024,4096]{1,0:T(8,128)(2,1)} %get-tuple-element.182, s32[]{:T(128)S(6)} %select_n.24, bf16[1024,1792]{1,0:T(8,128)(2,1)} %get-tuple-element.183, pred[768]{0:T(1024)(128)(4,1)S(1)} %dynamic-slice_compare_fusion.2), kind=kOutput, calls=%fused_computation.clone.1 | convolution fusion | flops 11297685504 | bytes 67766528 | tf_op jit(solution)/shard_map/while/body/eval_jaxpr/dot_general | solution.py:37
  346.4 33.6 %multiply_add_fusion = (f32[4096,1792]{1,0:T(8,128)}, f32[4096,1792]{1,0:T(8,128)}) fusion(f32[4096,1792]{1,0:T(8,128)} %get-tuple-element.99, bf16[1,4096,1792]{2,1,0:T(8,128)(2,1)} %param.9), kind=kLoop, calls=%fused_computation.11 | loop fusion | flops 29360128 | bytes 102760448 | tf_op jit(solution)/shard_map/add | solution.py:43
  380.1 0.7 reduce-scatter.3.cloned.1.call-update
  380.9 214.2 %reduce-scatter.5.cloned.1.call-done = f32[1024,1792]{1,0:T(8,128)} async-done(((f32[4096,1792]{1,0:T(8,128)}), f32[1024,1792]{1,0:T(8,128)}) %reduce-scatter.5.cloned.1.call-update) | async-done | bytes 7340048 | tf_op jit(solution)/shard_map/reduce_scatter | solution.py:47
  595.1 210.7 %reduce-scatter.3.cloned.1.call-done = f32[1024,1792]{1,0:T(8,128)} async-done(((f32[4096,1792]{1,0:T(8,128)}), f32[1024,1792]{1,0:T(8,128)}) %reduce-scatter.3.cloned.1.call-update) | async-done | bytes 7340048 | tf_op jit(solution)/shard_map/reduce_scatter | solution.py:46
  805.8 8.0 divide_convert_fusion
  813.9 94.2 %all-gather.3.cloned.1.call-done = bf16[4096,1792]{1,0:T(8,128)(2,1)} async-done(((bf16[1024,1792]{1,0:T(8,128)(2,1)}), bf16[4096,1792]{1,0:T(8,128)(2,1)}) %all-gather.3.cloned.1.call-update) | async-done | bytes 14680080 | tf_op jit(solution)/shard_map/all_gather | solution.py:50
  908.0 13.1 %copy.14 = bf16[4096,1792]{1,0:T(8,128)(2,1)} copy(bf16[4096,1792]{1,0:T(8,128)(2,1)} %all-gather.3.cloned.1.call-done) | data formatting | bytes 29360128
  (11 shorter events, 0.2 us)
Async XLA Ops:
  10.3 9.4 %copy-start = (bf16[1,128,8192]{2,1,0:T(8,128)(2,1)S(1)}, bf16[1,128,8192]{2,1,0:T(8,128)(2,1)}, u32[]{:S(2)}) copy-start(bf16[1,128,8192]{2,1,0:T(8,128)(2,1)} %param.6) | copy-start | bytes 6291460
  12.5 89.3 %all-to-all-start.1 = ((bf16[8,128,1792]{2,1,0:T(8,128)(2,1)}), bf16[8,128,1792]{2,1,0:T(8,128)(2,1)}, u32[]{:S(2)}, u32[]{:S(2)}) async-start(bf16[8,128,1792]{2,1,0:T(8,128)(2,1)} %bitcast.11), calls=%async_computation.1 | async-start | bytes 7340032 | tf_op jit(solution)/shard_map/all_to_all | solution.py:25
  106.2 5.1 copy-start.1
  106.2 187.3 %all-to-all-start = ((bf16[8,128,4096]{2,1,0:T(8,128)(2,1)}), bf16[8,128,4096]{2,1,0:T(8,128)(2,1)}, u32[]{:S(2)}, u32[]{:S(2)}) async-start(bf16[8,128,4096]{2,1,0:T(8,128)(2,1)} %bitcast.10), calls=%async_computation | async-start | bytes 16777216 | tf_op jit(solution)/shard_map/all_to_all | solution.py:24
  111.3 483.8 %reduce-scatter.5.cloned.1.call-start = ((), (), s32[]{:S(2)}) async-start(), calls=%async_computation.5 | async-start | bytes 36700160 | tf_op jit(solution)/shard_map/reduce_scatter | solution.py:47
  380.1 425.7 %reduce-scatter.3.cloned.1.call-start = ((), (), s32[]{:S(2)}) async-start(), calls=%async_computation.4 | async-start | bytes 36700160 | tf_op jit(solution)/shard_map/reduce_scatter | solution.py:46
  380.8 527.2 %all-gather.3.cloned.1.call-start = ((), (), s32[]{:S(2)}) async-start(), calls=%async_computation.6 | async-start | bytes 18350080 | tf_op jit(solution)/shard_map/all_gather | solution.py:50
Sparse Core Ops, SparseCore 0:
  380.2 214.8 reduce-scatter.4
  597.8 207.8 reduce-scatter.2
  814.0 93.9 all-gather.2
where the time goes:
time: 928 us
  waiting for transfers between devices  629 us (68%)
  blocking collectives  149 us (16%)
  matrix products  50.2 us (5%)
  other arithmetic  43.1 us (5%)
  local copies, waits for them, and re-layouts  29.1 us (3%)
  between operations  13.2 us (1%)
  starting transfers between devices  12.5 us (1%)
    reduce_scatter x1, waiting for transfers between devices, per_device(): lax.psum_scatter(prior, 'mp', scatter_dimension=0, tiled=True)  214 us
    reduce_scatter x1, waiting for transfers between devices, per_device(): lax.psum_scatter(numer, 'mp', scatter_dimension=0, tiled=True)  211 us
    all_gather x1, blocking collectives, per_device(): owners = lax.all_gather(seq_ids[0], 'fsdp', axis=0, tiled=True)  149 us
    all_gather x1, waiting for transfers between devices, per_device(): merged = lax.all_gather(share, 'mp', axis=0, tiled=True)  94.2 us
    all_to_all x1, waiting for transfers between devices, per_device(): lax.all_to_all(grad_send, 'fsdp', split_axis=0, concat_axis=1, tiled=True)  76.4 us
    dot_general x2, matrix products, per_sequence(): lax.dot_general(act_window, masked, (((0,), (0,)), ((), ())), preferred_e...  50.2 us
    add x1, other arithmetic, per_device(): prior = fisher / SEQS + smoothing  33.6 us
    all_to_all x1, waiting for transfers between devices, per_device(): lax.all_to_all(act_send, 'fsdp', split_axis=0, concat_axis=1, tiled=True)[0]  32.9 us
  transfers between devices with their start and end apart: 5, of which 5 were waited for; matrix products, arithmetic and copies ran while one was open for 1% of the time, Pallas kernels for 0%

commit v1 on v0

v1 whole, which is shorter than its diff:
```python
import functools

import jax
import jax.numpy as jnp
from jax import lax
from jax.experimental import pallas as pl
from jax.experimental.pallas import tpu as pltpu
from jax.sharding import PartitionSpec as P

F = 7168
SEQS = 2
CHUNKS = 2
COL_TILE = 256
ROW_TILE = 256

smoothing = 0.05


def merge_kernel(copies, shards, place_ref, slot_ref, *refs):
    own = refs[0]
    low = refs[1:shards]
    high = refs[shards:2 * shards - 1]
    refs = refs[2 * shards - 1:]
    grads = refs[:copies]
    weights = refs[copies:2 * copies]
    out_ref, acts, sem = refs[2 * copies:]
    rows, tok = own.shape[1], own.shape[2]
    spread = own.shape[0] // copies
    a = place_ref[0]

    def fetch(source, slot):
        return [
            pltpu.make_async_copy(
                source.at[copy * spread + part],
                acts.at[copy, slot, :, pl.ds(part * tok, tok)],
                sem,
            )
            for copy in range(copies)
            for part in range(spread)
        ]

    @pl.when(pl.program_id(0) == 0)
    def _():
        for copy in fetch(own, 0):
            copy.start()
        for slot in range(1, shards):
            @pl.when(a >= slot)
            def _(slot=slot):
                for copy in fetch(low[slot - 1], slot):
                    copy.start()

            @pl.when(a < slot)
            def _(slot=slot):
                for copy in fetch(high[shards - slot - 1], slot):
                    copy.start()
        pltpu.make_async_copy(acts, acts, sem).wait()

    height = min(ROW_TILE, rows)

    def row_tile(step, carry):
        at = pl.ds(pl.multiple_of(step * height, height), height)
        numer = denom = None
        for copy in range(copies):
            sums = []
            lone = slot_ref[copy]
            for first, count in ((0, 1), (1, shards - 1)):
                total = None
                for offset in range(first, first + count):
                    slot = lax.rem(lone + offset, shards)
                    term = jnp.dot(
                        acts[copy, slot, at, :], grads[copy][slot], preferred_element_type=jnp.float32
                    )
                    total = term if total is None else total + term
                sums.append(total)
            prior = (sums[0] * sums[0] + sums[1] * sums[1]) * (1.0 / SEQS) + smoothing
            term = prior * weights[copy][at, :].astype(jnp.float32)
            numer = term if numer is None else numer + term
            denom = prior if denom is None else denom + prior
        out_ref[at, :] = (numer / denom).astype(out_ref.dtype)
        return carry

    lax.fori_loop(0, rows // height, row_tile, 0)


def merge_rows(place, slots, own, low, high, grads, weights):
    copies, shards = len(grads), grads[0].shape[0]
    tok, width = grads[0].shape[1:]
    rows = own.shape[1]
    return pl.pallas_call(
        functools.partial(merge_kernel, copies, shards),
        out_shape=jax.ShapeDtypeStruct((rows, width), jnp.bfloat16),
        grid_spec=pltpu.PrefetchScalarGridSpec(
            num_scalar_prefetch=2,
            grid=(width // COL_TILE,),
            in_specs=[pl.BlockSpec(memory_space=pl.ANY)] * (2 * shards - 1)
            + [pl.BlockSpec((shards, tok, COL_TILE), lambda j, *_: (0, 0, j))] * copies
            + [pl.BlockSpec((rows, COL_TILE), lambda j, *_: (0, j))] * copies,
            out_specs=pl.BlockSpec((rows, COL_TILE), lambda j, *_: (0, j)),
            scratch_shapes=[
                pltpu.VMEM((copies, shards, rows, tok), jnp.bfloat16),
                pltpu.SemaphoreType.DMA,
            ],
        ),
        compiler_params=pltpu.CompilerParams(vmem_limit_bytes=56 * 1024 * 1024),
        cost_estimate=pl.CostEstimate(
            flops=2 * copies * shards * tok * rows * width,
            bytes_accessed=2 * copies * (shards * tok * (rows + width) + rows * width) + 2 * rows * width,
            transcendentals=0,
        ),
    )(place, slots, own, *low, *high, *grads, *weights)


def per_device(activations, out_grads, seq_ids, weights):
    copies = lax.axis_size("mp")
    devices = lax.axis_size("fsdp")
    rows, width = weights.shape[1:]
    blocks = F // width
    spread = devices // blocks
    tok = activations.shape[1]
    share = rows // copies
    part = share // CHUNKS
    m = lax.axis_index("mp")
    i = lax.axis_index("fsdp")
    a, h = i // spread, i % spread

    def to_copy(value, flip):
        return lax.ppermute(value, "mp", [(s, s ^ flip) for s in range(copies)])

    def to_block(value, shift):
        pairs = [(s, (s // spread + shift) % blocks * spread + s % spread) for s in range(devices)]
        return lax.ppermute(value, "fsdp", pairs)

    def to_half(value, shift):
        pairs = [(s, s // spread * spread + (s % spread + shift) % spread) for s in range(devices)]
        return lax.ppermute(value, "fsdp", pairs)

    def to_plane(value, flip, shift):
        pairs = [
            (c * devices + s, (c ^ flip) * devices + s // spread * spread + (s % spread + shift) % spread)
            for c in range(copies)
            for s in range(devices)
        ]
        return lax.ppermute(value, ("mp", "fsdp"), pairs)

    def along(value, step, direction):
        pairs = [
            (s, s + direction * spread)
            for s in range(devices)
            if 0 <= s // spread + direction < blocks and 0 <= s // spread - direction * (step - 1) < blocks
        ]
        return lax.ppermute(value, "fsdp", pairs)

    mine = jnp.where((a == 1) & (h == 0), seq_ids[0, 0], 0)
    second = lax.psum(jnp.where(jnp.arange(copies) == m, mine, 0), ("mp", "fsdp"))
    alone = jnp.where(second == 1, 0, blocks - 1)[m ^ jnp.arange(copies)]
    slots = ((a - alone) % blocks).astype(jnp.int32)
    place = a.astype(jnp.int32)[None]

    grad_blocks = out_grads[0].reshape(tok, blocks, width).transpose(1, 0, 2)
    grads = [None] * copies
    for flip, value in ((0, grad_blocks), (2, to_copy(grad_blocks, 2))):
        block = [lax.dynamic_index_in_dim(value, (a + k) % blocks, 0, keepdims=False) for k in range(blocks)]
        held = jnp.stack([block[0]] + [to_block(block[k], k) for k in range(1, blocks)])
        held = jnp.concatenate([held] + [to_half(held, d) for d in range(1, spread)], axis=1)
        grads[flip] = held
        grads[flip ^ 1] = to_copy(held, 1)

    acts = activations[0].T.reshape(spread, copies, share, tok)
    shard = []
    for flip in range(copies):
        for d in range(spread):
            piece = lax.dynamic_slice(acts, ((h + d) % spread, m ^ flip, 0, 0), (1, 1, share, tok))[0, 0]
            shard.append(piece if flip == d == 0 else to_plane(piece, flip, d))

    merged = jnp.zeros((rows, width), jnp.bfloat16)
    for chunk in range(CHUNKS):
        cut = slice(chunk * part, (chunk + 1) * part)
        own = jnp.stack([piece[cut] for piece in shard])
        low, high = [], []
        right = left = own
        for step in range(1, blocks):
            right = along(right, step, 1)
            left = along(left, step, -1)
            low.append(right)
            high.append(left)
        held = []
        for flip in range(copies):
            piece = lax.dynamic_slice_in_dim(weights[0], (m ^ flip) * share + chunk * part, part, 0)
            held.append(piece if flip == 0 else to_copy(piece, flip))
        mine = merge_rows(place, slots, own, low, high, grads, held)
        far = to_copy(mine, 2)
        for flip, value in ((0, mine), (1, to_copy(mine, 1)), (2, far), (3, to_copy(far, 1))):
            merged = lax.dynamic_update_slice_in_dim(merged, value, (m ^ flip) * share + chunk * part, 0)
    return merged


def solution(mesh):
    placed = (P("mp", "fsdp", None), P("mp", "fsdp", None), P("mp", "fsdp"), P("mp", "fsdp", None))
    return jax.shard_map(
        per_device, mesh=mesh, in_specs=placed, out_specs=P("fsdp", None), check_vma=False
    )
```

time: 928 us -> 517 us (0.56)
  waiting for transfers between devices: 629 us -> 240 us
  matrix products: 50.2 us -> 0 us
  starting transfers between devices: 12.5 us -> 53.1 us
  blocking collectives: 149 us -> 111 us
  Pallas kernels: 0 us -> 36.9 us
  local copies, waits for them, and re-layouts: 29.1 us -> 64.9 us
  other arithmetic: 43.1 us -> 9.95 us
  between operations: 13.2 us -> 0.42 us
    reduce_scatter x2 -> x0, waiting for transfers between devices: 425 us -> none  [the longest x1 214 us: per_device(): lax.psum_scatter(prior, 'mp', scatter_dimension=0, tiled=True)]
    ppermute x0 -> x42, waiting for transfers between devices: none -> 240 us  [the longest x15 99.2 us: to_copy(): return lax.ppermute(value, 'mp', [(s, s ^ flip) for s in range(copies)])]
    all_gather x1 -> x0, blocking collectives: 149 us -> none  [per_device(): owners = lax.all_gather(seq_ids[0], 'fsdp', axis=0, tiled=True)]
    psum x0 -> x1, blocking collectives: none -> 111 us  [per_device(): lax.psum(jnp.where(jnp.arange(copies) == m, mine, 0), ('mp', 'fsdp'))]
    all_to_all x2 -> x0, waiting for transfers between devices: 109 us -> none  [the longest x1 76.4 us: per_device(): lax.all_to_all(grad_send, 'fsdp', split_axis=0, concat_axis=1, tiled=True)]
    all_gather x1 -> x0, waiting for transfers between devices: 94.2 us -> none  [per_device(): merged = lax.all_gather(share, 'mp', axis=0, tiled=True)]
    ppermute x0 -> x42, starting transfers between devices: none -> 53.1 us  [the longest x12 24 us: along(): return lax.ppermute(value, 'fsdp', pairs)]
    dot_general x2 -> x0, matrix products: 50.2 us -> none  [per_sequence(): lax.dot_general(act_window, masked, (((0,), (0,)), ((), ())), preferred_e...]
  transfers between devices with their start and end apart: 5 -> 42, of which waited for: 5 -> 14; matrix products, arithmetic and copies ran while one was open for 1% -> 12% of each run, Pallas kernels for 0% -> 7%
where the time goes in v1:
time: 517 us; the launch traced here: 516 us
  waiting for transfers between devices  240 us (46%)
  blocking collectives  111 us (21%)
  local copies, waits for them, and re-layouts  64.9 us (13%)
  starting transfers between devices  53.1 us (10%)
  Pallas kernels  36.9 us (7%)
  other arithmetic  9.95 us (2%)
    psum x1, blocking collectives, per_device(): lax.psum(jnp.where(jnp.arange(copies) == m, mine, 0), ('mp', 'fsdp'))  111 us
    ppermute x15, waiting for transfers between devices, to_copy(): return lax.ppermute(value, 'mp', [(s, s ^ flip) for s in range(copies)])  99.2 us
    ppermute x12, waiting for transfers between devices, along(): return lax.ppermute(value, 'fsdp', pairs)  71.2 us
    pallas_call x2, Pallas kernels, merge_rows(): pl.pallas_call(functools.partial(merge_kernel, copies, shards), out_shape...  36.9 us
    ppermute x2, waiting for transfers between devices, to_half(): return lax.ppermute(value, 'fsdp', pairs)  34.6 us
    ppermute x6, waiting for transfers between devices, to_block(): return lax.ppermute(value, 'fsdp', pairs)  29.4 us
    ppermute x12, starting transfers between devices, along(): return lax.ppermute(value, 'fsdp', pairs)  24 us
    dynamic_update_slice x8, local copies, waits for them, and re-layouts, per_device(): lax.dynamic_update_slice_in_dim(merged, value, (m ^ flip) * share + chunk...  19.9 us
  transfers between devices with their start and end apart: 42, of which 14 were waited for; matrix products, arithmetic and copies ran while one was open for 12% of the time, Pallas kernels for 7%

profile of v1, /device:TPU:0, one launch (start us, length us, event | category | flops | bytes accessed | tf_op | source)
XLA Modules:
  0.0 516.1 jit_solution(6869572768831656705)
XLA Ops:
  0.0 3.3 copy.7
  8.7 4.1 copy.6
  31.5 4.8 collective-permute-done.2
  37.5 12.4 %collective-permute-done.18 = bf16[4,128,1792]{2,1,0:T(8,128)(2,1)} collective-permute-done((bf16[4,128,1792]{2,1,0:T(8,128)(2,1)}, bf16[4,128,1792]{2,1,0:T(8,128)(2,1)}, u32[]{:S(2)}, u32[]{:S(2)}) %collective-permute-start.18) | collective-permute-done | bytes 1835040 | tf_op jit(solution)/shard_map/ppermute | solution.py:127
  63.4 3.8 collective-permute-done.19
  67.2 25.6 %collective-permute-done.20 = bf16[128,1792]{1,0:T(8,128)(2,1)S(1)} collective-permute-done((bf16[128,1792]{1,0:T(8,128)(2,1)S(1)}, bf16[128,1792]{1,0:T(8,128)(2,1)S(1)}, u32[]{:S(2)}, u32[]{:S(2)}) %collective-permute-start.20) | collective-permute-done | bytes 458784 | tf_op jit(solution)/shard_map/ppermute | solution.py:131
  98.5 11.7 %collective-permute-start.30 = (bf16[8,512,128]{2,1,0:T(8,128)(2,1)}, bf16[8,512,128]{2,1,0:T(8,128)(2,1)}, u32[]{:S(2)}, u32[]{:S(2)}) collective-permute-start(bf16[8,512,128]{2,1,0:T(8,128)(2,1)} %get-tuple-element.30.refs_0_), channel_id=1, source_target_pairs={{0,2},{1,3},{2,4},{3,5},{4,6},{5,7},{8,10},{9,11},{10,12},{11,13},... | collective-permute-start | bytes 3145736 | tf_op jit(solution)/shard_map/ppermute | solution.py:151
  111.5 9.1 %dynamic-slice_bitcast_fusion = (bf16[512,1792]{1,0:T(8,128)(2,1)}, bf16[512,1792]{1,0:T(8,128)(2,1)}, bf16[512,1792]{1,0:T(8,128)(2,1)}, bf16[512,1792]{1,0:T(8...) fusion(bf16[1,4096,1792]{2,1,0:T(8,128)(2,1)} %param.7, ...), kind=kLoop, calls=%fused_computation.5 | loop fusion | bytes 29360160 | tf_op jit(solution)/shard_map/dynamic_slice | solution.py:188
  120.7 11.1 %collective-permute-done.30.refs_1_ = bf16[8,512,128]{2,1,0:T(8,128)(2,1)} collective-permute-done((bf16[8,512,128]{2,1,0:T(8,128)(2,1)}, bf16[8,512,128]{2,1,0:T(8,128)(2,1)}, u32[]{:S(2)}, u32[]{:S(2)}) %collective-permute-start.30) | collective-permute-done | bytes 1048608 | tf_op jit(solution)/shard_map/ppermute | solution.py:151
  133.1 4.4 collective-permute-done.33.refs_4_
  139.6 34.6 %collective-permute-done.22 = bf16[4,128,1792]{2,1,0:T(8,128)(2,1)} collective-permute-done((bf16[4,128,1792]{2,1,0:T(8,128)(2,1)}, bf16[4,128,1792]{2,1,0:T(8,128)(2,1)}, u32[]{:S(2)}, u32[]{:S(2)}) %collective-permute-start.22) | collective-permute-done | bytes 1835040 | tf_op jit(solution)/shard_map/ppermute | solution.py:135
  174.3 3.2 pad_maximum_fusion.refs_7_
  177.5 3.2 pad_maximum_fusion.1.refs_9_
  183.5 33.3 %collective-permute-done.26.refs_14_ = bf16[512,1792]{1,0:T(8,128)(2,1)} collective-permute-done((bf16[512,1792]{1,0:T(8,128)(2,1)S(1)}, bf16[512,1792]{1,0:T(8,128)(2,1)}, u32[]{:S(2)}, u32[]{:S(2)}) %collective-permute-start.26) | collective-permute-done | bytes 1835040 | tf_op jit(solution)/shard_map/ppermute | solution.py:127
  220.9 31.5 %collective-permute-done.34.refs_5_ = bf16[8,512,128]{2,1,0:T(8,128)(2,1)S(1)} collective-permute-done((bf16[8,512,128]{2,1,0:T(8,128)(2,1)}, bf16[8,512,128]{2,1,0:T(8,128)(2,1)S(1)}, u32[]{:S(2)}, u32[]{:S(2)}) %collective-permute-start.34) | collective-permute-done | bytes 1048608 | tf_op jit(solution)/shard_map/ppermute | solution.py:151
  253.4 20.7 %collective-permute-done.12.refs_6_ = bf16[8,512,128]{2,1,0:T(8,128)(2,1)S(1)} collective-permute-done((bf16[8,512,128]{2,1,0:T(8,128)(2,1)S(1)}, bf16[8,512,128]{2,1,0:T(8,128)(2,1)S(1)}, u32[]{:S(2)}, u32[]{:S(2)}) %collective-permute-start.12) | collective-permute-done | bytes 1048608 | tf_op jit(solution)/shard_map/ppermute | solution.py:151
  276.6 110.6 %psum.7 = s32[4]{0:T(128)S(1)} all-reduce(s32[4]{0:T(128)S(1)} %compare_select_fusion.4), channel_id=1, replica_groups=mesh['mp'=4,'fsdp'=8] {'mp','fsdp'}, use_global_device_ids=true, to_apply=%region_0.1 | all-reduce | flops 4 | bytes 32 | tf_op jit(solution)/shard_map/psum | solution.py:154
  390.6 18.4 %shard_map.46 = bf16[512,1792]{1,0:T(8,128)(2,1)} custom-call(s32[1]{0:T(128)} %bitcast.place_ref, s32[4]{0:T(128)} %and_select_fusion.slot_ref, bf16[8,512,128]{2,1,0:T(8,128)(2,1)} %get-tuple-element.31.refs_0_, bf16[8,512,128]{2,1,0:T(8,128)(2,1)} %copy-done.6, bf16[8,512,128]{2,1,0:T(8,128)(2,1)} %copy-done.10, bf16[8,512,128]{2,1,0:T(8,128)(2,1)} %copy-done.12, ...), custom_call_target="tpu_custom_call" | custom-call | flops 7516192768 | bytes 28049408 | tf_op jit(solution)/shard_map/pallas_call | solution.py:89
  411.4 3.4 collective-permute-done.35.refs_6_
  415.8 18.5 %shard_map.47 = bf16[512,1792]{1,0:T(8,128)(2,1)} custom-call(s32[1]{0:T(128)} %bitcast.place_ref, s32[4]{0:T(128)} %and_select_fusion.slot_ref, bf16[8,512,128]{2,1,0:T(8,128)(2,1)} %get-tuple-element.30.refs_0_, bf16[8,512,128]{2,1,0:T(8,128)(2,1)} %collective-permute-done.30.refs_1_, bf16[8,512,128]{2,1,0:T(8,128)(2,1)} %copy-done.7, ...), custom_call_target="tpu_custom_call" | custom-call | flops 7516192768 | bytes 28049408 | tf_op jit(solution)/shard_map/pallas_call | solution.py:89
  435.7 17.0 %collective-permute-done.28 = bf16[512,1792]{1,0:T(8,128)(2,1)} collective-permute-done((bf16[512,1792]{1,0:T(8,128)(2,1)}, bf16[512,1792]{1,0:T(8,128)(2,1)}, u32[]{:S(2)}, u32[]{:S(2)}) %collective-permute-start.28) | collective-permute-done | bytes 1835040 | tf_op jit(solution)/shard_map/ppermute | solution.py:127
  453.2 36.6 %collective-permute-done.40 = bf16[512,1792]{1,0:T(8,128)(2,1)} collective-permute-done((bf16[512,1792]{1,0:T(8,128)(2,1)}, bf16[512,1792]{1,0:T(8,128)(2,1)}, u32[]{:S(2)}, u32[]{:S(2)}) %collective-permute-start.40) | collective-permute-done | bytes 1835040 | tf_op jit(solution)/shard_map/ppermute | solution.py:127
  489.7 6.4 %broadcast_in_dim.23 = bf16[4096,1792]{1,0:T(8,128)(2,1)} broadcast(bf16[]{:T(256)} %constant.122.clone.1), dimensions={} | broadcast | bytes 14680066 | tf_op jit(solution)/shard_map/broadcast_in_dim | solution.py:175
  503.2 3.0 constant_dynamic-update-slice_fusion.4
  (141 shorter events, 85.1 us)
Async XLA Ops:
  5.8 44.1 %collective-permute-start.18 = (bf16[4,128,1792]{2,1,0:T(8,128)(2,1)}, bf16[4,128,1792]{2,1,0:T(8,128)(2,1)}, u32[]{:S(2)}, u32[]{:S(2)}) collective-permute-start(bf16[4,128,1792]{2,1,0:T(8,128)(2,1)} %bitcast.140), channel_id=1, source_target_pairs={{0,16},{8,24},{16,0},{24,8},{1,17},{9,25},{17,1},{25,9},{2,18},{10... | collective-permute-start | bytes 5505032 | tf_op jit(solution)/shard_map/ppermute | solution.py:127
  19.9 37.5 %collective-permute-start.13 = (bf16[128,1792]{1,0:T(8,128)(2,1)}, bf16[128,1792]{1,0:T(8,128)(2,1)S(1)}, u32[]{:S(2)}, u32[]{:S(2)}) collective-permute-start(bf16[128,1792]{1,0:T(8,128)(2,1)} %bitcast.23), channel_id=1, source_target_pairs={{0,2},{1,3},{2,4},{3,5},{4,6},{5,7},{6,0},{7,1},{8,10},{9,11},{10,... | collective-permute-start | bytes 1376264 | tf_op jit(solution)/shard_map/ppermute | solution.py:131
  22.5 37.0 %collective-permute-start.14 = (bf16[128,1792]{1,0:T(8,128)(2,1)}, bf16[128,1792]{1,0:T(8,128)(2,1)S(1)}, u32[]{:S(2)}, u32[]{:S(2)}) collective-permute-start(bf16[128,1792]{1,0:T(8,128)(2,1)} %bitcast.25), channel_id=1, source_target_pairs={{0,4},{1,5},{2,6},{3,7},{4,0},{5,1},{6,2},{7,3},{8,12},{9,13},{10,... | collective-permute-start | bytes 1376264 | tf_op jit(solution)/shard_map/ppermute | solution.py:131
  54.6 38.2 %collective-permute-start.20 = (bf16[128,1792]{1,0:T(8,128)(2,1)S(1)}, bf16[128,1792]{1,0:T(8,128)(2,1)S(1)}, u32[]{:S(2)}, u32[]{:S(2)}) collective-permute-start(bf16[128,1792]{1,0:T(8,128)(2,1)S(1)} %get-tuple-element.24), channel_id=1, source_target_pairs={{0,4},{1,5},{2,6},{3,7},{4,0},{5,1},{6,2},{7,3},{8,12},{9,13},{10,... | collective-permute-start | bytes 1376264 | tf_op jit(solution)/shard_map/ppermute | solution.py:131
  59.5 36.8 %collective-permute-start.4 = (bf16[1024,128]{1,0:T(8,128)(2,1)S(1)}, bf16[1024,128]{1,0:T(8,128)(2,1)S(1)}, u32[]{:S(2)}, u32[]{:S(2)}) collective-permute-start(bf16[1024,128]{1,0:T(8,128)(2,1)S(1)} %copy-done.17), channel_id=1, source_target_pairs={{0,17},{1,16},{2,19},{3,18},{4,21},{5,20},{6,23},{7,22},{8,25},{9,... | collective-permute-start | bytes 786440 | tf_op jit(solution)/shard_map/ppermute | solution.py:143
  92.8 46.2 %collective-permute-start.16 = (bf16[4,128,1792]{2,1,0:T(8,128)(2,1)}, bf16[4,128,1792]{2,1,0:T(8,128)(2,1)}, u32[]{:S(2)}, u32[]{:S(2)}) collective-permute-start(bf16[4,128,1792]{2,1,0:T(8,128)(2,1)} %pad_maximum_fusion.2), channel_id=1, source_target_pairs={{0,1},{1,0},{2,3},{3,2},{4,5},{5,4},{6,7},{7,6},{8,9},{9,8},{10,11... | collective-permute-start | bytes 5505032 | tf_op jit(solution)/shard_map/ppermute | solution.py:135
  94.8 79.5 %collective-permute-start.22 = (bf16[4,128,1792]{2,1,0:T(8,128)(2,1)}, bf16[4,128,1792]{2,1,0:T(8,128)(2,1)}, u32[]{:S(2)}, u32[]{:S(2)}) collective-permute-start(bf16[4,128,1792]{2,1,0:T(8,128)(2,1)} %pad_maximum_fusion.3), channel_id=1, source_target_pairs={{0,1},{1,0},{2,3},{3,2},{4,5},{5,4},{6,7},{7,6},{8,9},{9,8},{10,11... | collective-permute-start | bytes 5505032 | tf_op jit(solution)/shard_map/ppermute | solution.py:135
  120.6 60.8 %collective-permute-start.24 = (bf16[512,1792]{1,0:T(8,128)(2,1)S(1)}, bf16[512,1792]{1,0:T(8,128)(2,1)}, u32[]{:S(2)}, u32[]{:S(2)}) collective-permute-start(bf16[512,1792]{1,0:T(8,128)(2,1)S(1)} %get-tuple-element.10), channel_id=1, source_target_pairs={{0,8},{8,0},{16,24},{24,16},{1,9},{9,1},{17,25},{25,17},{2,10},{10... | collective-permute-start | bytes 5505032 | tf_op jit(solution)/shard_map/ppermute | solution.py:127
  131.8 48.9 %collective-permute-start.10 = (bf16[8,512,128]{2,1,0:T(8,128)(2,1)}, bf16[8,512,128]{2,1,0:T(8,128)(2,1)S(1)}, u32[]{:S(2)}, u32[]{:S(2)}) collective-permute-start(bf16[8,512,128]{2,1,0:T(8,128)(2,1)} %get-tuple-element.31.refs_0_), channel_id=1, source_target_pairs={{2,0},{3,1},{4,2},{5,3},{6,4},{7,5},{10,8},{11,9},{12,10},{13,11},... | collective-permute-start | bytes 3145736 | tf_op jit(solution)/shard_map/ppermute | solution.py:151
  137.5 43.8 %collective-permute-start.7 = (bf16[8,512,128]{2,1,0:T(8,128)(2,1)}, bf16[8,512,128]{2,1,0:T(8,128)(2,1)S(1)}, u32[]{:S(2)}, u32[]{:S(2)}) collective-permute-start(bf16[8,512,128]{2,1,0:T(8,128)(2,1)} %get-tuple-element.31.refs_0_), channel_id=1, source_target_pairs={{0,2},{1,3},{2,4},{3,5},{4,6},{5,7},{8,10},{9,11},{10,12},{11,13},... | collective-permute-start | bytes 3145736 | tf_op jit(solution)/shard_map/ppermute | solution.py:151
  139.0 43.1 %collective-permute-start.25 = (bf16[512,1792]{1,0:T(8,128)(2,1)S(1)}, bf16[512,1792]{1,0:T(8,128)(2,1)}, u32[]{:S(2)}, u32[]{:S(2)}) collective-permute-start(bf16[512,1792]{1,0:T(8,128)(2,1)S(1)} %get-tuple-element.9), channel_id=1, source_target_pairs={{0,16},{8,24},{16,0},{24,8},{1,17},{9,25},{17,1},{25,9},{2,18},{10... | collective-permute-start | bytes 5505032 | tf_op jit(solution)/shard_map/ppermute | solution.py:127
  174.3 42.5 %collective-permute-start.26 = (bf16[512,1792]{1,0:T(8,128)(2,1)S(1)}, bf16[512,1792]{1,0:T(8,128)(2,1)}, u32[]{:S(2)}, u32[]{:S(2)}) collective-permute-start(bf16[512,1792]{1,0:T(8,128)(2,1)S(1)} %get-tuple-element.8), channel_id=1, source_target_pairs={{0,24},{8,16},{16,8},{24,0},{1,25},{9,17},{17,9},{25,1},{2,26},{10... | collective-permute-start | bytes 5505032 | tf_op jit(solution)/shard_map/ppermute | solution.py:127
  180.7 207.1 %collective-permute-start.17 = (bf16[4,256,1792]{2,1,0:T(8,128)(2,1)}, bf16[4,256,1792]{2,1,0:T(8,128)(2,1)}, u32[]{:S(2)}, u32[]{:S(2)}) collective-permute-start(bf16[4,256,1792]{2,1,0:T(8,128)(2,1)} %pad_maximum_fusion.refs_7_), channel_id=1, source_target_pairs={{0,8},{8,0},{16,24},{24,16},{1,9},{9,1},{17,25},{25,17},{2,10},{10... | collective-permute-start | bytes 11010056 | tf_op jit(solution)/shard_map/ppermute | solution.py:127
  181.3 207.3 %collective-permute-start.23 = (bf16[4,256,1792]{2,1,0:T(8,128)(2,1)}, bf16[4,256,1792]{2,1,0:T(8,128)(2,1)}, u32[]{:S(2)}, u32[]{:S(2)}) collective-permute-start(bf16[4,256,1792]{2,1,0:T(8,128)(2,1)} %pad_maximum_fusion.1.refs_9_), channel_id=1, source_target_pairs={{0,8},{8,0},{16,24},{24,16},{1,9},{9,1},{17,25},{25,17},{2,10},{10... | collective-permute-start | bytes 11010056 | tf_op jit(solution)/shard_map/ppermute | solution.py:127
  218.8 55.2 %collective-permute-start.12 = (bf16[8,512,128]{2,1,0:T(8,128)(2,1)S(1)}, bf16[8,512,128]{2,1,0:T(8,128)(2,1)S(1)}, u32[]{:S(2)}, u32[]{:S(2)}) collective-permute-start(bf16[8,512,128]{2,1,0:T(8,128)(2,1)S(1)} %collective-permute-done.11.refs_5_), channel_id=1, source_target_pairs={{2,0},{3,1},{10,8},{11,9},{18,16},{19,17},{26,24},{27,25}} | collective-permute-start | bytes 3145736 | tf_op jit(solution)/shard_map/ppermute | solution.py:151
  220.1 55.4 %collective-permute-start.9 = (bf16[8,512,128]{2,1,0:T(8,128)(2,1)S(1)}, bf16[8,512,128]{2,1,0:T(8,128)(2,1)S(1)}, u32[]{:S(2)}, u32[]{:S(2)}) collective-permute-start(bf16[8,512,128]{2,1,0:T(8,128)(2,1)S(1)} %collective-permute-done.8.refs_2_), channel_id=1, source_target_pairs={{4,6},{5,7},{12,14},{13,15},{20,22},{21,23},{28,30},{29,31}} | collective-permute-start | bytes 3145736 | tf_op jit(solution)/shard_map/ppermute | solution.py:151
  252.4 156.6 %collective-permute-start.36 = (bf16[512,1792]{1,0:T(8,128)(2,1)}, bf16[512,1792]{1,0:T(8,128)(2,1)S(1)}, u32[]{:S(2)}, u32[]{:S(2)}) collective-permute-start(bf16[512,1792]{1,0:T(8,128)(2,1)} %get-tuple-element.6), channel_id=1, source_target_pairs={{0,8},{8,0},{16,24},{24,16},{1,9},{9,1},{17,25},{25,17},{2,10},{10... | collective-permute-start | bytes 5505032 | tf_op jit(solution)/shard_map/ppermute | solution.py:127
  274.1 137.3 %collective-permute-start.37 = (bf16[512,1792]{1,0:T(8,128)(2,1)}, bf16[512,1792]{1,0:T(8,128)(2,1)}, u32[]{:S(2)}, u32[]{:S(2)}) collective-permute-start(bf16[512,1792]{1,0:T(8,128)(2,1)} %get-tuple-element.12), channel_id=1, source_target_pairs={{0,16},{8,24},{16,0},{24,8},{1,17},{9,25},{17,1},{25,9},{2,18},{10... | collective-permute-start | bytes 5505032 | tf_op jit(solution)/shard_map/ppermute | solution.py:127
  276.5 134.9 %collective-permute-start.38 = (bf16[512,1792]{1,0:T(8,128)(2,1)}, bf16[512,1792]{1,0:T(8,128)(2,1)}, u32[]{:S(2)}, u32[]{:S(2)}) collective-permute-start(bf16[512,1792]{1,0:T(8,128)(2,1)} %get-tuple-element.5), channel_id=1, source_target_pairs={{0,24},{8,16},{16,8},{24,0},{1,25},{9,17},{17,9},{25,1},{2,26},{10... | collective-permute-start | bytes 5505032 | tf_op jit(solution)/shard_map/ppermute | solution.py:127
  409.1 43.6 %collective-permute-start.28 = (bf16[512,1792]{1,0:T(8,128)(2,1)}, bf16[512,1792]{1,0:T(8,128)(2,1)}, u32[]{:S(2)}, u32[]{:S(2)}) collective-permute-start(bf16[512,1792]{1,0:T(8,128)(2,1)} %shard_map.46), channel_id=1, source_target_pairs={{0,16},{8,24},{16,0},{24,8},{1,17},{9,25},{17,1},{25,9},{2,18},{10... | collective-permute-start | bytes 5505032 | tf_op jit(solution)/shard_map/ppermute | solution.py:127
  434.3 55.4 %collective-permute-start.40 = (bf16[512,1792]{1,0:T(8,128)(2,1)}, bf16[512,1792]{1,0:T(8,128)(2,1)}, u32[]{:S(2)}, u32[]{:S(2)}) collective-permute-start(bf16[512,1792]{1,0:T(8,128)(2,1)} %shard_map.47), channel_id=1, source_target_pairs={{0,16},{8,24},{16,0},{24,8},{1,17},{9,25},{17,1},{25,9},{2,18},{10... | collective-permute-start | bytes 5505032 | tf_op jit(solution)/shard_map/ppermute | solution.py:127
  435.7 61.8 %collective-permute-start.27 = (bf16[512,1792]{1,0:T(8,128)(2,1)S(1)}, bf16[512,1792]{1,0:T(8,128)(2,1)}, u32[]{:S(2)}, u32[]{:S(2)}) collective-permute-start(bf16[512,1792]{1,0:T(8,128)(2,1)S(1)} %copy-done), channel_id=1, source_target_pairs={{0,8},{8,0},{16,24},{24,16},{1,9},{9,1},{17,25},{25,17},{2,10},{10... | collective-permute-start | bytes 5505032 | tf_op jit(solution)/shard_map/ppermute | solution.py:127
  452.7 50.5 %collective-permute-start.29 = (bf16[512,1792]{1,0:T(8,128)(2,1)}, bf16[512,1792]{1,0:T(8,128)(2,1)}, u32[]{:S(2)}, u32[]{:S(2)}) collective-permute-start(bf16[512,1792]{1,0:T(8,128)(2,1)} %collective-permute-done.28), channel_id=1, source_target_pairs={{0,8},{8,0},{16,24},{24,16},{1,9},{9,1},{17,25},{25,17},{2,10},{10... | collective-permute-start | bytes 5505032 | tf_op jit(solution)/shard_map/ppermute | solution.py:127
  452.7 54.9 %collective-permute-start.39 = (bf16[512,1792]{1,0:T(8,128)(2,1)}, bf16[512,1792]{1,0:T(8,128)(2,1)}, u32[]{:S(2)}, u32[]{:S(2)}) collective-permute-start(bf16[512,1792]{1,0:T(8,128)(2,1)} %shard_map.47), channel_id=1, source_target_pairs={{0,8},{8,0},{16,24},{24,16},{1,9},{9,1},{17,25},{25,17},{2,10},{10... | collective-permute-start | bytes 5505032 | tf_op jit(solution)/shard_map/ppermute | solution.py:127
  (38 other events, 1092.6 us)

commit v2 on v1

--- a/solution.py
+++ b/solution.py
@@ -10,6 +10,7 @@
 F = 7168
 SEQS = 2
 CHUNKS = 2
+PIECES = 4
 COL_TILE = 256
 ROW_TILE = 256
 
@@ -110,6 +111,10 @@
     )(place, slots, own, *low, *high, *grads, *weights)
 
 
+def after(value, *others):
+    return lax.optimization_barrier((value, *others))[0]
+
+
 def per_device(activations, out_grads, seq_ids, weights):
     copies = lax.axis_size("mp")
     devices = lax.axis_size("fsdp")
@@ -119,9 +124,11 @@
     tok = activations.shape[1]
     share = rows // copies
     part = share // CHUNKS
+    piece = share // PIECES
     m = lax.axis_index("mp")
     i = lax.axis_index("fsdp")
     a, h = i // spread, i % spread
+    chip, core = m // 2, m % 2
 
     def to_copy(value, flip):
         return lax.ppermute(value, "mp", [(s, s ^ flip) for s in range(copies)])
@@ -133,14 +140,6 @@
     def to_half(value, shift):
         pairs = [(s, s // spread * spread + (s % spread + shift) % spread) for s in range(devices)]
         return lax.ppermute(value, "fsdp", pairs)
-
-    def to_plane(value, flip, shift):
-        pairs = [
-            (c * devices + s, (c ^ flip) * devices + s // spread * spread + (s % spread + shift) % spread)
-            for c in range(copies)
-            for s in range(devices)
-        ]
-        return lax.ppermute(value, ("mp", "fsdp"), pairs)
 
     def along(value, step, direction):
         pairs = [
@@ -150,45 +149,98 @@
         ]
         return lax.ppermute(value, "fsdp", pairs)
 
-    mine = jnp.where((a == 1) & (h == 0), seq_ids[0, 0], 0)
-    second = lax.psum(jnp.where(jnp.arange(copies) == m, mine, 0), ("mp", "fsdp"))
-    alone = jnp.where(second == 1, 0, blocks - 1)[m ^ jnp.arange(copies)]
+    def column_block(value, shift):
+        return lax.dynamic_slice_in_dim(value, (a + shift) % blocks * width, width, 1)
+
+    def spread_blocks(value):
+        return [column_block(value, 0)] + [to_block(column_block(value, k), k) for k in range(1, blocks)]
+
+    def weight_rows(owner, start, count):
+        return lax.dynamic_slice_in_dim(weights[0], owner * share + start, count, 0)
+
+    grad_far = to_copy(out_grads[0], 2)
+    acts = activations[0].T.reshape(spread, copies // 2, 2, share, tok)
+    acts_near = lax.dynamic_index_in_dim(acts, chip, 1, keepdims=False)
+    acts_far = to_copy(lax.dynamic_index_in_dim(acts, 1 - chip, 1, keepdims=False), 2)
+    near = spread_blocks(out_grads[0])
+    grad_near = jnp.stack(near)
+
+    held = jnp.stack([acts_near, acts_far])
+    held = after(held, grad_near, grad_far)
+    grad_far = after(grad_far, grad_near, held)
+    weight_far = []
+
+    def send_weights(k, *others):
+        start = k * piece
+        both = jnp.stack([weight_rows((1 - chip) * 2 + c, start, piece) for c in range(2)])
+        weight_far.append(to_copy(after(both, *others), 2))
+
+    send_weights(0, grad_near, grad_far, held)
+    halves = [
+        lax.dynamic_index_in_dim(held, (h + d) % spread, 1, keepdims=False) for d in range(spread)
+    ]
+    halves = [halves[0]] + [to_half(halves[d], d) for d in range(1, spread)]
+    held = jnp.stack(halves, 1)
+    acts_mine = lax.dynamic_index_in_dim(held, core, 2, keepdims=False)
+    acts_mate = to_copy(lax.dynamic_index_in_dim(held, 1 - core, 2, keepdims=False), 1)
+    shard = jnp.stack([acts_mine, acts_mate], 1).reshape(copies * spread, share, tok)
+    flags = jnp.where(jnp.arange(copies) == m, seq_ids[0, 0], 0)
+    flags = after(flags, grad_near)
+    flags = flags + to_copy(flags, 2)
+    grad_far = jnp.stack(spread_blocks(grad_far))
+
+    stage = (shard, grad_far, weight_far[0], flags)
+    shards = [shard[:, k * part:(k + 1) * part] for k in range(CHUNKS)]
+    low = [[] for _ in range(CHUNKS)]
+    high = [[] for _ in range(CHUNKS)]
+    grads = [None] * copies
+
+    def step(k, *others):
+        n = len(low[k]) + 1
+        right, left = (low[k][-1], high[k][-1]) if n > 1 else (shards[k], shards[k])
+        low[k].append(along(after(right, *others), n, 1))
+        high[k].append(along(after(left, *others), n, -1))
+
+    def over_halves(value):
+        return jnp.concatenate([value] + [to_half(value, d) for d in range(1, spread)], axis=1)
+
+    step(0, *stage)
+    step(0)
+    send_weights(1, *stage)
+    grads[0] = over_halves(after(grad_near, *stage))
+    mate_rows = to_copy(after(weight_rows(chip * 2 + 1 - core, 0, share), *stage), 1)
+    flags = flags + to_copy(after(flags, *stage), 1)
+    stage = (low[0][-1], high[0][-1], weight_far[1], grads[0], mate_rows, flags)
+    step(0, *stage)
+    step(1, *stage)
+    send_weights(2, *stage)
+    grads[2] = over_halves(after(grad_far, *stage))
+    grads[1] = to_copy(after(grads[0], *stage), 1)
+    ends = [(s, s - spread) for s in range(spread, 2 * spread)]
+    ends += [(s, s + spread) for s in range(devices - 2 * spread, devices - spread)]
+    outer = lax.ppermute(after(flags, *stage), "fsdp", ends)
+    flags = jnp.where((a == 0) | (a == blocks - 1), outer, flags)
+    stage = (low[0][-1], high[0][-1], low[1][-1], high[1][-1], weight_far[2], grads[1], grads[2], flags)
+    step(1, *stage)
+    step(1)
+    send_weights(3, *stage)
+    grads[3] = to_copy(after(grads[2], *stage), 1)
+
+    alone = jnp.where(flags == 1, 0, blocks - 1)[m ^ jnp.arange(copies)]
     slots = ((a - alone) % blocks).astype(jnp.int32)
     place = a.astype(jnp.int32)[None]
 
-    grad_blocks = out_grads[0].reshape(tok, blocks, width).transpose(1, 0, 2)
-    grads = [None] * copies
-    for flip, value in ((0, grad_blocks), (2, to_copy(grad_blocks, 2))):
-        block = [lax.dynamic_index_in_dim(value, (a + k) % blocks, 0, keepdims=False) for k in range(blocks)]
-        held = jnp.stack([block[0]] + [to_block(block[k], k) for k in range(1, blocks)])
-        held = jnp.concatenate([held] + [to_half(held, d) for d in range(1, spread)], axis=1)
-        grads[flip] = held
-        grads[flip ^ 1] = to_copy(held, 1)
-
-    acts = activations[0].T.reshape(spread, copies, share, tok)
-    shard = []
-    for flip in range(copies):
-        for d in range(spread):
-            piece = lax.dynamic_slice(acts, ((h + d) % spread, m ^ flip, 0, 0), (1, 1, share, tok))[0, 0]
-            shard.append(piece if flip == d == 0 else to_plane(piece, flip, d))
-
-    merged = jnp.zeros((rows, width), jnp.bfloat16)
+    merged = None
+    count = PIECES // CHUNKS
     for chunk in range(CHUNKS):
-        cut = slice(chunk * part, (chunk + 1) * part)
-        own = jnp.stack([piece[cut] for piece in shard])
-        low, high = [], []
-        right = left = own
-        for step in range(1, blocks):
-            right = along(right, step, 1)
-            left = along(left, step, -1)
-            low.append(right)
-            high.append(left)
-        held = []
-        for flip in range(copies):
-            piece = lax.dynamic_slice_in_dim(weights[0], (m ^ flip) * share + chunk * part, part, 0)
-            held.append(piece if flip == 0 else to_copy(piece, flip))
-        mine = merge_rows(place, slots, own, low, high, grads, held)
+        far = jnp.concatenate(weight_far[chunk * count:(chunk + 1) * count], axis=1)
+        mine = lax.dynamic_index_in_dim(far, core, 0, keepdims=False)
+        mate = to_copy(lax.dynamic_index_in_dim(far, 1 - core, 0, keepdims=False), 1)
+        held = [weight_rows(m, chunk * part, part), mate_rows[chunk * part:(chunk + 1) * part], mine, mate]
+        mine = merge_rows(place, slots, shards[chunk], low[chunk], high[chunk], grads, held)
         far = to_copy(mine, 2)
+        if merged is None:
+            merged = jnp.zeros((rows, width), jnp.bfloat16)
         for flip, value in ((0, mine), (1, to_copy(mine, 1)), (2, far), (3, to_copy(far, 1))):
             merged = lax.dynamic_update_slice_in_dim(merged, value, (m ^ flip) * share + chunk * part, 0)
     return merged

time: 517 us -> 454 us (0.88); the launches traced: 516 us -> 447 us
  blocking collectives: 111 us -> 0 us
  waiting for transfers between devices: 240 us -> 265 us
  local copies, waits for them, and re-layouts: 64.9 us -> 72.7 us
  starting transfers between devices: 53.1 us -> 59.6 us
    psum x1 -> x0, blocking collectives: 111 us -> none  [per_device(): lax.psum(jnp.where(jnp.arange(copies) == m, mine, 0), ('mp', 'fsdp'))]
    ppermute x15 -> x20, waiting for transfers between devices: 99.2 us -> 115 us  [to_copy(): return lax.ppermute(value, 'mp', [(s, s ^ flip) for s in range(copies)])]
    ppermute x6, waiting for transfers between devices: 29.4 us -> 42.4 us  [to_block(): return lax.ppermute(value, 'fsdp', pairs)]
    another operation x2 -> x9, other arithmetic: 2.94 us -> 10.8 us  [the longest x4 3.18 us: send_weights(): jnp.stack([weight_rows((1 - chip) * 2 + c, start, piece) for c in range(2)])]
    concatenate x2 -> x0, other arithmetic: 6.44 us -> none  [per_device(): jnp.concatenate([held] + [to_half(held, d) for d in range(1, spread)], ax...]
    ppermute x12, waiting for transfers between devices: 71.2 us -> 64.8 us  [along(): return lax.ppermute(value, 'fsdp', pairs)]
    ppermute x2 -> x3, waiting for transfers between devices: 34.6 us -> 39.6 us  [to_half(): return lax.ppermute(value, 'fsdp', pairs)]
    dynamic_slice x2 -> x4, local copies, waits for them, and re-layouts: 10.7 us -> 14.5 us  [the longest x3 12 us: weight_rows(): return lax.dynamic_slice_in_dim(weights[0], owner * share + start, count, 0)]
  transfers between devices with their start and end apart: 42 -> 42, of which waited for: 14 -> 20; matrix products, arithmetic and copies ran while one was open for 12% -> 17% of each run, Pallas kernels for 7% -> 8%
where the time goes in v2:
time: 454 us; the launch traced here: 447 us
  waiting for transfers between devices  265 us (58%)
  local copies, waits for them, and re-layouts  72.7 us (16%)
  starting transfers between devices  59.6 us (13%)
  Pallas kernels  37 us (8%)
  other arithmetic  11.4 us (3%)
    ppermute x20, waiting for transfers between devices, to_copy(): return lax.ppermute(value, 'mp', [(s, s ^ flip) for s in range(copies)])  115 us
    ppermute x12, waiting for transfers between devices, along(): return lax.ppermute(value, 'fsdp', pairs)  64.8 us
    ppermute x6, waiting for transfers between devices, to_block(): return lax.ppermute(value, 'fsdp', pairs)  42.4 us
    ppermute x3, waiting for transfers between devices, to_half(): return lax.ppermute(value, 'fsdp', pairs)  39.6 us
    pallas_call x2, Pallas kernels, merge_rows(): pl.pallas_call(functools.partial(merge_kernel, copies, shards), out_shape...  37 us
    ppermute x12, starting transfers between devices, along(): return lax.ppermute(value, 'fsdp', pairs)  26.9 us
    dynamic_update_slice x8, local copies, waits for them, and re-layouts, per_device(): lax.dynamic_update_slice_in_dim(merged, value, (m ^ flip) * share + chunk...  19.9 us
    unnamed x59, local copies, waits for them, and re-layouts  15.6 us
  transfers between devices with their start and end apart: 42, of which 20 were waited for; matrix products, arithmetic and copies ran while one was open for 17% of the time, Pallas kernels for 8%

profile of v2, /device:TPU:0, one launch (start us, length us, event | category | flops | bytes accessed | tf_op | source)
XLA Modules:
  0.0 446.5 jit_solution(17554769857481263609)
XLA Ops:
  15.8 9.9 %collective-permute-done = bf16[128,1792]{1,0:T(8,128)(2,1)S(1)} collective-permute-done((bf16[128,1792]{1,0:T(8,128)(2,1)}, bf16[128,1792]{1,0:T(8,128)(2,1)S(1)}, u32[]{:S(2)}, u32[]{:S(2)}) %collective-permute-start) | collective-permute-done | bytes 458784 | tf_op jit(solution)/shard_map/ppermute | solution.py:138
  25.7 18.2 %collective-permute-done.1 = bf16[128,1792]{1,0:T(8,128)(2,1)S(1)} collective-permute-done((bf16[128,1792]{1,0:T(8,128)(2,1)S(1)}, bf16[128,1792]{1,0:T(8,128)(2,1)S(1)}, u32[]{:S(2)}, u32[]{:S(2)}) %collective-permute-start.1) | collective-permute-done | bytes 458784 | tf_op jit(solution)/shard_map/ppermute | solution.py:138
  46.3 19.4 %collective-permute-done.4 = bf16[2,2,1024,128]{3,2,1,0:T(8,128)(2,1)} collective-permute-done((bf16[2,2,1024,128]{3,2,1,0:T(8,128)(2,1)}, bf16[2,2,1024,128]{3,2,1,0:T(8,128)(2,1)}, u32[]{:S(2)}, u32[]{:S(2)}) %collective-permute-start.4) | collective-permute-done | bytes 1048608 | tf_op jit(solution)/shard_map/ppermute | solution.py:134
  70.1 5.6 %constant_dynamic-slice_fusion.1 = (bf16[1,256,1792]{2,1,0:T(8,128)(2,1)}, bf16[1,256,1792]{2,1,0:T(8,128)(2,1)}, bf16[1,256,1792]{2,1,0:T(8,128)(2,1)}, bf16[1,...) fusion(bf16[1,4096,1792]{2,1,0:T(8,128)(2,1)} %param.7, ...), kind=kLoop, calls=%fused_computation.44 | loop fusion | bytes 14680096 | tf_op jit(solution)/shard_map/dynamic_slice | solution.py:159
  78.6 14.4 %collective-permute-done.6 = bf16[2,2,1024,128]{3,2,1,0:T(8,128)(2,1)} collective-permute-done((bf16[2,2,1024,128]{3,2,1,0:T(8,128)(2,1)}, bf16[2,2,1024,128]{3,2,1,0:T(8,128)(2,1)}, u32[]{:S(2)}, u32[]{:S(2)}) %collective-permute-start.6) | collective-permute-done | bytes 1048608 | tf_op jit(solution)/shard_map/ppermute | solution.py:142
  104.0 14.0 %collective-permute-done.3 = s32[4]{0:T(128)S(1)} collective-permute-done((s32[4]{0:T(128)S(1)}, s32[4]{0:T(128)S(1)}, u32[]{:S(2)}, u32[]{:S(2)}) %collective-permute-start.3) | collective-permute-done | bytes 48 | tf_op jit(solution)/shard_map/ppermute | solution.py:134
  123.9 10.5 %collective-permute-done.9 = bf16[128,1792]{1,0:T(8,128)(2,1)} collective-permute-done((bf16[128,1792]{1,0:T(8,128)(2,1)}, bf16[128,1792]{1,0:T(8,128)(2,1)}, u32[]{:S(2)}, u32[]{:S(2)}) %collective-permute-start.9) | collective-permute-done | bytes 458784 | tf_op jit(solution)/shard_map/ppermute | solution.py:138
  140.4 8.8 %collective-permute-start.13 = (bf16[8,512,128]{2,1,0:T(8,128)(2,1)S(1)}, bf16[8,512,128]{2,1,0:T(8,128)(2,1)S(1)}, u32[]{:S(2)}, u32[]{:S(2)}) collective-permute-start(bf16[8,512,128]{2,1,0:T(8,128)(2,1)S(1)} %get-tuple-element.30.refs_0_), channel_id=1, source_target_pairs={{0,2},{1,3},{2,4},{3,5},{4,6},{5,7},{8,10},{9,11},{10,12},{11,13},... | collective-permute-start | bytes 3145736 | tf_op jit(solution)/shard_map/ppermute | solution.py:150
  152.8 19.3 %collective-permute-done.13.refs_1_ = bf16[8,512,128]{2,1,0:T(8,128)(2,1)S(1)} collective-permute-done((bf16[8,512,128]{2,1,0:T(8,128)(2,1)S(1)}, bf16[8,512,128]{2,1,0:T(8,128)(2,1)S(1)}, u32[]{:S(2)}, u32[]{:S(2)}) %collective-permute-start.13) | collective-permute-done | bytes 1048608 | tf_op jit(solution)/shard_map/ppermute | solution.py:150
  172.1 4.2 collective-permute-done.15.refs_4_
  180.6 12.0 %collective-permute-done.18 = bf16[4,128,1792]{2,1,0:T(8,128)(2,1)S(1)} collective-permute-done((bf16[4,128,1792]{2,1,0:T(8,128)(2,1)S(1)}, bf16[4,128,1792]{2,1,0:T(8,128)(2,1)S(1)}, u32[]{:S(2)}, u32[]{:S(2)}) %collective-permute-start.18) | collective-permute-done | bytes 1835040 | tf_op jit(solution)/shard_map/ppermute | solution.py:142
  194.1 11.0 %collective-permute-done.16.refs_5_ = bf16[8,512,128]{2,1,0:T(8,128)(2,1)} collective-permute-done((bf16[8,512,128]{2,1,0:T(8,128)(2,1)S(1)}, bf16[8,512,128]{2,1,0:T(8,128)(2,1)}, u32[]{:S(2)}, u32[]{:S(2)}) %collective-permute-start.16) | collective-permute-done | bytes 1048608 | tf_op jit(solution)/shard_map/ppermute | solution.py:150
  206.7 4.6 %collective-permute-start.25 = (bf16[8,512,128]{2,1,0:T(8,128)(2,1)S(1)}, bf16[8,512,128]{2,1,0:T(8,128)(2,1)}, u32[]{:S(2)}, u32[]{:S(2)}) collective-permute-start(bf16[8,512,128]{2,1,0:T(8,128)(2,1)S(1)} %get-tuple-element.39.refs_0_), channel_id=1, source_target_pairs={{0,2},{1,3},{2,4},{3,5},{4,6},{5,7},{8,10},{9,11},{10,12},{11,13},... | collective-permute-start | bytes 3145736 | tf_op jit(solution)/shard_map/ppermute | solution.py:150
  214.6 4.1 collective-permute-done.20
  220.1 13.0 %collective-permute-done.25.refs_1_ = bf16[8,512,128]{2,1,0:T(8,128)(2,1)} collective-permute-done((bf16[8,512,128]{2,1,0:T(8,128)(2,1)S(1)}, bf16[8,512,128]{2,1,0:T(8,128)(2,1)}, u32[]{:S(2)}, u32[]{:S(2)}) %collective-permute-start.25) | collective-permute-done | bytes 1048608 | tf_op jit(solution)/shard_map/ppermute | solution.py:150
  234.4 13.2 %collective-permute-done.24 = bf16[4,128,1792]{2,1,0:T(8,128)(2,1)S(1)} collective-permute-done((bf16[4,128,1792]{2,1,0:T(8,128)(2,1)S(1)}, bf16[4,128,1792]{2,1,0:T(8,128)(2,1)S(1)}, u32[]{:S(2)}, u32[]{:S(2)}) %collective-permute-start.24) | collective-permute-done | bytes 1835040 | tf_op jit(solution)/shard_map/ppermute | solution.py:142
  254.0 13.2 %collective-permute-done.22.refs_6_ = bf16[8,512,128]{2,1,0:T(8,128)(2,1)} collective-permute-done((bf16[8,512,128]{2,1,0:T(8,128)(2,1)}, bf16[8,512,128]{2,1,0:T(8,128)(2,1)}, u32[]{:S(2)}, u32[]{:S(2)}) %collective-permute-start.22) | collective-permute-done | bytes 1048608 | tf_op jit(solution)/shard_map/ppermute | solution.py:150
  269.0 4.1 dynamic-slice_bitcast_fusion.3
  282.2 27.8 %collective-permute-done.37 = bf16[2,256,1792]{2,1,0:T(8,128)(2,1)} collective-permute-done((bf16[2,256,1792]{2,1,0:T(8,128)(2,1)S(1)}, bf16[2,256,1792]{2,1,0:T(8,128)(2,1)}, u32[]{:S(2)}, u32[]{:S(2)}) %collective-permute-start.37) | collective-permute-done | bytes 1835040 | tf_op jit(solution)/shard_map/ppermute | solution.py:134
  320.4 18.4 %shard_map.46 = bf16[512,1792]{1,0:T(8,128)(2,1)} custom-call(s32[1]{0:T(128)} %bitcast.place_ref, s32[4]{0:T(128)} %and_select_fusion.slot_ref, bf16[8,512,128]{2,1,0:T(8,128)(2,1)} %copy-done.5, bf16[8,512,128]{2,1,0:T(8,128)(2,1)} %copy-done.20, bf16[8,512,128]{2,1,0:T(8,128)(2,1)} %collective-permute-done.14.refs_2_, ...), custom_call_target="tpu_custom_call" | custom-call | flops 7516192768 | bytes 28049408 | tf_op jit(solution)/shard_map/pallas_call | solution.py:90
  346.5 18.5 %shard_map.47 = bf16[512,1792]{1,0:T(8,128)(2,1)} custom-call(s32[1]{0:T(128)} %bitcast.place_ref, s32[4]{0:T(128)} %and_select_fusion.slot_ref, bf16[8,512,128]{2,1,0:T(8,128)(2,1)} %copy-done.4, bf16[8,512,128]{2,1,0:T(8,128)(2,1)} %collective-permute-done.25.refs_1_, bf16[8,512,128]{2,1,0:T(8,128)(2,1)} %collective-permute-done.33.refs_2_, ...), custom_call_target="tpu_custom_call" | custom-call | flops 7516192768 | bytes 28049408 | tf_op jit(solution)/shard_map/pallas_call | solution.py:90
  366.6 15.6 %collective-permute-done.31 = bf16[512,1792]{1,0:T(8,128)(2,1)} collective-permute-done((bf16[512,1792]{1,0:T(8,128)(2,1)}, bf16[512,1792]{1,0:T(8,128)(2,1)}, u32[]{:S(2)}, u32[]{:S(2)}) %collective-permute-start.31) | collective-permute-done | bytes 1835040 | tf_op jit(solution)/shard_map/ppermute | solution.py:134
  382.7 37.5 %collective-permute-done.40 = bf16[512,1792]{1,0:T(8,128)(2,1)} collective-permute-done((bf16[512,1792]{1,0:T(8,128)(2,1)}, bf16[512,1792]{1,0:T(8,128)(2,1)}, u32[]{:S(2)}, u32[]{:S(2)}) %collective-permute-start.40) | collective-permute-done | bytes 1835040 | tf_op jit(solution)/shard_map/ppermute | solution.py:134
  420.2 6.4 %broadcast_in_dim.23 = bf16[4096,1792]{1,0:T(8,128)(2,1)} broadcast(bf16[]{:T(256)} %constant.149.clone.1), dimensions={} | broadcast | bytes 14680066 | tf_op jit(solution)/shard_map/broadcast_in_dim | solution.py:243
  (162 shorter events, 122.3 us)
Async XLA Ops:
  0.0 67.2 %collective-permute-start.5 = (bf16[128,7168]{1,0:T(8,128)(2,1)}, bf16[128,7168]{1,0:T(8,128)(2,1)}, u32[]{:S(2)}, u32[]{:S(2)}) collective-permute-start(bf16[128,7168]{1,0:T(8,128)(2,1)} %bitcast.55), channel_id=1, source_target_pairs={{0,16},{8,24},{16,0},{24,8},{1,17},{9,25},{17,1},{25,9},{2,18},{10... | collective-permute-start | bytes 5505032 | tf_op jit(solution)/shard_map/ppermute | solution.py:134
  7.3 58.4 %collective-permute-start.4 = (bf16[2,2,1024,128]{3,2,1,0:T(8,128)(2,1)}, bf16[2,2,1024,128]{3,2,1,0:T(8,128)(2,1)}, u32[]{:S(2)}, u32[]{:S(2)}) collective-permute-start(bf16[2,2,1024,128]{3,2,1,0:T(8,128)(2,1)} %get-tuple-element.70), channel_id=1, source_target_pairs={{0,16},{8,24},{16,0},{24,8},{1,17},{9,25},{17,1},{25,9},{2,18},{10... | collective-permute-start | bytes 3145736 | tf_op jit(solution)/shard_map/ppermute | solution.py:134
  11.9 32.0 %collective-permute-start.1 = (bf16[128,1792]{1,0:T(8,128)(2,1)S(1)}, bf16[128,1792]{1,0:T(8,128)(2,1)S(1)}, u32[]{:S(2)}, u32[]{:S(2)}) collective-permute-start(bf16[128,1792]{1,0:T(8,128)(2,1)S(1)} %get-tuple-element.76), channel_id=1, source_target_pairs={{0,4},{1,5},{2,6},{3,7},{4,0},{5,1},{6,2},{7,3},{8,12},{9,13},{10,... | collective-permute-start | bytes 1376264 | tf_op jit(solution)/shard_map/ppermute | solution.py:138
  77.1 63.0 %collective-permute-start.11 = (bf16[2,256,1792]{2,1,0:T(8,128)(2,1)}, bf16[2,256,1792]{2,1,0:T(8,128)(2,1)}, u32[]{:S(2)}, u32[]{:S(2)}) collective-permute-start(bf16[2,256,1792]{2,1,0:T(8,128)(2,1)} %pad_maximum_fusion.4), channel_id=1, source_target_pairs={{0,16},{8,24},{16,0},{24,8},{1,17},{9,25},{17,1},{25,9},{2,18},{10... | collective-permute-start | bytes 5505032 | tf_op jit(solution)/shard_map/ppermute | solution.py:134
  95.7 44.2 %collective-permute-start.7 = (bf16[2,2,1024,128]{3,2,1,0:T(8,128)(2,1)}, bf16[2,2,1024,128]{3,2,1,0:T(8,128)(2,1)S(1)}, u32[]{:S(2)}, u32[]{:S(2)}) collective-permute-start(bf16[2,2,1024,128]{3,2,1,0:T(8,128)(2,1)} %get-tuple-element.66), channel_id=1, source_target_pairs={{0,8},{8,0},{16,24},{24,16},{1,9},{9,1},{17,25},{25,17},{2,10},{10... | collective-permute-start | bytes 3145736 | tf_op jit(solution)/shard_map/ppermute | solution.py:134
  101.4 33.1 %collective-permute-start.9 = (bf16[128,1792]{1,0:T(8,128)(2,1)}, bf16[128,1792]{1,0:T(8,128)(2,1)}, u32[]{:S(2)}, u32[]{:S(2)}) collective-permute-start(bf16[128,1792]{1,0:T(8,128)(2,1)} %get-tuple-element.73), channel_id=1, source_target_pairs={{0,4},{1,5},{2,6},{3,7},{4,0},{5,1},{6,2},{7,3},{8,12},{9,13},{10,... | collective-permute-start | bytes 1376264 | tf_op jit(solution)/shard_map/ppermute | solution.py:138
  140.1 65.0 %collective-permute-start.19 = (bf16[1024,1792]{1,0:T(8,128)(2,1)S(1)}, bf16[1024,1792]{1,0:T(8,128)(2,1)S(1)}, u32[]{:S(2)}, u32[]{:S(2)}) collective-permute-start(bf16[1024,1792]{1,0:T(8,128)(2,1)S(1)} %dynamic-slice_bitcast_fusion), channel_id=1, source_target_pairs={{0,8},{8,0},{16,24},{24,16},{1,9},{9,1},{17,25},{25,17},{2,10},{10... | collective-permute-start | bytes 11010056 | tf_op jit(solution)/shard_map/ppermute | solution.py:134
  150.4 42.2 %collective-permute-start.18 = (bf16[4,128,1792]{2,1,0:T(8,128)(2,1)S(1)}, bf16[4,128,1792]{2,1,0:T(8,128)(2,1)S(1)}, u32[]{:S(2)}, u32[]{:S(2)}) collective-permute-start(bf16[4,128,1792]{2,1,0:T(8,128)(2,1)S(1)} %pad_maximum_fusion.2), channel_id=1, source_target_pairs={{0,1},{1,0},{2,3},{3,2},{4,5},{5,4},{6,7},{7,6},{8,9},{9,8},{10,11... | collective-permute-start | bytes 5505032 | tf_op jit(solution)/shard_map/ppermute | solution.py:142
  152.2 41.9 %collective-permute-start.17 = (bf16[2,256,1792]{2,1,0:T(8,128)(2,1)S(1)}, bf16[2,256,1792]{2,1,0:T(8,128)(2,1)S(1)}, u32[]{:S(2)}, u32[]{:S(2)}) collective-permute-start(bf16[2,256,1792]{2,1,0:T(8,128)(2,1)S(1)} %pad_maximum_fusion.5), channel_id=1, source_target_pairs={{0,16},{8,24},{16,0},{24,8},{1,17},{9,25},{17,1},{25,9},{2,18},{10... | collective-permute-start | bytes 5505032 | tf_op jit(solution)/shard_map/ppermute | solution.py:134
  205.1 62.0 %collective-permute-start.23 = (bf16[4,256,1792]{2,1,0:T(8,128)(2,1)}, bf16[4,256,1792]{2,1,0:T(8,128)(2,1)}, u32[]{:S(2)}, u32[]{:S(2)}) collective-permute-start(bf16[4,256,1792]{2,1,0:T(8,128)(2,1)} %constant_dynamic-update-slice_fusion.refs_7_), channel_id=1, source_target_pairs={{0,8},{8,0},{16,24},{24,16},{1,9},{9,1},{17,25},{25,17},{2,10},{10... | collective-permute-start | bytes 11010056 | tf_op jit(solution)/shard_map/ppermute | solution.py:134
  205.2 42.4 %collective-permute-start.24 = (bf16[4,128,1792]{2,1,0:T(8,128)(2,1)S(1)}, bf16[4,128,1792]{2,1,0:T(8,128)(2,1)S(1)}, u32[]{:S(2)}, u32[]{:S(2)}) collective-permute-start(bf16[4,128,1792]{2,1,0:T(8,128)(2,1)S(1)} %pad_maximum_fusion.3), channel_id=1, source_target_pairs={{0,1},{1,0},{2,3},{3,2},{4,5},{5,4},{6,7},{7,6},{8,9},{9,8},{10,11... | collective-permute-start | bytes 5505032 | tf_op jit(solution)/shard_map/ppermute | solution.py:142
  212.8 54.3 %collective-permute-start.27 = (bf16[2,256,1792]{2,1,0:T(8,128)(2,1)}, bf16[2,256,1792]{2,1,0:T(8,128)(2,1)}, u32[]{:S(2)}, u32[]{:S(2)}) collective-permute-start(bf16[2,256,1792]{2,1,0:T(8,128)(2,1)} %pad_maximum_fusion.6), channel_id=1, source_target_pairs={{0,16},{8,24},{16,0},{24,8},{1,17},{9,25},{17,1},{25,9},{2,18},{10... | collective-permute-start | bytes 5505032 | tf_op jit(solution)/shard_map/ppermute | solution.py:134
  218.8 35.2 %collective-permute-start.26 = (bf16[8,512,128]{2,1,0:T(8,128)(2,1)S(1)}, bf16[8,512,128]{2,1,0:T(8,128)(2,1)}, u32[]{:S(2)}, u32[]{:S(2)}) collective-permute-start(bf16[8,512,128]{2,1,0:T(8,128)(2,1)S(1)} %get-tuple-element.39.refs_0_), channel_id=1, source_target_pairs={{2,0},{3,1},{4,2},{5,3},{6,4},{7,5},{10,8},{11,9},{12,10},{13,11},... | collective-permute-start | bytes 3145736 | tf_op jit(solution)/shard_map/ppermute | solution.py:150
  233.1 34.1 %collective-permute-start.22 = (bf16[8,512,128]{2,1,0:T(8,128)(2,1)}, bf16[8,512,128]{2,1,0:T(8,128)(2,1)}, u32[]{:S(2)}, u32[]{:S(2)}) collective-permute-start(bf16[8,512,128]{2,1,0:T(8,128)(2,1)} %collective-permute-done.16.refs_5_), channel_id=1, source_target_pairs={{2,0},{3,1},{10,8},{11,9},{18,16},{19,17},{26,24},{27,25}} | collective-permute-start | bytes 3145736 | tf_op jit(solution)/shard_map/ppermute | solution.py:150
  267.2 53.3 %collective-permute-start.28 = (bf16[4,256,1792]{2,1,0:T(8,128)(2,1)}, bf16[4,256,1792]{2,1,0:T(8,128)(2,1)}, u32[]{:S(2)}, u32[]{:S(2)}) collective-permute-start(bf16[4,256,1792]{2,1,0:T(8,128)(2,1)} %constant_dynamic-update-slice_fusion.2.refs_9_), channel_id=1, source_target_pairs={{0,8},{8,0},{16,24},{24,16},{1,9},{9,1},{17,25},{25,17},{2,10},{10... | collective-permute-start | bytes 11010056 | tf_op jit(solution)/shard_map/ppermute | solution.py:134
  267.5 42.6 %collective-permute-start.37 = (bf16[2,256,1792]{2,1,0:T(8,128)(2,1)S(1)}, bf16[2,256,1792]{2,1,0:T(8,128)(2,1)}, u32[]{:S(2)}, u32[]{:S(2)}) collective-permute-start(bf16[2,256,1792]{2,1,0:T(8,128)(2,1)S(1)} %pad_maximum_fusion.7), channel_id=1, source_target_pairs={{0,16},{8,24},{16,0},{24,8},{1,17},{9,25},{17,1},{25,9},{2,18},{10... | collective-permute-start | bytes 5505032 | tf_op jit(solution)/shard_map/ppermute | solution.py:134
  277.4 43.1 %collective-permute-start.29 = (bf16[512,1792]{1,0:T(8,128)(2,1)}, bf16[512,1792]{1,0:T(8,128)(2,1)}, u32[]{:S(2)}, u32[]{:S(2)}) collective-permute-start(bf16[512,1792]{1,0:T(8,128)(2,1)} %get-tuple-element.61), channel_id=1, source_target_pairs={{0,8},{8,0},{16,24},{24,16},{1,9},{9,1},{17,25},{25,17},{2,10},{10... | collective-permute-start | bytes 5505032 | tf_op jit(solution)/shard_map/ppermute | solution.py:134
  279.2 38.5 %collective-permute-start.35 = (bf16[8,512,128]{2,1,0:T(8,128)(2,1)}, bf16[8,512,128]{2,1,0:T(8,128)(2,1)}, u32[]{:S(2)}, u32[]{:S(2)}) collective-permute-start(bf16[8,512,128]{2,1,0:T(8,128)(2,1)} %collective-permute-done.26.refs_4_), channel_id=1, source_target_pairs={{2,0},{3,1},{4,2},{5,3},{10,8},{11,9},{12,10},{13,11},{18,16},{19,... | collective-permute-start | bytes 3145736 | tf_op jit(solution)/shard_map/ppermute | solution.py:150
  280.5 38.5 %collective-permute-start.33 = (bf16[8,512,128]{2,1,0:T(8,128)(2,1)}, bf16[8,512,128]{2,1,0:T(8,128)(2,1)}, u32[]{:S(2)}, u32[]{:S(2)}) collective-permute-start(bf16[8,512,128]{2,1,0:T(8,128)(2,1)} %collective-permute-done.25.refs_1_), channel_id=1, source_target_pairs={{2,4},{3,5},{4,6},{5,7},{10,12},{11,13},{12,14},{13,15},{18,20},{1... | collective-permute-start | bytes 3145736 | tf_op jit(solution)/shard_map/ppermute | solution.py:150
  338.9 43.3 %collective-permute-start.31 = (bf16[512,1792]{1,0:T(8,128)(2,1)}, bf16[512,1792]{1,0:T(8,128)(2,1)}, u32[]{:S(2)}, u32[]{:S(2)}) collective-permute-start(bf16[512,1792]{1,0:T(8,128)(2,1)} %shard_map.46), channel_id=1, source_target_pairs={{0,16},{8,24},{16,0},{24,8},{1,17},{9,25},{17,1},{25,9},{2,18},{10... | collective-permute-start | bytes 5505032 | tf_op jit(solution)/shard_map/ppermute | solution.py:134
  365.0 55.2 %collective-permute-start.40 = (bf16[512,1792]{1,0:T(8,128)(2,1)}, bf16[512,1792]{1,0:T(8,128)(2,1)}, u32[]{:S(2)}, u32[]{:S(2)}) collective-permute-start(bf16[512,1792]{1,0:T(8,128)(2,1)} %shard_map.47), channel_id=1, source_target_pairs={{0,16},{8,24},{16,0},{24,8},{1,17},{9,25},{17,1},{25,9},{2,18},{10... | collective-permute-start | bytes 5505032 | tf_op jit(solution)/shard_map/ppermute | solution.py:134
  366.6 61.4 %collective-permute-start.30 = (bf16[512,1792]{1,0:T(8,128)(2,1)S(1)}, bf16[512,1792]{1,0:T(8,128)(2,1)}, u32[]{:S(2)}, u32[]{:S(2)}) collective-permute-start(bf16[512,1792]{1,0:T(8,128)(2,1)S(1)} %copy-done.2), channel_id=1, source_target_pairs={{0,8},{8,0},{16,24},{24,16},{1,9},{9,1},{17,25},{25,17},{2,10},{10... | collective-permute-start | bytes 5505032 | tf_op jit(solution)/shard_map/ppermute | solution.py:134
  382.2 51.5 %collective-permute-start.32 = (bf16[512,1792]{1,0:T(8,128)(2,1)}, bf16[512,1792]{1,0:T(8,128)(2,1)}, u32[]{:S(2)}, u32[]{:S(2)}) collective-permute-start(bf16[512,1792]{1,0:T(8,128)(2,1)} %collective-permute-done.31), channel_id=1, source_target_pairs={{0,8},{8,0},{16,24},{24,16},{1,9},{9,1},{17,25},{25,17},{2,10},{10... | collective-permute-start | bytes 5505032 | tf_op jit(solution)/shard_map/ppermute | solution.py:134
  382.2 55.8 %collective-permute-start.39 = (bf16[512,1792]{1,0:T(8,128)(2,1)}, bf16[512,1792]{1,0:T(8,128)(2,1)}, u32[]{:S(2)}, u32[]{:S(2)}) collective-permute-start(bf16[512,1792]{1,0:T(8,128)(2,1)} %shard_map.47), channel_id=1, source_target_pairs={{0,8},{8,0},{16,24},{24,16},{1,9},{9,1},{17,25},{25,17},{2,10},{10... | collective-permute-start | bytes 5505032 | tf_op jit(solution)/shard_map/ppermute | solution.py:134
  (45 other events, 846.4 us)

commit v3 on v1

v3 whole, which is shorter than its diff:
```python
import functools

import jax
import jax.numpy as jnp
from jax import lax
from jax.experimental import pallas as pl
from jax.experimental.pallas import tpu as pltpu
from jax.sharding import PartitionSpec as P

F = 7168
SEQS = 2
CHUNKS = (4, 4, 5, 3)
FLAG_ROWS = 16
COL_TILE = 256

smoothing = 0.05


def merge_kernel(copies, shards, starts, place_ref, slot_ref, *refs):
    count = 2 * shards - 1
    sources, refs = refs[:count], refs[count:]
    grads = refs[:copies]
    weights = refs[copies:2 * copies]
    out_ref, acts, sem = refs[2 * copies:]
    rows = acts.shape[2]
    tok = sources[0].shape[2]
    spread = sources[0].shape[0] // copies
    a = place_ref[0]

    def fetch(n, slot):
        for copy in range(copies):
            for part in range(spread):
                pltpu.make_async_copy(
                    sources[n].at[copy * spread + part, pl.ds(starts[n], rows), :],
                    acts.at[copy, slot, :, pl.ds(part * tok, tok)],
                    sem,
                ).start()

    @pl.when(pl.program_id(0) == 0)
    def _():
        fetch(0, 0)
        for slot in range(1, shards):
            @pl.when(a >= slot)
            def _(slot=slot):
                fetch(slot, slot)

            @pl.when(a < slot)
            def _(slot=slot):
                fetch(2 * shards - 1 - slot, slot)
        pltpu.make_async_copy(acts, acts, sem).wait()

    numer = denom = None
    for copy in range(copies):
        sums = []
        lone = slot_ref[copy]
        for first, count in ((0, 1), (1, shards - 1)):
            total = None
            for offset in range(first, first + count):
                slot = lax.rem(lone + offset, shards)
                term = jnp.dot(acts[copy, slot], grads[copy][slot], preferred_element_type=jnp.float32)
                total = term if total is None else total + term
            sums.append(total)
        prior = (sums[0] * sums[0] + sums[1] * sums[1]) * (1.0 / SEQS) + smoothing
        term = prior * weights[copy][...].astype(jnp.float32)
        numer = term if numer is None else numer + term
        denom = prior if denom is None else denom + prior
    out_ref[...] = (numer / denom).astype(out_ref.dtype)


def merge_rows(place, slots, sources, starts, grads, weights):
    copies, shards = len(grads), grads[0].shape[0]
    tok, width = grads[0].shape[1:]
    rows = weights[0].shape[0]
    return pl.pallas_call(
        functools.partial(merge_kernel, copies, shards, starts),
        out_shape=jax.ShapeDtypeStruct((rows, width), jnp.bfloat16),
        grid_spec=pltpu.PrefetchScalarGridSpec(
            num_scalar_prefetch=2,
            grid=(width // COL_TILE,),
            in_specs=[pl.BlockSpec(memory_space=pl.ANY)] * len(sources)
            + [pl.BlockSpec((shards, tok, COL_TILE), lambda j, *_: (0, 0, j))] * copies
            + [pl.BlockSpec((rows, COL_TILE), lambda j, *_: (0, j))] * copies,
            out_specs=pl.BlockSpec((rows, COL_TILE), lambda j, *_: (0, j)),
            scratch_shapes=[
                pltpu.VMEM((copies, shards, rows, tok), jnp.bfloat16),
                pltpu.SemaphoreType.DMA,
            ],
        ),
        compiler_params=pltpu.CompilerParams(vmem_limit_bytes=56 * 1024 * 1024),
        cost_estimate=pl.CostEstimate(
            flops=2 * copies * shards * tok * rows * width,
            bytes_accessed=2 * copies * (shards * tok * (rows + width) + rows * width) + 2 * rows * width,
            transcendentals=0,
        ),
    )(place, slots, *sources, *grads, *weights)


def place_kernel(count, where_ref, *refs):
    pieces, (out_ref, sems) = refs[:count], refs[-2:]
    moves = [
        pltpu.make_async_copy(
            piece,
            out_ref.at[pl.ds(pl.multiple_of(where_ref[n], 16), piece.shape[0]), :],
            sems.at[n],
        )
        for n, piece in enumerate(pieces)
    ]
    for move in moves:
        move.start()
    for move in moves:
        move.wait()


def place_rows(total, pieces, where, whole):
    count = len(pieces)
    shape = jax.ShapeDtypeStruct((total, pieces[0].shape[1]), pieces[0].dtype)
    more = [] if whole is None else [whole]
    return pl.pallas_call(
        functools.partial(place_kernel, count),
        out_shape=shape,
        grid_spec=pltpu.PrefetchScalarGridSpec(
            num_scalar_prefetch=1,
            grid=(1,),
            in_specs=[pl.BlockSpec(memory_space=pl.ANY)] * (count + len(more)),
            out_specs=pl.BlockSpec(memory_space=pl.ANY),
            scratch_shapes=[pltpu.SemaphoreType.DMA((count,))],
        ),
        input_output_aliases={1 + count: 0} if more else {},
        cost_estimate=pl.CostEstimate(
            flops=0, bytes_accessed=4 * sum(p.size for p in pieces), transcendentals=0
        ),
    )(jnp.stack(where).astype(jnp.int32), *pieces, *more)


def after(value, *others):
    return lax.optimization_barrier((value, *others))[0]


def per_device(activations, out_grads, seq_ids, weights):
    copies = lax.axis_size("mp")
    devices = lax.axis_size("fsdp")
    rows, width = weights.shape[1:]
    blocks = F // width
    spread = devices // blocks
    tok = activations.shape[1]
    share = rows // copies
    sizes = [share * n // sum(CHUNKS) for n in CHUNKS]
    starts = [sum(sizes[:k]) for k in range(len(sizes))]
    m = lax.axis_index("mp")
    i = lax.axis_index("fsdp")
    a, h = i // spread, i % spread
    chip, core = m // 2, m % 2

    def to_copy(value, flip):
        return lax.ppermute(value, "mp", [(s, s ^ flip) for s in range(copies)])

    def to_block(value, shift):
        pairs = [(s, (s // spread + shift) % blocks * spread + s % spread) for s in range(devices)]
        return lax.ppermute(value, "fsdp", pairs)

    def to_half(value, shift):
        pairs = [(s, s // spread * spread + (s % spread + shift) % spread) for s in range(devices)]
        return lax.ppermute(value, "fsdp", pairs)

    def along(value, step, direction):
        pairs = [
            (s, s + direction * spread)
            for s in range(devices)
            if 0 <= s // spread + direction < blocks and 0 <= s // spread - direction * (step - 1) < blocks
        ]
        return lax.ppermute(value, "fsdp", pairs)

    def spread_blocks(value):
        cut = [lax.dynamic_slice_in_dim(value, (a + k) % blocks * width, width, 1) for k in range(blocks)]
        return jnp.stack([cut[0]] + [to_block(cut[k], k) for k in range(1, blocks)])

    def over_halves(value):
        return jnp.concatenate([value] + [to_half(value, d) for d in range(1, spread)], axis=1)

    def weight_rows(owner, k):
        return lax.dynamic_slice_in_dim(weights[0], owner * share + starts[k], sizes[k], 0)

    weight_far, weight_mate = [None] * len(sizes), [None] * len(sizes)

    def send_weights(k, *others):
        both = jnp.stack([weight_rows((1 - chip) * 2 + c, k) for c in range(2)])
        weight_far[k] = to_copy(after(both, *others), 2)

    grad_far = to_copy(out_grads[0], 2)
    grad_near = spread_blocks(out_grads[0])

    acts = activations[0].T.reshape(spread, copies // 2, 2, share, tok)
    named = jnp.broadcast_to(seq_ids[0].astype(acts.dtype), acts.shape[:3] + (FLAG_ROWS, tok))
    acts = jnp.concatenate([acts, named], axis=3)
    acts_near = lax.dynamic_index_in_dim(acts, chip, 1, keepdims=False)
    acts_far = lax.dynamic_index_in_dim(acts, 1 - chip, 1, keepdims=False)
    acts_far = to_copy(after(acts_far, grad_far), 2)
    grad_far = spread_blocks(after(grad_far, grad_near))
    send_weights(3, acts_far)
    held = jnp.stack([acts_near, acts_far])
    halves = [lax.dynamic_index_in_dim(held, (h + d) % spread, 1, keepdims=False) for d in range(spread)]
    halves = [halves[0]] + [to_half(halves[d], d) for d in range(1, spread)]
    held = jnp.stack(halves, 1)
    acts_mine = lax.dynamic_index_in_dim(held, core, 2, keepdims=False)
    acts_mate = to_copy(lax.dynamic_index_in_dim(held, 1 - core, 2, keepdims=False), 1)
    own = jnp.stack([acts_mine, acts_mate], 1).reshape(copies * spread, share + FLAG_ROWS, tok)

    grads = [None] * copies
    stage = (own, grad_far, weight_far[3])
    low, high = [along(after(own, *stage), 1, 1)], [along(after(own, *stage), 1, -1)]
    send_weights(0, *stage)
    grads[0] = over_halves(after(grad_near, *stage))
    mate_rows = lax.dynamic_slice_in_dim(weights[0], (chip * 2 + 1 - core) * share, share, 0)
    mate_rows = to_copy(after(mate_rows, *stage), 1)

    stage = (low[0], high[0], weight_far[0], grads[0], mate_rows)
    low.append(along(after(low[0], *stage), 2, 1))
    high.append(along(after(high[0], *stage), 2, -1))
    send_weights(1, *stage)
    grads[2] = over_halves(after(grad_far, *stage))
    grads[1] = to_copy(after(grads[0], *stage), 1)
    named = jnp.where(a == 0, high[0][:, share, 0], jnp.where(a == blocks - 1, low[0][:, share, 0], own[:, share, 0]))
    alone = jnp.where(named[::spread] > 0.5, 0, blocks - 1)
    slots = ((a - alone) % blocks).astype(jnp.int32)
    place = a.astype(jnp.int32)[None]

    stage = (low[1], high[1], weight_far[1], grads[1], grads[2])
    grads[3] = to_copy(after(grads[2], *stage), 1)
    send_weights(2, *stage)
    half = starts[2]
    low_last, high_last = [], []
    for first, count in ((0, half), (half, share - half)):
        cut = (slice(None), slice(first, first + count))
        low_last.append(along(after(low[1][cut], *stage), 3, 1))
        high_last.append(along(after(high[1][cut], *stage), 3, -1))

    wholes = [None]
    for k in range(len(sizes)):
        mine = lax.dynamic_index_in_dim(weight_far[k], core, 0, keepdims=False)
        mate = to_copy(lax.dynamic_index_in_dim(weight_far[k], 1 - core, 0, keepdims=False), 1)
        held = [weight_rows(m, k), mate_rows[starts[k]:starts[k] + sizes[k]], mine, mate]
        part = k // 2
        sources = [own, low[0], low[1], low_last[part], high[0], high[1], high_last[part]]
        begin = [starts[k]] * 7
        begin[3] = begin[6] = starts[k] - part * half
        mine = merge_rows(place, slots, sources, begin, grads, held)
        place = after(place, mine)
        if k == len(sizes) - 1:
            mine = after(mine, wholes[-2])
        far = to_copy(mine, 2)
        pieces = [mine, to_copy(mine, 1), far, to_copy(far, 1)]
        where = [(m ^ flip) * share + starts[k] for flip in range(copies)]
        wholes.append(place_rows(rows, pieces, where, wholes[-1]))
    return wholes[-1]


def solution(mesh):
    placed = (P("mp", "fsdp", None), P("mp", "fsdp", None), P("mp", "fsdp"), P("mp", "fsdp", None))
    return jax.shard_map(
        per_device, mesh=mesh, in_specs=placed, out_specs=P("fsdp", None), check_vma=False
    )
```

time: 517 us -> 887 us (1.72)
  Pallas kernels: 36.9 us -> 506 us
  blocking collectives: 111 us -> 0 us
  waiting for transfers between devices: 240 us -> 266 us
  starting transfers between devices: 53.1 us -> 38.5 us
  local copies, waits for them, and re-layouts: 64.9 us -> 54.8 us
  other arithmetic: 9.95 us -> 19.1 us
    pallas_call x2 -> x8, Pallas kernels: 36.9 us -> 506 us  [the longest x4 452 us: place_rows(): pl.pallas_call(functools.partial(place_kernel, count), out_shape=shape, g...]
    psum x1 -> x0, blocking collectives: 111 us -> none  [per_device(): lax.psum(jnp.where(jnp.arange(copies) == m, mine, 0), ('mp', 'fsdp'))]
    ppermute x12 -> x8, waiting for transfers between devices: 71.2 us -> 8.62 us  [along(): return lax.ppermute(value, 'fsdp', pairs)]
    ppermute x2 -> x3, waiting for transfers between devices: 34.6 us -> 88.9 us  [to_half(): return lax.ppermute(value, 'fsdp', pairs)]
    ppermute x6, waiting for transfers between devices: 29.4 us -> 51.2 us  [to_block(): return lax.ppermute(value, 'fsdp', pairs)]
    dynamic_update_slice x8 -> x0, local copies, waits for them, and re-layouts: 19.9 us -> none  [per_device(): lax.dynamic_update_slice_in_dim(merged, value, (m ^ flip) * share + chunk...]
    ppermute x15 -> x26, waiting for transfers between devices: 99.2 us -> 117 us  [to_copy(): return lax.ppermute(value, 'mp', [(s, s ^ flip) for s in range(copies)])]
    ppermute x12 -> x8, starting transfers between devices: 24 us -> 9.26 us  [along(): return lax.ppermute(value, 'fsdp', pairs)]
  transfers between devices with their start and end apart: 42 -> 43, of which waited for: 14 -> 14; matrix products, arithmetic and copies ran while one was open for 12% -> 7% of each run, Pallas kernels for 7% -> 48%
where the time goes in v3:
time: 887 us; the launch traced here: 885 us
  Pallas kernels  506 us (57%)
  waiting for transfers between devices  266 us (30%)
  local copies, waits for them, and re-layouts  54.8 us (6%)
  starting transfers between devices  38.5 us (4%)
  other arithmetic  19.1 us (2%)
    pallas_call x4, Pallas kernels, place_rows(): pl.pallas_call(functools.partial(place_kernel, count), out_shape=shape, g...  452 us
    ppermute x26, waiting for transfers between devices, to_copy(): return lax.ppermute(value, 'mp', [(s, s ^ flip) for s in range(copies)])  117 us
    ppermute x3, waiting for transfers between devices, to_half(): return lax.ppermute(value, 'fsdp', pairs)  88.9 us
    pallas_call x4, Pallas kernels, merge_rows(): pl.pallas_call(functools.partial(merge_kernel, copies, shards, starts), o...  54 us
    ppermute x6, waiting for transfers between devices, to_block(): return lax.ppermute(value, 'fsdp', pairs)  51.2 us
  transfers between devices with their start and end apart: 43, of which 14 were waited for; matrix products, arithmetic and copies ran while one was open for 7% of the time, Pallas kernels for 48%

profile of v3, /device:TPU:0, one launch (start us, length us, event | category | flops | bytes accessed | tf_op | source)
XLA Modules:
  0.0 884.8 jit_solution(16717138622305679433)
XLA Ops:
  2.9 3.2 copy.8
  7.4 35.9 %collective-permute-done = bf16[128,7168]{1,0:T(8,128)(2,1)} collective-permute-done((bf16[128,7168]{1,0:T(8,128)(2,1)}, bf16[128,7168]{1,0:T(8,128)(2,1)}, u32[]{:S(2)}, u32[]{:S(2)}) %collective-permute-start) | collective-permute-done | bytes 1835040 | tf_op jit(solution)/shard_map/ppermute | solution.py:155
  45.0 23.2 %collective-permute-done.1 = bf16[2,2,1040,128]{3,2,1,0:T(8,128)(2,1)S(1)} collective-permute-done((bf16[2,2,1040,128]{3,2,1,0:T(8,128)(2,1)}, bf16[2,2,1040,128]{3,2,1,0:T(8,128)(2,1)S(1)}, u32[]{:S(2)}, u32[]{:S(2)}) %collective-permute-start.1) | collective-permute-done | bytes 1064992 | tf_op jit(solution)/shard_map/ppermute | solution.py:155
  75.5 3.6 collective-permute-start.6
  85.3 10.2 %collective-permute-done.2 = bf16[2,2,1040,128]{3,2,1,0:T(8,128)(2,1)S(1)} collective-permute-done((bf16[2,2,1040,128]{3,2,1,0:T(8,128)(2,1)}, bf16[2,2,1040,128]{3,2,1,0:T(8,128)(2,1)S(1)}, u32[]{:S(2)}, u32[]{:S(2)}) %collective-permute-start.2) | collective-permute-done | bytes 1064992 | tf_op jit(solution)/shard_map/ppermute | solution.py:163
  99.0 17.6 %collective-permute-done.5 = bf16[128,1792]{1,0:T(8,128)(2,1)} collective-permute-done((bf16[128,1792]{1,0:T(8,128)(2,1)}, bf16[128,1792]{1,0:T(8,128)(2,1)}, u32[]{:S(2)}, u32[]{:S(2)}) %collective-permute-start.5) | collective-permute-done | bytes 458784 | tf_op jit(solution)/shard_map/ppermute | solution.py:159
  126.5 4.1 dynamic-slice_bitcast_fusion
  133.0 31.1 %collective-permute-done.8 = bf16[128,1792]{1,0:T(8,128)(2,1)} collective-permute-done((bf16[128,1792]{1,0:T(8,128)(2,1)S(1)}, bf16[128,1792]{1,0:T(8,128)(2,1)}, u32[]{:S(2)}, u32[]{:S(2)}) %collective-permute-start.8) | collective-permute-done | bytes 458784 | tf_op jit(solution)/shard_map/ppermute | solution.py:159
  171.3 4.2 dynamic-slice_bitcast_fusion.6
  177.9 39.9 %collective-permute-done.14 = bf16[4,128,1792]{2,1,0:T(8,128)(2,1)S(1)} collective-permute-done((bf16[4,128,1792]{2,1,0:T(8,128)(2,1)S(1)}, bf16[4,128,1792]{2,1,0:T(8,128)(2,1)S(1)}, u32[]{:S(2)}, u32[]{:S(2)}) %collective-permute-start.14) | collective-permute-done | bytes 1835040 | tf_op jit(solution)/shard_map/ppermute | solution.py:163
  226.3 38.8 %collective-permute-done.20 = bf16[4,128,1792]{2,1,0:T(8,128)(2,1)S(1)} collective-permute-done((bf16[4,128,1792]{2,1,0:T(8,128)(2,1)S(1)}, bf16[4,128,1792]{2,1,0:T(8,128)(2,1)S(1)}, u32[]{:S(2)}, u32[]{:S(2)}) %collective-permute-start.20) | collective-permute-done | bytes 1835040 | tf_op jit(solution)/shard_map/ppermute | solution.py:163
  266.6 6.3 collective-permute-done.17.refs_5_
  276.1 3.2 constant_dynamic-slice_fusion.1
  297.5 36.0 %collective-permute-done.28 = bf16[2,320,1792]{2,1,0:T(8,128)(2,1)} collective-permute-done((bf16[2,320,1792]{2,1,0:T(8,128)(2,1)}, bf16[2,320,1792]{2,1,0:T(8,128)(2,1)}, u32[]{:S(2)}, u32[]{:S(2)}) %collective-permute-start.28) | collective-permute-done | bytes 2293792 | tf_op jit(solution)/shard_map/ppermute | solution.py:155
  339.4 13.5 %shard_map.46.refs_0_ = bf16[256,1792]{1,0:T(8,128)(2,1)} custom-call(s32[1]{0:T(128)} %bitcast.4.place_ref, s32[4]{0:T(128)} %and_select_fusion.slot_ref, bf16[8,1040,128]{2,1,0:T(8,128)(2,1)} %bitcast.82, bf16[8,1040,128]{2,1,0:T(8,128)(2,1)} %copy-done.6, bf16[8,1040,128]{2,1,0:T(8,128)(2,1)} %copy-done.3, bf16[8,512,128]{2,1,0:T(8,128)(2,1)} %copy-done.13, ...), custom_call_target="tpu_custom_call" | custom-call | flops 3758096384 | bytes 21364736 | tf_op jit(solution)/shard_map/pallas_call | solution.py:74
  354.4 13.5 %shard_map.47.refs_0_ = bf16[256,1792]{1,0:T(8,128)(2,1)} custom-call(s32[1]{0:T(128)} %bitcast.4.place_ref, s32[4]{0:T(128)} %and_select_fusion.slot_ref, bf16[8,1040,128]{2,1,0:T(8,128)(2,1)} %bitcast.83, bf16[8,1040,128]{2,1,0:T(8,128)(2,1)} %copy-done.6, bf16[8,1040,128]{2,1,0:T(8,128)(2,1)} %copy-done.3, bf16[8,512,128]{2,1,0:T(8,128)(2,1)} %copy-done.13, ...), custom_call_target="tpu_custom_call" | custom-call | flops 3758096384 | bytes 21364736 | tf_op jit(solution)/shard_map/pallas_call | solution.py:74
  375.0 14.5 %shard_map.48.refs_0_ = bf16[320,1792]{1,0:T(8,128)(2,1)} custom-call(s32[1]{0:T(128)} %bitcast.4.place_ref, s32[4]{0:T(128)} %and_select_fusion.slot_ref, bf16[8,1040,128]{2,1,0:T(8,128)(2,1)} %bitcast.84, bf16[8,1040,128]{2,1,0:T(8,128)(2,1)} %copy-done.6, bf16[8,1040,128]{2,1,0:T(8,128)(2,1)} %copy-done.3, bf16[8,512,128]{2,1,0:T(8,128)(2,1)} %copy-done.11, ...), custom_call_target="tpu_custom_call" | custom-call | flops 4697620480 | bytes 23035904 | tf_op jit(solution)/shard_map/pallas_call | solution.py:74
  389.9 5.0 collective-permute-done.32.refs_2_
  399.7 12.5 %shard_map.49.refs_0_ = bf16[192,1792]{1,0:T(8,128)(2,1)} custom-call(s32[1]{0:T(128)} %bitcast.4.place_ref, s32[4]{0:T(128)} %and_select_fusion.slot_ref, bf16[8,1040,128]{2,1,0:T(8,128)(2,1)} %bitcast.85, bf16[8,1040,128]{2,1,0:T(8,128)(2,1)} %copy-done.6, bf16[8,1040,128]{2,1,0:T(8,128)(2,1)} %copy-done.3, bf16[8,512,128]{2,1,0:T(8,128)(2,1)} %copy-done.11, ...), custom_call_target="tpu_custom_call" | custom-call | flops 2818572288 | bytes 19693568 | tf_op jit(solution)/shard_map/pallas_call | solution.py:74
  413.1 113.0 %shard_map.50.refs_4_ = bf16[4096,1792]{1,0:T(8,128)(2,1)} custom-call(s32[4]{0:T(128)} %pad_add_fusion.2.where_ref, bf16[256,1792]{1,0:T(8,128)(2,1)} %shard_map.46.refs_0_, bf16[256,1792]{1,0:T(8,128)(2,1)} %collective-permute-done.34.refs_1_, bf16[256,1792]{1,0:T(8,128)(2,1)} %collective-permute-done.35.refs_2_, bf16[256,1792]{1,0:T(8,128)(2,1)} %copy-done.25), custom_call_target="tpu_custom_call" | custom-call | bytes 7340032 | tf_op jit(solution)/shard_map/pallas_call | solution.py:118
  526.1 113.1 %shard_map.51.refs_4_ = bf16[4096,1792]{1,0:T(8,128)(2,1)} custom-call(s32[4]{0:T(128)} %pad_add_fusion.1.where_ref, bf16[256,1792]{1,0:T(8,128)(2,1)} %shard_map.47.refs_0_, bf16[256,1792]{1,0:T(8,128)(2,1)} %collective-permute-done.31.refs_1_, bf16[256,1792]{1,0:T(8,128)(2,1)} %collective-permute-done.32.refs_2_, ...), custom_call_target="tpu_custom_call", output_to_operand_aliasing={{}: (5, {})} | custom-call | bytes 7340032 | tf_op jit(solution)/shard_map/pallas_call | solution.py:118
  640.4 16.5 %collective-permute-done.38.refs_2_ = bf16[192,1792]{1,0:T(8,128)(2,1)} collective-permute-done((bf16[192,1792]{1,0:T(8,128)(2,1)S(1)}, bf16[192,1792]{1,0:T(8,128)(2,1)}, u32[]{:S(2)}, u32[]{:S(2)}) %collective-permute-start.38) | collective-permute-done | bytes 688160 | tf_op jit(solution)/shard_map/ppermute | solution.py:155
  658.6 140.8 %shard_map.52.refs_4_ = bf16[4096,1792]{1,0:T(8,128)(2,1)} custom-call(s32[4]{0:T(128)} %get-tuple-element.90.where_ref, bf16[320,1792]{1,0:T(8,128)(2,1)} %shard_map.48.refs_0_, bf16[320,1792]{1,0:T(8,128)(2,1)} %copy-done.21, bf16[320,1792]{1,0:T(8,128)(2,1)} %collective-permute-done.41.refs_2_, ...), custom_call_target="tpu_custom_call", output_to_operand_aliasing={{}: (5, {})} | custom-call | bytes 9175040 | tf_op jit(solution)/shard_map/pallas_call | solution.py:118
  799.4 85.2 %shard_map.53 = bf16[4096,1792]{1,0:T(8,128)(2,1)} custom-call(s32[4]{0:T(128)} %get-tuple-element.89.where_ref, bf16[192,1792]{1,0:T(8,128)(2,1)} %shard_map.49.refs_0_, bf16[192,1792]{1,0:T(8,128)(2,1)} %collective-permute-done.37.refs_1_, bf16[192,1792]{1,0:T(8,128)(2,1)} %collective-permute-done.38.refs_2_, ...), custom_call_target="tpu_custom_call", output_to_operand_aliasing={{}: (5, {})} | custom-call | bytes 5505024 | tf_op jit(solution)/shard_map/pallas_call | solution.py:118
  (162 shorter events, 99.2 us)
Async XLA Ops:
  0.0 43.3 %collective-permute-start = (bf16[128,7168]{1,0:T(8,128)(2,1)}, bf16[128,7168]{1,0:T(8,128)(2,1)}, u32[]{:S(2)}, u32[]{:S(2)}) collective-permute-start(bf16[128,7168]{1,0:T(8,128)(2,1)} %bitcast.87), channel_id=1, source_target_pairs={{0,16},{8,24},{16,0},{24,8},{1,17},{9,25},{17,1},{25,9},{2,18},{10... | collective-permute-start | bytes 5505032 | tf_op jit(solution)/shard_map/ppermute | solution.py:155
  83.9 84.3 %collective-permute-start.10 = (bf16[2,192,1792]{2,1,0:T(8,128)(2,1)}, bf16[2,192,1792]{2,1,0:T(8,128)(2,1)}, u32[]{:S(2)}, u32[]{:S(2)}) collective-permute-start(bf16[2,192,1792]{2,1,0:T(8,128)(2,1)} %pad_maximum_fusion.6), channel_id=1, source_target_pairs={{0,16},{8,24},{16,0},{24,8},{1,17},{9,25},{17,1},{25,9},{2,18},{10... | collective-permute-start | bytes 4128776 | tf_op jit(solution)/shard_map/ppermute | solution.py:155
  98.9 67.8 %collective-permute-start.3 = (bf16[2,2,1040,128]{3,2,1,0:T(8,128)(2,1)}, bf16[2,2,1040,128]{3,2,1,0:T(8,128)(2,1)}, u32[]{:S(2)}, u32[]{:S(2)}) collective-permute-start(bf16[2,2,1040,128]{3,2,1,0:T(8,128)(2,1)} %get-tuple-element.70), channel_id=1, source_target_pairs={{0,8},{8,0},{16,24},{24,16},{1,9},{9,1},{17,25},{25,17},{2,10},{10... | collective-permute-start | bytes 3194888 | tf_op jit(solution)/shard_map/ppermute | solution.py:155
  121.6 42.5 %collective-permute-start.8 = (bf16[128,1792]{1,0:T(8,128)(2,1)S(1)}, bf16[128,1792]{1,0:T(8,128)(2,1)}, u32[]{:S(2)}, u32[]{:S(2)}) collective-permute-start(bf16[128,1792]{1,0:T(8,128)(2,1)S(1)} %get-tuple-element.81), channel_id=1, source_target_pairs={{0,4},{1,5},{2,6},{3,7},{4,0},{5,1},{6,2},{7,3},{8,12},{9,13},{10,... | collective-permute-start | bytes 1376264 | tf_op jit(solution)/shard_map/ppermute | solution.py:159
  168.2 52.3 %collective-permute-start.15 = (bf16[1024,1792]{1,0:T(8,128)(2,1)}, bf16[1024,1792]{1,0:T(8,128)(2,1)}, u32[]{:S(2)}, u32[]{:S(2)}) collective-permute-start(bf16[1024,1792]{1,0:T(8,128)(2,1)} %dynamic-slice_bitcast_fusion), channel_id=1, source_target_pairs={{0,8},{8,0},{16,24},{24,16},{1,9},{9,1},{17,25},{25,17},{2,10},{10... | collective-permute-start | bytes 11010056 | tf_op jit(solution)/shard_map/ppermute | solution.py:155
  168.3 49.9 %collective-permute-start.12 = (bf16[8,1040,128]{2,1,0:T(8,128)(2,1)S(1)}, bf16[8,1040,128]{2,1,0:T(8,128)(2,1)S(1)}, u32[]{:S(2)}, u32[]{:S(2)}) collective-permute-start(bf16[8,1040,128]{2,1,0:T(8,128)(2,1)S(1)} %bitcast.79), channel_id=1, source_target_pairs={{0,2},{1,3},{2,4},{3,5},{4,6},{5,7},{8,10},{9,11},{10,12},{11,13},... | collective-permute-start | bytes 6389768 | tf_op jit(solution)/shard_map/ppermute | solution.py:171
  170.0 50.4 %collective-permute-start.11 = (bf16[8,1040,128]{2,1,0:T(8,128)(2,1)S(1)}, bf16[8,1040,128]{2,1,0:T(8,128)(2,1)S(1)}, u32[]{:S(2)}, u32[]{:S(2)}) collective-permute-start(bf16[8,1040,128]{2,1,0:T(8,128)(2,1)S(1)} %bitcast.80), channel_id=1, source_target_pairs={{2,0},{3,1},{4,2},{5,3},{6,4},{7,5},{10,8},{11,9},{12,10},{13,11},... | collective-permute-start | bytes 6389768 | tf_op jit(solution)/shard_map/ppermute | solution.py:171
  175.5 42.2 %collective-permute-start.14 = (bf16[4,128,1792]{2,1,0:T(8,128)(2,1)S(1)}, bf16[4,128,1792]{2,1,0:T(8,128)(2,1)S(1)}, u32[]{:S(2)}, u32[]{:S(2)}) collective-permute-start(bf16[4,128,1792]{2,1,0:T(8,128)(2,1)S(1)} %copy-done.8), channel_id=1, source_target_pairs={{0,1},{1,0},{2,3},{3,2},{4,5},{5,4},{6,7},{7,6},{8,9},{9,8},{10,11... | collective-permute-start | bytes 5505032 | tf_op jit(solution)/shard_map/ppermute | solution.py:163
  176.2 42.0 %collective-permute-start.13 = (bf16[2,256,1792]{2,1,0:T(8,128)(2,1)S(1)}, bf16[2,256,1792]{2,1,0:T(8,128)(2,1)S(1)}, u32[]{:S(2)}, u32[]{:S(2)}) collective-permute-start(bf16[2,256,1792]{2,1,0:T(8,128)(2,1)S(1)} %pad_maximum_fusion.4), channel_id=1, source_target_pairs={{0,16},{8,24},{16,0},{24,8},{1,17},{9,25},{17,1},{25,9},{2,18},{10... | collective-permute-start | bytes 5505032 | tf_op jit(solution)/shard_map/ppermute | solution.py:155
  220.5 52.4 %collective-permute-start.19 = (bf16[4,256,1792]{2,1,0:T(8,128)(2,1)S(1)}, bf16[4,256,1792]{2,1,0:T(8,128)(2,1)S(1)}, u32[]{:S(2)}, u32[]{:S(2)}) collective-permute-start(bf16[4,256,1792]{2,1,0:T(8,128)(2,1)S(1)} %constant_dynamic-update-slice_fusion.refs_7_), channel_id=1, source_target_pairs={{0,8},{8,0},{16,24},{24,16},{1,9},{9,1},{17,25},{25,17},{2,10},{10... | collective-permute-start | bytes 11010056 | tf_op jit(solution)/shard_map/ppermute | solution.py:155
  220.6 46.0 %collective-permute-start.16 = (bf16[8,1040,128]{2,1,0:T(8,128)(2,1)S(1)}, bf16[8,1040,128]{2,1,0:T(8,128)(2,1)S(1)}, u32[]{:S(2)}, u32[]{:S(2)}) collective-permute-start(bf16[8,1040,128]{2,1,0:T(8,128)(2,1)S(1)} %collective-permute-done.12.refs_1_), channel_id=1, source_target_pairs={{2,4},{3,5},{4,6},{5,7},{10,12},{11,13},{12,14},{13,15},{18,20},{1... | collective-permute-start | bytes 6389768 | tf_op jit(solution)/shard_map/ppermute | solution.py:171
  221.4 51.5 %collective-permute-start.17 = (bf16[8,1040,128]{2,1,0:T(8,128)(2,1)S(1)}, bf16[8,1040,128]{2,1,0:T(8,128)(2,1)S(1)}, u32[]{:S(2)}, u32[]{:S(2)}) collective-permute-start(bf16[8,1040,128]{2,1,0:T(8,128)(2,1)S(1)} %collective-permute-done.11.refs_4_), channel_id=1, source_target_pairs={{2,0},{3,1},{4,2},{5,3},{10,8},{11,9},{12,10},{13,11},{18,16},{19,... | collective-permute-start | bytes 6389768 | tf_op jit(solution)/shard_map/ppermute | solution.py:171
  222.7 42.5 %collective-permute-start.20 = (bf16[4,128,1792]{2,1,0:T(8,128)(2,1)S(1)}, bf16[4,128,1792]{2,1,0:T(8,128)(2,1)S(1)}, u32[]{:S(2)}, u32[]{:S(2)}) collective-permute-start(bf16[4,128,1792]{2,1,0:T(8,128)(2,1)S(1)} %copy-done.9), channel_id=1, source_target_pairs={{0,1},{1,0},{2,3},{3,2},{4,5},{5,4},{6,7},{7,6},{8,9},{9,8},{10,11... | collective-permute-start | bytes 5505032 | tf_op jit(solution)/shard_map/ppermute | solution.py:163
  223.4 43.1 %collective-permute-start.18 = (bf16[2,256,1792]{2,1,0:T(8,128)(2,1)S(1)}, bf16[2,256,1792]{2,1,0:T(8,128)(2,1)S(1)}, u32[]{:S(2)}, u32[]{:S(2)}) collective-permute-start(bf16[2,256,1792]{2,1,0:T(8,128)(2,1)S(1)} %pad_maximum_fusion.5), channel_id=1, source_target_pairs={{0,16},{8,24},{16,0},{24,8},{1,17},{9,25},{17,1},{25,9},{2,18},{10... | collective-permute-start | bytes 5505032 | tf_op jit(solution)/shard_map/ppermute | solution.py:155
  276.1 62.4 %collective-permute-start.23 = (bf16[4,256,1792]{2,1,0:T(8,128)(2,1)}, bf16[4,256,1792]{2,1,0:T(8,128)(2,1)}, u32[]{:S(2)}, u32[]{:S(2)}) collective-permute-start(bf16[4,256,1792]{2,1,0:T(8,128)(2,1)} %constant_dynamic-update-slice_fusion.2.refs_9_), channel_id=1, source_target_pairs={{0,8},{8,0},{16,24},{24,16},{1,9},{9,1},{17,25},{25,17},{2,10},{10... | collective-permute-start | bytes 11010056 | tf_op jit(solution)/shard_map/ppermute | solution.py:155
  280.9 52.6 %collective-permute-start.28 = (bf16[2,320,1792]{2,1,0:T(8,128)(2,1)}, bf16[2,320,1792]{2,1,0:T(8,128)(2,1)}, u32[]{:S(2)}, u32[]{:S(2)}) collective-permute-start(bf16[2,320,1792]{2,1,0:T(8,128)(2,1)} %pad_maximum_fusion), channel_id=1, source_target_pairs={{0,16},{8,24},{16,0},{24,8},{1,17},{9,25},{17,1},{25,9},{2,18},{10... | collective-permute-start | bytes 6881288 | tf_op jit(solution)/shard_map/ppermute | solution.py:155
  290.9 46.0 %collective-permute-start.21 = (bf16[8,512,128]{2,1,0:T(8,128)(2,1)S(1)}, bf16[8,512,128]{2,1,0:T(8,128)(2,1)S(1)}, u32[]{:S(2)}, u32[]{:S(2)}) collective-permute-start(bf16[8,512,128]{2,1,0:T(8,128)(2,1)S(1)} %get-tuple-element.39), channel_id=1, source_target_pairs={{4,6},{5,7},{12,14},{13,15},{20,22},{21,23},{28,30},{29,31}} | collective-permute-start | bytes 3145736 | tf_op jit(solution)/shard_map/ppermute | solution.py:171
  291.6 46.8 %collective-permute-start.22 = (bf16[8,512,128]{2,1,0:T(8,128)(2,1)S(1)}, bf16[8,512,128]{2,1,0:T(8,128)(2,1)S(1)}, u32[]{:S(2)}, u32[]{:S(2)}) collective-permute-start(bf16[8,512,128]{2,1,0:T(8,128)(2,1)S(1)} %get-tuple-element.40), channel_id=1, source_target_pairs={{2,0},{3,1},{10,8},{11,9},{18,16},{19,17},{26,24},{27,25}} | collective-permute-start | bytes 3145736 | tf_op jit(solution)/shard_map/ppermute | solution.py:171
  294.4 60.1 %collective-permute-start.25 = (bf16[256,1792]{1,0:T(8,128)(2,1)}, bf16[256,1792]{1,0:T(8,128)(2,1)}, u32[]{:S(2)}, u32[]{:S(2)}) collective-permute-start(bf16[256,1792]{1,0:T(8,128)(2,1)} %get-tuple-element.75), channel_id=1, source_target_pairs={{0,8},{8,0},{16,24},{24,16},{1,9},{9,1},{17,25},{25,17},{2,10},{10... | collective-permute-start | bytes 2752520 | tf_op jit(solution)/shard_map/ppermute | solution.py:155
  373.6 152.5 %collective-permute-start.31 = (bf16[256,1792]{1,0:T(8,128)(2,1)S(1)}, bf16[256,1792]{1,0:T(8,128)(2,1)}, u32[]{:S(2)}, u32[]{:S(2)}) collective-permute-start(bf16[256,1792]{1,0:T(8,128)(2,1)S(1)} %copy-done.15), channel_id=1, source_target_pairs={{0,8},{8,0},{16,24},{24,16},{1,9},{9,1},{17,25},{25,17},{2,10},{10... | collective-permute-start | bytes 2752520 | tf_op jit(solution)/shard_map/ppermute | solution.py:155
  394.9 131.2 %collective-permute-start.33 = (bf16[256,1792]{1,0:T(8,128)(2,1)}, bf16[256,1792]{1,0:T(8,128)(2,1)}, u32[]{:S(2)}, u32[]{:S(2)}) collective-permute-start(bf16[256,1792]{1,0:T(8,128)(2,1)} %collective-permute-done.32.refs_2_), channel_id=1, source_target_pairs={{0,8},{8,0},{16,24},{24,16},{1,9},{9,1},{17,25},{25,17},{2,10},{10... | collective-permute-start | bytes 2752520 | tf_op jit(solution)/shard_map/ppermute | solution.py:155
  394.9 245.0 %collective-permute-start.41 = (bf16[320,1792]{1,0:T(8,128)(2,1)}, bf16[320,1792]{1,0:T(8,128)(2,1)}, u32[]{:S(2)}, u32[]{:S(2)}) collective-permute-start(bf16[320,1792]{1,0:T(8,128)(2,1)} %shard_map.48.refs_0_), channel_id=1, source_target_pairs={{0,16},{8,24},{16,0},{24,8},{1,17},{9,25},{17,1},{25,9},{2,18},{10... | collective-permute-start | bytes 3440648 | tf_op jit(solution)/shard_map/ppermute | solution.py:155
  640.4 159.0 %collective-permute-start.37 = (bf16[192,1792]{1,0:T(8,128)(2,1)S(1)}, bf16[192,1792]{1,0:T(8,128)(2,1)}, u32[]{:S(2)}, u32[]{:S(2)}) collective-permute-start(bf16[192,1792]{1,0:T(8,128)(2,1)S(1)} %copy-done.16), channel_id=1, source_target_pairs={{0,8},{8,0},{16,24},{24,16},{1,9},{9,1},{17,25},{25,17},{2,10},{10... | collective-permute-start | bytes 2064392 | tf_op jit(solution)/shard_map/ppermute | solution.py:155
  657.0 142.4 %collective-permute-start.39 = (bf16[192,1792]{1,0:T(8,128)(2,1)}, bf16[192,1792]{1,0:T(8,128)(2,1)}, u32[]{:S(2)}, u32[]{:S(2)}) collective-permute-start(bf16[192,1792]{1,0:T(8,128)(2,1)} %collective-permute-done.38.refs_2_), channel_id=1, source_target_pairs={{0,8},{8,0},{16,24},{24,16},{1,9},{9,1},{17,25},{25,17},{2,10},{10... | collective-permute-start | bytes 2064392 | tf_op jit(solution)/shard_map/ppermute | solution.py:155
  (46 other events, 1060.4 us)

commit v4 on v3

v4 whole, which is shorter than its diff:
```python
import functools

import jax
import jax.numpy as jnp
from jax import lax
from jax.experimental import pallas as pl
from jax.experimental.pallas import tpu as pltpu
from jax.sharding import PartitionSpec as P

F = 7168
SEQS = 2
CHUNKS = (16, 20, 20, 8)
FLAG_ROWS = 16
COL_TILE = 256

smoothing = 0.05


def merge_kernel(copies, shards, starts, sizes, place_ref, slot_ref, *refs):
    count = 2 * shards - 1
    sources, refs = refs[:count], refs[count:]
    grads = refs[:copies]
    weights, (out_ref, acts, sem) = refs[copies:-3], refs[-3:]
    rows = acts.shape[2]
    tok = sources[0].shape[2]
    spread = sources[0].shape[0] // copies
    a, m, h = place_ref[0], place_ref[1], place_ref[2]

    def fetch(n, slot):
        for copy in range(copies):
            for part in range(spread):
                pltpu.make_async_copy(
                    sources[n].at[
                        lax.bitwise_xor(m, copy) * spread + lax.rem(h + spread - part, spread),
                        pl.ds(starts[n], rows),
                        :,
                    ],
                    acts.at[copy, slot, :, pl.ds(part * tok, tok)],
                    sem,
                ).start()

    @pl.when(pl.program_id(0) == 0)
    def _():
        fetch(0, 0)
        for slot in range(1, shards):
            @pl.when(a >= slot)
            def _(slot=slot):
                fetch(slot, slot)

            @pl.when(a < slot)
            def _(slot=slot):
                fetch(2 * shards - 1 - slot, slot)
        pltpu.make_async_copy(acts, acts, sem).wait()

    first = 0
    for piece, size in enumerate(sizes):
        at = slice(first, first + size)
        numer = denom = None
        for copy in range(copies):
            sums = []
            lone = slot_ref[copy]
            for offset, count in ((0, 1), (1, shards - 1)):
                total = None
                for n in range(offset, offset + count):
                    slot = lax.rem(lone + n, shards)
                    term = jnp.dot(
                        acts[copy, slot, at, :], grads[copy][slot], preferred_element_type=jnp.float32
                    )
                    total = term if total is None else total + term
                sums.append(total)
            prior = (sums[0] * sums[0] + sums[1] * sums[1]) * (1.0 / SEQS) + smoothing
            term = prior * weights[piece * copies + copy][...].astype(jnp.float32)
            numer = term if numer is None else numer + term
            denom = prior if denom is None else denom + prior
        out_ref[at, :] = (numer / denom).astype(out_ref.dtype)
        first += size


def merge_rows(place, slots, sources, starts, grads, weights):
    copies, shards = len(grads), grads[0].shape[0]
    tok, width = grads[0].shape[1:]
    sizes = [piece.shape[0] for piece in weights[::copies]]
    rows = sum(sizes)
    return pl.pallas_call(
        functools.partial(merge_kernel, copies, shards, starts, sizes),
        out_shape=jax.ShapeDtypeStruct((rows, width), jnp.bfloat16),
        grid_spec=pltpu.PrefetchScalarGridSpec(
            num_scalar_prefetch=2,
            grid=(width // COL_TILE,),
            in_specs=[pl.BlockSpec(memory_space=pl.ANY)] * len(sources)
            + [pl.BlockSpec((shards, tok, COL_TILE), lambda j, *_: (0, 0, j))] * copies
            + [pl.BlockSpec((piece.shape[0], COL_TILE), lambda j, *_: (0, j)) for piece in weights],
            out_specs=pl.BlockSpec((rows, COL_TILE), lambda j, *_: (0, j)),
            scratch_shapes=[
                pltpu.VMEM((copies, shards, rows, tok), jnp.bfloat16),
                pltpu.SemaphoreType.DMA,
            ],
        ),
        compiler_params=pltpu.CompilerParams(vmem_limit_bytes=56 * 1024 * 1024),
        cost_estimate=pl.CostEstimate(
            flops=2 * copies * shards * tok * rows * width, bytes_accessed=2 * copies * shards * tok * width, transcendentals=0
        ),
    )(place, slots, *sources, *grads, *weights)


def place_kernel(count, where_ref, *refs):
    pieces, (out_ref, sems) = refs[:count], refs[-2:]
    moves = [
        pltpu.make_async_copy(
            piece,
            out_ref.at[pl.ds(pl.multiple_of(where_ref[n], 16), piece.shape[0]), :],
            sems.at[n],
        )
        for n, piece in enumerate(pieces)
    ]
    for move in moves:
        move.start()
    for move in moves:
        move.wait()


def place_rows(total, pieces, where, whole):
    count = len(pieces)
    shape = jax.ShapeDtypeStruct((total, pieces[0].shape[1]), pieces[0].dtype)
    more = [] if whole is None else [whole]
    return pl.pallas_call(
        functools.partial(place_kernel, count),
        out_shape=shape,
        grid_spec=pltpu.PrefetchScalarGridSpec(
            num_scalar_prefetch=1,
            grid=(1,),
            in_specs=[pl.BlockSpec(piece.shape, lambda *_: (0, 0)) for piece in pieces]
            + [pl.BlockSpec(memory_space=pl.ANY)] * len(more),
            out_specs=pl.BlockSpec(memory_space=pl.ANY),
            scratch_shapes=[pltpu.SemaphoreType.DMA((count,))],
        ),
        input_output_aliases={1 + count: 0} if more else {},
        compiler_params=pltpu.CompilerParams(vmem_limit_bytes=32 * 1024 * 1024),
        cost_estimate=pl.CostEstimate(
            flops=0, bytes_accessed=4 * sum(p.size for p in pieces), transcendentals=0
        ),
    )(jnp.stack(where).astype(jnp.int32), *pieces, *more)


def after(value, *others):
    return lax.optimization_barrier((value, *others))[0]


def per_device(activations, out_grads, seq_ids, weights):
    copies = lax.axis_size("mp")
    devices = lax.axis_size("fsdp")
    rows, width = weights.shape[1:]
    blocks = F // width
    spread = devices // blocks
    tok = activations.shape[1]
    share = rows // copies
    sizes = [share * n // sum(CHUNKS) for n in CHUNKS]
    starts = [sum(sizes[:k]) for k in range(len(sizes))]
    m = lax.axis_index("mp")
    i = lax.axis_index("fsdp")
    a, h = i // spread, i % spread
    chip, core = m // 2, m % 2

    def to_copy(value, flip):
        return lax.ppermute(value, "mp", [(s, s ^ flip) for s in range(copies)])

    def to_block(value, shift):
        pairs = [(s, (s // spread + shift) % blocks * spread + s % spread) for s in range(devices)]
        return lax.ppermute(value, "fsdp", pairs)

    def to_half(value, shift):
        pairs = [(s, s // spread * spread + (s % spread + shift) % spread) for s in range(devices)]
        return lax.ppermute(value, "fsdp", pairs)

    def along(value, step, direction):
        pairs = [
            (s, s + direction * spread)
            for s in range(devices)
            if 0 <= s // spread + direction < blocks and 0 <= s // spread - direction * (step - 1) < blocks
        ]
        return lax.ppermute(value, "fsdp", pairs)

    def spread_blocks(value):
        cut = [lax.dynamic_slice_in_dim(value, (a + k) % blocks * width, width, 1) for k in range(blocks)]
        return jnp.stack([cut[0]] + [to_block(cut[k], k) for k in range(1, blocks)])

    def over_halves(value):
        return jnp.concatenate([value] + [to_half(value, d) for d in range(1, spread)], axis=1)

    def weight_rows(owner, k):
        return lax.dynamic_slice_in_dim(weights[0], owner * share + starts[k], sizes[k], 0)

    def mate(value, *others):
        return to_copy(after(value, *others), 1)

    grad_far = to_copy(out_grads[0], 2)
    grad_near = spread_blocks(out_grads[0])
    acts = activations[0].T.reshape(spread, copies, share, tok).transpose(1, 0, 2, 3)
    named = jnp.broadcast_to(seq_ids[0].astype(acts.dtype), acts.shape[:2] + (FLAG_ROWS, tok))
    acts = jnp.concatenate([acts, named], axis=2).reshape(copies * spread, share + FLAG_ROWS, tok)
    planes = [
        [c * devices + block * spread + s for c in range(copies) for s in range(spread)] for block in range(blocks)
    ]
    own = lax.all_to_all(acts, ("mp", "fsdp"), 0, 0, axis_index_groups=planes, tiled=True)
    leaving = [jnp.stack([weight_rows((1 - chip) * 2 + c, k) for c in range(2)]) for k in range(len(sizes))]
    mate_rows = lax.dynamic_slice_in_dim(weights[0], (chip * 2 + 1 - core) * share, share, 0)

    weight_far = [None] * len(sizes)
    weight_mate = [None] * len(sizes)

    def send_weights(k, *others):
        weight_far[k] = to_copy(after(leaving[k], *others), 2)

    def cores(k, *others):
        weight_mate[k] = mate(lax.dynamic_index_in_dim(weight_far[k], 1 - core, 0, keepdims=False), *others)

    grads = [None] * copies
    stage = (own, grad_near, mate_rows, *leaving)
    low, high = [along(after(own, *stage), 1, 1)], [along(after(own, *stage), 1, -1)]
    send_weights(0, *stage, grad_far)
    grads[0] = over_halves(after(grad_near, *stage))

    stage = (low[0], high[0], grad_far, grads[0], weight_far[0])
    grad_far = spread_blocks(after(grad_far, *stage))
    send_weights(1, *stage)
    grads[1] = mate(grads[0], *stage)
    cores(0, *stage, grads[1])

    stage = (grad_far, grads[1], weight_far[1], weight_mate[0])
    low.append(along(after(low[0], *stage), 2, 1))
    high.append(along(after(high[0], *stage), 2, -1))
    send_weights(2, *stage)
    grads[2] = over_halves(after(grad_far, *stage))
    mate_rows = mate(mate_rows, *stage)
    cores(1, *stage, mate_rows)
    named = jnp.where(a == 0, high[0][:, share, 0], jnp.where(a == blocks - 1, low[0][:, share, 0], own[:, share, 0]))
    alone = jnp.where(named[::spread] > 0.5, 0, blocks - 1)[m ^ jnp.arange(copies)]
    slots = ((a - alone) % blocks).astype(jnp.int32)
    place = jnp.stack([a, m, h]).astype(jnp.int32)

    stage = (low[1], high[1], weight_far[2], grads[1], grads[2], weight_mate[1], slots)
    half = starts[2]
    grads[3] = mate(grads[2], *stage)
    low_last = [along(after(low[1], *stage)[:, :half], 3, 1)]
    high_last = [along(after(high[1], *stage)[:, :half], 3, -1)]
    low_last.append(along(after(low[1], *stage)[:, half:share], 3, 1))
    high_last.append(along(after(high[1], *stage)[:, half:share], 3, -1))
    cores(2, *stage, grads[3])
    send_weights(3, *stage)
    cores(3, low_last[0], high_last[0])

    whole = None
    for part in range(2):
        held = []
        for k in (2 * part, 2 * part + 1):
            mine = lax.dynamic_index_in_dim(weight_far[k], core, 0, keepdims=False)
            held += [weight_rows(m, k), mate_rows[starts[k]:starts[k] + sizes[k]], mine, weight_mate[k]]
        if part == 0:
            place = after(place, weight_far[3], weight_mate[2])
        sources = [own, low[0], low[1], low_last[part], high[0], high[1], high_last[part]]
        begin = [part * half] * len(sources)
        begin[3] = begin[6] = 0
        mine = merge_rows(place, slots, sources, begin, grads, held)
        if part == 0:
            place = after(place, mine)
        far = to_copy(mine, 2)
        last = far if whole is None else after(far, whole)
        pieces = [mine, to_copy(mine, 1), far, to_copy(last, 1)]
        where = [(m ^ flip) * share + part * half for flip in range(copies)]
        whole = place_rows(rows, pieces, where, whole)
    return whole


def solution(mesh):
    placed = (P("mp", "fsdp", None), P("mp", "fsdp", None), P("mp", "fsdp"), P("mp", "fsdp", None))
    return jax.shard_map(
        per_device, mesh=mesh, in_specs=placed, out_specs=P("fsdp", None), check_vma=False
    )
```

time: 887 us -> 405 us (0.46)
  Pallas kernels: 506 us -> 47.1 us
  waiting for transfers between devices: 266 us -> 235 us
  local copies, waits for them, and re-layouts: 54.8 us -> 67.3 us
    pallas_call x4 -> x2, Pallas kernels: 452 us -> 12 us  [place_rows(): pl.pallas_call(functools.partial(place_kernel, count), out_shape=shape, g...]
    ppermute x3 -> x2, waiting for transfers between devices: 88.9 us -> 61.6 us  [to_half(): return lax.ppermute(value, 'fsdp', pairs)]
    pallas_call x4 -> x2, Pallas kernels: 54 us -> 35.1 us  [merge_rows(): pl.pallas_call(functools.partial(merge_kernel, copies, shards, starts, si...]
    ppermute x26 -> x18, waiting for transfers between devices: 117 us -> 108 us  [to_copy(): return lax.ppermute(value, 'mp', [(s, s ^ flip) for s in range(copies)])]
  transfers between devices with their start and end apart: 43 -> 35, of which waited for: 14 -> 14; matrix products, arithmetic and copies ran while one was open for 7% -> 16% of each run, Pallas kernels for 48% -> 6%
where the time goes in v4:
time: 405 us; the launch traced here: 403 us
  waiting for transfers between devices  235 us (58%)
  local copies, waits for them, and re-layouts  67.3 us (17%)
  Pallas kernels  47.1 us (12%)
  starting transfers between devices  39.9 us (10%)
  other arithmetic  13.5 us (3%)
    ppermute x18, waiting for transfers between devices, to_copy(): return lax.ppermute(value, 'mp', [(s, s ^ flip) for s in range(copies)])  108 us
    ppermute x2, waiting for transfers between devices, to_half(): return lax.ppermute(value, 'fsdp', pairs)  61.6 us
    ppermute x6, waiting for transfers between devices, to_block(): return lax.ppermute(value, 'fsdp', pairs)  56.8 us
    pallas_call x2, Pallas kernels, merge_rows(): pl.pallas_call(functools.partial(merge_kernel, copies, shards, starts, si...  35.1 us
    ppermute x8, starting transfers between devices, along(): return lax.ppermute(value, 'fsdp', pairs)  12.9 us
    unnamed x30, local copies, waits for them, and re-layouts  12.6 us
    pallas_call x2, Pallas kernels, place_rows(): pl.pallas_call(functools.partial(place_kernel, count), out_shape=shape, g...  12 us
    dynamic_slice x3, local copies, waits for them, and re-layouts, weight_rows(): lax.dynamic_slice_in_dim(weights[0], owner * share + starts[k], sizes[k], 0)  9.88 us
  transfers between devices with their start and end apart: 35, of which 14 were waited for; matrix products, arithmetic and copies ran while one was open for 16% of the time, Pallas kernels for 6%

profile of v4, /device:TPU:0, one launch (start us, length us, event | category | flops | bytes accessed | tf_op | source)
XLA Modules:
  0.0 403.0 jit_solution(2804102803061979085)
XLA Ops:
  0.7 4.5 %reshape.53 = bf16[2,4,1024,128]{2,1,0,3:T(4,128)(2,1)} reshape(bf16[8192,128]{0,1:T(8,128)(2,1)} %bitcast.65) | data formatting | bytes 4194304 | tf_op jit(solution)/shard_map/reshape | solution.py:198
  10.1 5.2 %all-to-all-start = ((bf16[8,1040,128]{2,1,0:T(8,128)(2,1)}), bf16[8,1040,128]{2,1,0:T(8,128)(2,1)S(1)}, u32[]{:S(2)}, u32[]{:S(2)}) async-start(bf16[8,1040,128]{2,1,0:T(8,128)(2,1)} %bitcast.63), calls=%async_computation | async-start | bytes 4259840 | tf_op jit(solution)/shard_map/all_to_all | solution.py:204
  17.8 3.6 collective-permute-start.2
  30.9 4.8 %dynamic-slice_bitcast_fusion.2 = (bf16[320,1792]{1,0:T(8,128)(2,1)}, bf16[320,1792]{1,0:T(8,128)(2,1)}, bf16[1,320,1792]{2,1,0:T(8,128)(2,1)S(1)}, bf16[1,320,1...) fusion(bf16[1,4096,1792]{2,1,0:T(8,128)(2,1)} %param.7, ...), kind=kLoop, calls=%fused_computation.9 | loop fusion | bytes 13762584 | tf_op jit(solution)/shard_map/dynamic_slice | solution.py:191
  35.7 4.2 %dynamic-slice_bitcast_fusion = bf16[1024,1792]{1,0:T(8,128)(2,1)} fusion(bf16[1,4096,1792]{2,1,0:T(8,128)(2,1)} %param.7, s32[]{:T(128)S(6)} %select_n.164), kind=kLoop, calls=%fused_computation.1 | loop fusion | bytes 7340036 | tf_op jit(solution)/shard_map/dynamic_slice | solution.py:206
  43.4 18.2 %collective-permute-done.1 = bf16[128,1792]{1,0:T(8,128)(2,1)} collective-permute-done((bf16[128,1792]{1,0:T(8,128)(2,1)}, bf16[128,1792]{1,0:T(8,128)(2,1)}, u32[]{:S(2)}, u32[]{:S(2)}) %collective-permute-start.1) | collective-permute-done | bytes 458784 | tf_op jit(solution)/shard_map/ppermute | solution.py:169
  64.4 4.1 %collective-permute-start.3 = (bf16[8,1040,128]{2,1,0:T(8,128)(2,1)S(1)}, bf16[8,1040,128]{2,1,0:T(8,128)(2,1)}, u32[]{:S(2)}, u32[]{:S(2)}) collective-permute-start(bf16[8,1040,128]{2,1,0:T(8,128)(2,1)S(1)} %all-to-all-done.refs_0_), channel_id=1, source_target_pairs={{0,2},{1,3},{2,4},{3,5},{4,6},{5,7},{8,10},{9,11},{10,12},{11,13},... | collective-permute-start | bytes 6389768 | tf_op jit(solution)/shard_map/ppermute | solution.py:181
  71.5 9.3 %collective-permute-done.4 = bf16[128,7168]{1,0:T(8,128)(2,1)} collective-permute-done((bf16[128,7168]{1,0:T(8,128)(2,1)}, bf16[128,7168]{1,0:T(8,128)(2,1)}, u32[]{:S(2)}, u32[]{:S(2)}) %collective-permute-start.4) | collective-permute-done | bytes 1835040 | tf_op jit(solution)/shard_map/ppermute | solution.py:165
  84.0 27.1 %collective-permute-done.6 = bf16[4,128,1792]{2,1,0:T(8,128)(2,1)S(1)} collective-permute-done((bf16[4,128,1792]{2,1,0:T(8,128)(2,1)}, bf16[4,128,1792]{2,1,0:T(8,128)(2,1)S(1)}, u32[]{:S(2)}, u32[]{:S(2)}) %collective-permute-start.6) | collective-permute-done | bytes 1835040 | tf_op jit(solution)/shard_map/ppermute | solution.py:173
  112.4 10.1 %collective-permute-done.7 = bf16[2,256,1792]{2,1,0:T(8,128)(2,1)S(1)} collective-permute-done((bf16[2,256,1792]{2,1,0:T(8,128)(2,1)}, bf16[2,256,1792]{2,1,0:T(8,128)(2,1)S(1)}, u32[]{:S(2)}, u32[]{:S(2)}) %collective-permute-start.7) | collective-permute-done | bytes 1835040 | tf_op jit(solution)/shard_map/ppermute | solution.py:165
  127.0 3.6 collective-permute-done.11.refs_8_
  132.3 3.7 collective-permute-start.10
  136.9 9.9 %collective-permute-done.10 = bf16[128,1792]{1,0:T(8,128)(2,1)S(1)} collective-permute-done((bf16[128,1792]{1,0:T(8,128)(2,1)S(1)}, bf16[128,1792]{1,0:T(8,128)(2,1)S(1)}, u32[]{:S(2)}, u32[]{:S(2)}) %collective-permute-start.10) | collective-permute-done | bytes 458784 | tf_op jit(solution)/shard_map/ppermute | solution.py:169
  146.9 28.7 %collective-permute-done.9 = bf16[128,1792]{1,0:T(8,128)(2,1)S(1)} collective-permute-done((bf16[128,1792]{1,0:T(8,128)(2,1)S(1)}, bf16[128,1792]{1,0:T(8,128)(2,1)S(1)}, u32[]{:S(2)}, u32[]{:S(2)}) %collective-permute-start.9) | collective-permute-done | bytes 458784 | tf_op jit(solution)/shard_map/ppermute | solution.py:169
  190.3 34.5 %collective-permute-done.17 = bf16[4,128,1792]{2,1,0:T(8,128)(2,1)} collective-permute-done((bf16[4,128,1792]{2,1,0:T(8,128)(2,1)}, bf16[4,128,1792]{2,1,0:T(8,128)(2,1)}, u32[]{:S(2)}, u32[]{:S(2)}) %collective-permute-start.17) | collective-permute-done | bytes 1835040 | tf_op jit(solution)/shard_map/ppermute | solution.py:173
  226.4 7.8 %collective-permute-done.15.refs_5_ = bf16[8,1040,128]{2,1,0:T(8,128)(2,1)} collective-permute-done((bf16[8,1040,128]{2,1,0:T(8,128)(2,1)}, bf16[8,1040,128]{2,1,0:T(8,128)(2,1)}, u32[]{:S(2)}, u32[]{:S(2)}) %collective-permute-start.15) | collective-permute-done | bytes 2129952 | tf_op jit(solution)/shard_map/ppermute | solution.py:181
  254.0 15.0 %collective-permute-done.20 = bf16[2,128,1792]{2,1,0:T(8,128)(2,1)} collective-permute-done((bf16[2,128,1792]{2,1,0:T(8,128)(2,1)S(1)}, bf16[2,128,1792]{2,1,0:T(8,128)(2,1)}, u32[]{:S(2)}, u32[]{:S(2)}) %collective-permute-start.20) | collective-permute-done | bytes 917536 | tf_op jit(solution)/shard_map/ppermute | solution.py:165
  271.3 18.7 %shard_map.46.refs_0_ = bf16[576,1792]{1,0:T(8,128)(2,1)} custom-call(s32[3]{0:T(128)} %pad_add_fusion.1.place_ref, s32[4]{0:T(128)} %and_select_fusion.slot_ref, bf16[8,1040,128]{2,1,0:T(8,128)(2,1)} %copy-done.3, bf16[8,1040,128]{2,1,0:T(8,128)(2,1)} %collective-permute-done.3.refs_1_, bf16[8,1040,128]{2,1,0:T(8,128)(2,1)} %collective-permute-done.14.refs_2_, ...), custom_call_target="tpu_custom_call" | custom-call | flops 8455716864 | bytes 14680064 | tf_op jit(solution)/shard_map/pallas_call | solution.py:84
  300.5 36.5 %collective-permute-done.31.refs_2_ = bf16[576,1792]{1,0:T(8,128)(2,1)} collective-permute-done((bf16[576,1792]{1,0:T(8,128)(2,1)}, bf16[576,1792]{1,0:T(8,128)(2,1)}, u32[]{:S(2)}, u32[]{:S(2)}) %collective-permute-start.31) | collective-permute-done | bytes 2064416 | tf_op jit(solution)/shard_map/ppermute | solution.py:165
  338.4 16.4 %shard_map.47.refs_0_ = bf16[448,1792]{1,0:T(8,128)(2,1)} custom-call(s32[3]{0:T(128)} %pad_add_fusion.1.place_ref, s32[4]{0:T(128)} %and_select_fusion.slot_ref, bf16[8,1040,128]{2,1,0:T(8,128)(2,1)} %copy-done.3, bf16[8,1040,128]{2,1,0:T(8,128)(2,1)} %collective-permute-done.3.refs_1_, bf16[8,1040,128]{2,1,0:T(8,128)(2,1)} %collective-permute-done.14.refs_2_, ...), custom_call_target="tpu_custom_call" | custom-call | flops 6576668672 | bytes 14680064 | tf_op jit(solution)/shard_map/pallas_call | solution.py:84
  356.6 6.7 %shard_map.48.refs_4_ = bf16[4096,1792]{1,0:T(8,128)(2,1)} custom-call(s32[4]{0:T(128)S(1)} %pad_add_fusion.2.where_ref, bf16[576,1792]{1,0:T(8,128)(2,1)S(1)} %copy-done, bf16[576,1792]{1,0:T(8,128)(2,1)} %collective-permute-done.30.refs_1_, bf16[576,1792]{1,0:T(8,128)(2,1)} %collective-permute-done.31.refs_2_, ...), custom_call_target="tpu_custom_call" | custom-call | bytes 16515072 | tf_op jit(solution)/shard_map/pallas_call | solution.py:126
  363.4 29.4 %collective-permute-done.29.refs_2_ = bf16[448,1792]{1,0:T(8,128)(2,1)} collective-permute-done((bf16[448,1792]{1,0:T(8,128)(2,1)}, bf16[448,1792]{1,0:T(8,128)(2,1)}, u32[]{:S(2)}, u32[]{:S(2)}) %collective-permute-start.29) | collective-permute-done | bytes 1605664 | tf_op jit(solution)/shard_map/ppermute | solution.py:165
  392.8 3.6 collective-permute-done.33.refs_3_
  397.8 5.2 %shard_map.49 = bf16[4096,1792]{1,0:T(8,128)(2,1)} custom-call(s32[4]{0:T(128)S(1)} %pad_add_fusion.where_ref, bf16[448,1792]{1,0:T(8,128)(2,1)S(1)} %copy-done.1, bf16[448,1792]{1,0:T(8,128)(2,1)} %collective-permute-done.28.refs_1_, bf16[448,1792]{1,0:T(8,128)(2,1)} %collective-permute-done.29.refs_2_, ...), custom_call_target="tpu_custom_call", output_to_operand_aliasing={{}: (5, {})} | custom-call | bytes 12845056 | tf_op jit(solution)/shard_map/pallas_call | solution.py:126
  (119 shorter events, 91.9 us)
Async XLA Ops:
  10.1 54.3 %all-to-all-start = ((bf16[8,1040,128]{2,1,0:T(8,128)(2,1)}), bf16[8,1040,128]{2,1,0:T(8,128)(2,1)S(1)}, u32[]{:S(2)}, u32[]{:S(2)}) async-start(bf16[8,1040,128]{2,1,0:T(8,128)(2,1)} %bitcast.63), calls=%async_computation | async-start | bytes 4259840 | tf_op jit(solution)/shard_map/all_to_all | solution.py:204
  21.4 40.1 %collective-permute-start.1 = (bf16[128,1792]{1,0:T(8,128)(2,1)}, bf16[128,1792]{1,0:T(8,128)(2,1)}, u32[]{:S(2)}, u32[]{:S(2)}) collective-permute-start(bf16[128,1792]{1,0:T(8,128)(2,1)} %get-tuple-element.74), channel_id=1, source_target_pairs={{0,4},{1,5},{2,6},{3,7},{4,0},{5,1},{6,2},{7,3},{8,12},{9,13},{10,... | collective-permute-start | bytes 1376264 | tf_op jit(solution)/shard_map/ppermute | solution.py:169
  21.4 40.1 %collective-permute-start = (bf16[128,1792]{1,0:T(8,128)(2,1)}, bf16[128,1792]{1,0:T(8,128)(2,1)}, u32[]{:S(2)}, u32[]{:S(2)}) collective-permute-start(bf16[128,1792]{1,0:T(8,128)(2,1)} %get-tuple-element.75), channel_id=1, source_target_pairs={{0,2},{1,3},{2,4},{3,5},{4,6},{5,7},{6,0},{7,1},{8,10},{9,11},{10,... | collective-permute-start | bytes 1376264 | tf_op jit(solution)/shard_map/ppermute | solution.py:169
  22.4 58.4 %collective-permute-start.4 = (bf16[128,7168]{1,0:T(8,128)(2,1)}, bf16[128,7168]{1,0:T(8,128)(2,1)}, u32[]{:S(2)}, u32[]{:S(2)}) collective-permute-start(bf16[128,7168]{1,0:T(8,128)(2,1)} %bitcast.19), channel_id=1, source_target_pairs={{0,16},{8,24},{16,0},{24,8},{1,17},{9,25},{17,1},{25,9},{2,18},{10... | collective-permute-start | bytes 5505032 | tf_op jit(solution)/shard_map/ppermute | solution.py:165
  64.4 58.2 %collective-permute-start.3 = (bf16[8,1040,128]{2,1,0:T(8,128)(2,1)S(1)}, bf16[8,1040,128]{2,1,0:T(8,128)(2,1)}, u32[]{:S(2)}, u32[]{:S(2)}) collective-permute-start(bf16[8,1040,128]{2,1,0:T(8,128)(2,1)S(1)} %all-to-all-done.refs_0_), channel_id=1, source_target_pairs={{0,2},{1,3},{2,4},{3,5},{4,6},{5,7},{8,10},{9,11},{10,12},{11,13},... | collective-permute-start | bytes 6389768 | tf_op jit(solution)/shard_map/ppermute | solution.py:181
  68.5 54.1 %collective-permute-start.5 = (bf16[8,1040,128]{2,1,0:T(8,128)(2,1)S(1)}, bf16[8,1040,128]{2,1,0:T(8,128)(2,1)}, u32[]{:S(2)}, u32[]{:S(2)}) collective-permute-start(bf16[8,1040,128]{2,1,0:T(8,128)(2,1)S(1)} %all-to-all-done.refs_0_), channel_id=1, source_target_pairs={{2,0},{3,1},{4,2},{5,3},{6,4},{7,5},{10,8},{11,9},{12,10},{13,11},... | collective-permute-start | bytes 6389768 | tf_op jit(solution)/shard_map/ppermute | solution.py:181
  69.8 41.3 %collective-permute-start.6 = (bf16[4,128,1792]{2,1,0:T(8,128)(2,1)}, bf16[4,128,1792]{2,1,0:T(8,128)(2,1)S(1)}, u32[]{:S(2)}, u32[]{:S(2)}) collective-permute-start(bf16[4,128,1792]{2,1,0:T(8,128)(2,1)} %pad_maximum_fusion.3), channel_id=1, source_target_pairs={{0,1},{1,0},{2,3},{3,2},{4,5},{5,4},{6,7},{7,6},{8,9},{9,8},{10,11... | collective-permute-start | bytes 5505032 | tf_op jit(solution)/shard_map/ppermute | solution.py:173
  80.8 41.8 %collective-permute-start.7 = (bf16[2,256,1792]{2,1,0:T(8,128)(2,1)}, bf16[2,256,1792]{2,1,0:T(8,128)(2,1)S(1)}, u32[]{:S(2)}, u32[]{:S(2)}) collective-permute-start(bf16[2,256,1792]{2,1,0:T(8,128)(2,1)} %pad_maximum_fusion.4), channel_id=1, source_target_pairs={{0,16},{8,24},{16,0},{24,8},{1,17},{9,25},{17,1},{25,9},{2,18},{10... | collective-permute-start | bytes 5505032 | tf_op jit(solution)/shard_map/ppermute | solution.py:165
  123.8 53.3 %collective-permute-start.12 = (bf16[2,320,1792]{2,1,0:T(8,128)(2,1)}, bf16[2,320,1792]{2,1,0:T(8,128)(2,1)}, u32[]{:S(2)}, u32[]{:S(2)}) collective-permute-start(bf16[2,320,1792]{2,1,0:T(8,128)(2,1)} %get-tuple-element.32), channel_id=1, source_target_pairs={{0,16},{8,24},{16,0},{24,8},{1,17},{9,25},{17,1},{25,9},{2,18},{10... | collective-permute-start | bytes 6881288 | tf_op jit(solution)/shard_map/ppermute | solution.py:165
  130.6 46.5 %collective-permute-start.13 = (bf16[256,1792]{1,0:T(8,128)(2,1)S(1)}, bf16[256,1792]{1,0:T(8,128)(2,1)S(1)}, u32[]{:S(2)}, u32[]{:S(2)}) collective-permute-start(bf16[256,1792]{1,0:T(8,128)(2,1)S(1)} %get-tuple-element.33), channel_id=1, source_target_pairs={{0,8},{8,0},{16,24},{24,16},{1,9},{9,1},{17,25},{25,17},{2,10},{10... | collective-permute-start | bytes 2752520 | tf_op jit(solution)/shard_map/ppermute | solution.py:165
  135.9 39.7 %collective-permute-start.9 = (bf16[128,1792]{1,0:T(8,128)(2,1)S(1)}, bf16[128,1792]{1,0:T(8,128)(2,1)S(1)}, u32[]{:S(2)}, u32[]{:S(2)}) collective-permute-start(bf16[128,1792]{1,0:T(8,128)(2,1)S(1)} %get-tuple-element.71), channel_id=1, source_target_pairs={{0,4},{1,5},{2,6},{3,7},{4,0},{5,1},{6,2},{7,3},{8,12},{9,13},{10,... | collective-permute-start | bytes 1376264 | tf_op jit(solution)/shard_map/ppermute | solution.py:169
  135.9 39.7 %collective-permute-start.8 = (bf16[128,1792]{1,0:T(8,128)(2,1)S(1)}, bf16[128,1792]{1,0:T(8,128)(2,1)S(1)}, u32[]{:S(2)}, u32[]{:S(2)}) collective-permute-start(bf16[128,1792]{1,0:T(8,128)(2,1)S(1)} %get-tuple-element.72), channel_id=1, source_target_pairs={{0,2},{1,3},{2,4},{3,5},{4,6},{5,7},{6,0},{7,1},{8,10},{9,11},{10,... | collective-permute-start | bytes 1376264 | tf_op jit(solution)/shard_map/ppermute | solution.py:169
  178.3 55.9 %collective-permute-start.16 = (bf16[2,320,1792]{2,1,0:T(8,128)(2,1)}, bf16[2,320,1792]{2,1,0:T(8,128)(2,1)}, u32[]{:S(2)}, u32[]{:S(2)}) collective-permute-start(bf16[2,320,1792]{2,1,0:T(8,128)(2,1)} %get-tuple-element.36), channel_id=1, source_target_pairs={{0,16},{8,24},{16,0},{24,8},{1,17},{9,25},{17,1},{25,9},{2,18},{10... | collective-permute-start | bytes 6881288 | tf_op jit(solution)/shard_map/ppermute | solution.py:165
  179.0 47.4 %collective-permute-start.14 = (bf16[8,1040,128]{2,1,0:T(8,128)(2,1)}, bf16[8,1040,128]{2,1,0:T(8,128)(2,1)}, u32[]{:S(2)}, u32[]{:S(2)}) collective-permute-start(bf16[8,1040,128]{2,1,0:T(8,128)(2,1)} %collective-permute-done.3.refs_1_), channel_id=1, source_target_pairs={{2,4},{3,5},{4,6},{5,7},{10,12},{11,13},{12,14},{13,15},{18,20},{1... | collective-permute-start | bytes 6389768 | tf_op jit(solution)/shard_map/ppermute | solution.py:181
  181.0 53.3 %collective-permute-start.15 = (bf16[8,1040,128]{2,1,0:T(8,128)(2,1)}, bf16[8,1040,128]{2,1,0:T(8,128)(2,1)}, u32[]{:S(2)}, u32[]{:S(2)}) collective-permute-start(bf16[8,1040,128]{2,1,0:T(8,128)(2,1)} %collective-permute-done.5.refs_4_), channel_id=1, source_target_pairs={{2,0},{3,1},{4,2},{5,3},{10,8},{11,9},{12,10},{13,11},{18,16},{19,... | collective-permute-start | bytes 6389768 | tf_op jit(solution)/shard_map/ppermute | solution.py:181
  182.2 42.5 %collective-permute-start.17 = (bf16[4,128,1792]{2,1,0:T(8,128)(2,1)}, bf16[4,128,1792]{2,1,0:T(8,128)(2,1)}, u32[]{:S(2)}, u32[]{:S(2)}) collective-permute-start(bf16[4,128,1792]{2,1,0:T(8,128)(2,1)} %pad_maximum_fusion.5), channel_id=1, source_target_pairs={{0,1},{1,0},{2,3},{3,2},{4,5},{5,4},{6,7},{7,6},{8,9},{9,8},{10,11... | collective-permute-start | bytes 5505032 | tf_op jit(solution)/shard_map/ppermute | solution.py:173
  186.4 47.8 %collective-permute-start.19 = (bf16[320,1792]{1,0:T(8,128)(2,1)S(1)}, bf16[320,1792]{1,0:T(8,128)(2,1)}, u32[]{:S(2)}, u32[]{:S(2)}) collective-permute-start(bf16[320,1792]{1,0:T(8,128)(2,1)S(1)} %get-tuple-element.39), channel_id=1, source_target_pairs={{0,8},{8,0},{16,24},{24,16},{1,9},{9,1},{17,25},{25,17},{2,10},{10... | collective-permute-start | bytes 3440648 | tf_op jit(solution)/shard_map/ppermute | solution.py:165
  290.0 46.9 %collective-permute-start.31 = (bf16[576,1792]{1,0:T(8,128)(2,1)}, bf16[576,1792]{1,0:T(8,128)(2,1)}, u32[]{:S(2)}, u32[]{:S(2)}) collective-permute-start(bf16[576,1792]{1,0:T(8,128)(2,1)} %shard_map.46.refs_0_), channel_id=1, source_target_pairs={{0,16},{8,24},{16,0},{24,8},{1,17},{9,25},{17,1},{25,9},{2,18},{10... | collective-permute-start | bytes 6193160 | tf_op jit(solution)/shard_map/ppermute | solution.py:165
  294.0 43.0 %collective-permute-start.25 = (bf16[8,448,128]{2,1,0:T(8,128)(2,1)S(1)}, bf16[8,448,128]{2,1,0:T(8,128)(2,1)S(1)}, u32[]{:S(2)}, u32[]{:S(2)}) collective-permute-start(bf16[8,448,128]{2,1,0:T(8,128)(2,1)S(1)} %slice.44), channel_id=1, source_target_pairs={{4,6},{5,7},{12,14},{13,15},{20,22},{21,23},{28,30},{29,31}} | collective-permute-start | bytes 2752520 | tf_op jit(solution)/shard_map/ppermute | solution.py:181
  294.8 42.1 %collective-permute-start.26 = (bf16[8,448,128]{2,1,0:T(8,128)(2,1)S(1)}, bf16[8,448,128]{2,1,0:T(8,128)(2,1)S(1)}, u32[]{:S(2)}, u32[]{:S(2)}) collective-permute-start(bf16[8,448,128]{2,1,0:T(8,128)(2,1)S(1)} %slice.45), channel_id=1, source_target_pairs={{2,0},{3,1},{10,8},{11,9},{18,16},{19,17},{26,24},{27,25}} | collective-permute-start | bytes 2752520 | tf_op jit(solution)/shard_map/ppermute | solution.py:181
  298.1 38.8 %collective-permute-start.27 = (bf16[128,1792]{1,0:T(8,128)(2,1)S(1)}, bf16[128,1792]{1,0:T(8,128)(2,1)S(1)}, u32[]{:S(2)}, u32[]{:S(2)}) collective-permute-start(bf16[128,1792]{1,0:T(8,128)(2,1)S(1)} %get-tuple-element.47), channel_id=1, source_target_pairs={{0,8},{8,0},{16,24},{24,16},{1,9},{9,1},{17,25},{25,17},{2,10},{10... | collective-permute-start | bytes 1376264 | tf_op jit(solution)/shard_map/ppermute | solution.py:165
  300.0 56.6 %collective-permute-start.30 = (bf16[576,1792]{1,0:T(8,128)(2,1)S(1)}, bf16[576,1792]{1,0:T(8,128)(2,1)}, u32[]{:S(2)}, u32[]{:S(2)}) collective-permute-start(bf16[576,1792]{1,0:T(8,128)(2,1)S(1)} %copy-done), channel_id=1, source_target_pairs={{0,8},{8,0},{16,24},{24,16},{1,9},{9,1},{17,25},{25,17},{2,10},{10... | collective-permute-start | bytes 6193160 | tf_op jit(solution)/shard_map/ppermute | solution.py:165
  354.8 37.9 %collective-permute-start.29 = (bf16[448,1792]{1,0:T(8,128)(2,1)}, bf16[448,1792]{1,0:T(8,128)(2,1)}, u32[]{:S(2)}, u32[]{:S(2)}) collective-permute-start(bf16[448,1792]{1,0:T(8,128)(2,1)} %shard_map.47.refs_0_), channel_id=1, source_target_pairs={{0,16},{8,24},{16,0},{24,8},{1,17},{9,25},{17,1},{25,9},{2,18},{10... | collective-permute-start | bytes 4816904 | tf_op jit(solution)/shard_map/ppermute | solution.py:165
  356.4 36.4 %collective-permute-start.28 = (bf16[448,1792]{1,0:T(8,128)(2,1)}, bf16[448,1792]{1,0:T(8,128)(2,1)}, u32[]{:S(2)}, u32[]{:S(2)}) collective-permute-start(bf16[448,1792]{1,0:T(8,128)(2,1)} %shard_map.47.refs_0_), channel_id=1, source_target_pairs={{0,8},{8,0},{16,24},{24,16},{1,9},{9,1},{17,25},{25,17},{2,10},{10... | collective-permute-start | bytes 4816904 | tf_op jit(solution)/shard_map/ppermute | solution.py:165
  (25 other events, 363.6 us)

commit v5 on v4

--- a/solution.py
+++ b/solution.py
@@ -180,8 +180,10 @@
         ]
         return lax.ppermute(value, "fsdp", pairs)
 
-    def spread_blocks(value):
-        cut = [lax.dynamic_slice_in_dim(value, (a + k) % blocks * width, width, 1) for k in range(blocks)]
+    def cut_blocks(value):
+        return [lax.dynamic_slice_in_dim(value, (a + k) % blocks * width, width, 1) for k in range(blocks)]
+
+    def spread_blocks(cut):
         return jnp.stack([cut[0]] + [to_block(cut[k], k) for k in range(1, blocks)])
 
     def over_halves(value):
@@ -194,8 +196,9 @@
         return to_copy(after(value, *others), 1)
 
     grad_far = to_copy(out_grads[0], 2)
-    grad_near = spread_blocks(out_grads[0])
-    acts = activations[0].T.reshape(spread, copies, share, tok).transpose(1, 0, 2, 3)
+    cut = cut_blocks(out_grads[0])
+    grad_near = spread_blocks(cut)
+    acts = after(activations[0], *cut).T.reshape(spread, copies, share, tok).transpose(1, 0, 2, 3)
     named = jnp.broadcast_to(seq_ids[0].astype(acts.dtype), acts.shape[:2] + (FLAG_ROWS, tok))
     acts = jnp.concatenate([acts, named], axis=2).reshape(copies * spread, share + FLAG_ROWS, tok)
     planes = [
@@ -204,6 +207,7 @@
     own = lax.all_to_all(acts, ("mp", "fsdp"), 0, 0, axis_index_groups=planes, tiled=True)
     leaving = [jnp.stack([weight_rows((1 - chip) * 2 + c, k) for c in range(2)]) for k in range(len(sizes))]
     mate_rows = lax.dynamic_slice_in_dim(weights[0], (chip * 2 + 1 - core) * share, share, 0)
+    mate_rows = mate(mate_rows, *cut)
 
     weight_far = [None] * len(sizes)
     weight_mate = [None] * len(sizes)
@@ -216,23 +220,26 @@
 
     grads = [None] * copies
     stage = (own, grad_near, mate_rows, *leaving)
+    early = stage
     low, high = [along(after(own, *stage), 1, 1)], [along(after(own, *stage), 1, -1)]
-    send_weights(0, *stage, grad_far)
+    send_weights(0, *stage)
     grads[0] = over_halves(after(grad_near, *stage))
 
-    stage = (low[0], high[0], grad_far, grads[0], weight_far[0])
-    grad_far = spread_blocks(after(grad_far, *stage))
-    send_weights(1, *stage)
+    send_weights(1, *early)
+    cut = cut_blocks(grad_far)
+    stage = (low[0], high[0], grads[0], weight_far[0], *cut)
+    early = stage
+    grad_far = spread_blocks([after(block, *stage) for block in cut])
     grads[1] = mate(grads[0], *stage)
-    cores(0, *stage, grads[1])
-
-    stage = (grad_far, grads[1], weight_far[1], weight_mate[0])
+
+    stage = (grad_far, grads[1], weight_far[1])
     low.append(along(after(low[0], *stage), 2, 1))
     high.append(along(after(high[0], *stage), 2, -1))
-    send_weights(2, *stage)
+    send_weights(2, *early)
+    early = stage
     grads[2] = over_halves(after(grad_far, *stage))
-    mate_rows = mate(mate_rows, *stage)
-    cores(1, *stage, mate_rows)
+    cores(0, *stage)
+    cores(1, weight_mate[0])
     named = jnp.where(a == 0, high[0][:, share, 0], jnp.where(a == blocks - 1, low[0][:, share, 0], own[:, share, 0]))
     alone = jnp.where(named[::spread] > 0.5, 0, blocks - 1)[m ^ jnp.arange(copies)]
     slots = ((a - alone) % blocks).astype(jnp.int32)
@@ -246,26 +253,28 @@
     low_last.append(along(after(low[1], *stage)[:, half:share], 3, 1))
     high_last.append(along(after(high[1], *stage)[:, half:share], 3, -1))
     cores(2, *stage, grads[3])
-    send_weights(3, *stage)
+    send_weights(3, *early)
     cores(3, low_last[0], high_last[0])
 
-    whole = None
+    merged = []
     for part in range(2):
         held = []
         for k in (2 * part, 2 * part + 1):
             mine = lax.dynamic_index_in_dim(weight_far[k], core, 0, keepdims=False)
             held += [weight_rows(m, k), mate_rows[starts[k]:starts[k] + sizes[k]], mine, weight_mate[k]]
-        if part == 0:
-            place = after(place, weight_far[3], weight_mate[2])
         sources = [own, low[0], low[1], low_last[part], high[0], high[1], high_last[part]]
         begin = [part * half] * len(sources)
         begin[3] = begin[6] = 0
-        mine = merge_rows(place, slots, sources, begin, grads, held)
-        if part == 0:
-            place = after(place, mine)
-        far = to_copy(mine, 2)
-        last = far if whole is None else after(far, whole)
-        pieces = [mine, to_copy(mine, 1), far, to_copy(last, 1)]
+        merged.append(merge_rows(place, slots, sources, begin, grads, held))
+        place = after(place, merged[-1])
+    far = [to_copy(mine, 2) for mine in merged]
+    near = after(merged[0], merged[1])
+    came = after(far[0], merged[1])
+    whole = None
+    for part in range(2):
+        if part == 1:
+            near, came = merged[1], after(far[1], whole)
+        pieces = [merged[part], to_copy(near, 1), far[part], to_copy(came, 1)]
         where = [(m ^ flip) * share + part * half for flip in range(copies)]
         whole = place_rows(rows, pieces, where, whole)
     return whole

time: 405 us -> 389 us (0.960)
  waiting for transfers between devices: 235 us -> 215 us
  starting transfers between devices: 39.9 us -> 44.1 us
  local copies, waits for them, and re-layouts: 67.3 us -> 63.1 us
    ppermute x8, waiting for transfers between devices: 9.07 us -> 42 us  [along(): return lax.ppermute(value, 'fsdp', pairs)]
    ppermute x6, waiting for transfers between devices: 56.8 us -> 26.9 us  [to_block(): return lax.ppermute(value, 'fsdp', pairs)]
    ppermute x2, waiting for transfers between devices: 61.6 us -> 41.1 us  [to_half(): return lax.ppermute(value, 'fsdp', pairs)]
    ppermute x18, waiting for transfers between devices: 108 us -> 99.3 us  [to_copy(): return lax.ppermute(value, 'mp', [(s, s ^ flip) for s in range(copies)])]
    all_to_all x1, waiting for transfers between devices: 0.01 us -> 5.92 us  [per_device(): lax.all_to_all(acts, ('mp', 'fsdp'), 0, 0, axis_index_groups=planes, tile...]
    ppermute x8, starting transfers between devices: 12.9 us -> 17.2 us  [along(): return lax.ppermute(value, 'fsdp', pairs)]
    squeeze x3 -> x2, local copies, waits for them, and re-layouts: 8.44 us -> 5.33 us  [per_device(): mine = lax.dynamic_index_in_dim(weight_far[k], core, 0, keepdims=False)]
    unnamed x30 -> x32, local copies, waits for them, and re-layouts: 12.6 us -> 10.7 us
  transfers between devices with their start and end apart: 35 -> 35, of which waited for: 14 -> 16; matrix products, arithmetic and copies ran while one was open for 16% -> 17% of each run, Pallas kernels for 6% -> 11%
where the time goes in v5:
time: 389 us; the launch traced here: 385 us
  waiting for transfers between devices  215 us (55%)
  local copies, waits for them, and re-layouts  63.1 us (16%)
  Pallas kernels  47.2 us (12%)
  starting transfers between devices  44.1 us (11%)
  other arithmetic  15 us (4%)
    ppermute x18, waiting for transfers between devices, to_copy(): return lax.ppermute(value, 'mp', [(s, s ^ flip) for s in range(copies)])  99.3 us
    ppermute x8, waiting for transfers between devices, along(): return lax.ppermute(value, 'fsdp', pairs)  42 us
    ppermute x2, waiting for transfers between devices, to_half(): return lax.ppermute(value, 'fsdp', pairs)  41.1 us
    pallas_call x2, Pallas kernels, merge_rows(): pl.pallas_call(functools.partial(merge_kernel, copies, shards, starts, si...  35.3 us
    ppermute x6, waiting for transfers between devices, to_block(): return lax.ppermute(value, 'fsdp', pairs)  26.9 us
    ppermute x8, starting transfers between devices, along(): return lax.ppermute(value, 'fsdp', pairs)  17.2 us
    pallas_call x2, Pallas kernels, place_rows(): pl.pallas_call(functools.partial(place_kernel, count), out_shape=shape, g...  12 us
    unnamed x32, local copies, waits for them, and re-layouts  10.7 us
  transfers between devices with their start and end apart: 35, of which 16 were waited for; matrix products, arithmetic and copies ran while one was open for 17% of the time, Pallas kernels for 11%

profile of v5, /device:TPU:0, one launch (start us, length us, event | category | flops | bytes accessed | tf_op | source)
XLA Modules:
  0.0 384.8 jit_solution(13383285046927934334)
XLA Ops:
  0.0 4.1 %dynamic-slice_bitcast_fusion = bf16[1024,1792]{1,0:T(8,128)(2,1)} fusion(bf16[1,4096,1792]{2,1,0:T(8,128)(2,1)} %param.7, s32[]{:T(128)S(6)} %select_n.163), kind=kLoop, calls=%fused_computation.1 | loop fusion | bytes 7340036 | tf_op jit(solution)/shard_map/dynamic_slice | solution.py:209
  16.3 3.5 copy.7
  21.3 3.7 all-to-all-start
  27.1 2.9 dynamic-slice_bitcast_fusion.8
  31.4 4.8 %dynamic-slice_bitcast_fusion.3 = (bf16[320,1792]{1,0:T(8,128)(2,1)}, bf16[320,1792]{1,0:T(8,128)(2,1)}, bf16[1,320,1792]{2,1,0:T(8,128)(2,1)S(1)}, bf16[1,320,1...) fusion(bf16[1,4096,1792]{2,1,0:T(8,128)(2,1)} %param.7, ...), kind=kLoop, calls=%fused_computation.10 | loop fusion | bytes 13762584 | tf_op jit(solution)/shard_map/dynamic_slice | solution.py:193
  45.7 5.9 %all-to-all-done.refs_0_ = bf16[8,1040,128]{2,1,0:T(8,128)(2,1)S(1)} async-done(((bf16[8,1040,128]{2,1,0:T(8,128)(2,1)}), bf16[8,1040,128]{2,1,0:T(8,128)(2,1)S(1)}, u32[]{:S(2)}, u32[]{:S(2)}) %all-to-all-start) | async-done | bytes 2129952 | tf_op jit(solution)/shard_map/all_to_all | solution.py:207
  53.2 8.3 %collective-permute-start.5 = (bf16[8,1040,128]{2,1,0:T(8,128)(2,1)S(1)}, bf16[8,1040,128]{2,1,0:T(8,128)(2,1)}, u32[]{:S(2)}, u32[]{:S(2)}) collective-permute-start(bf16[8,1040,128]{2,1,0:T(8,128)(2,1)S(1)} %all-to-all-done.refs_0_), channel_id=1, source_target_pairs={{0,2},{1,3},{2,4},{3,5},{4,6},{5,7},{8,10},{9,11},{10,12},{11,13},... | collective-permute-start | bytes 6389768 | tf_op jit(solution)/shard_map/ppermute | solution.py:181
  64.5 26.5 %collective-permute-done.6 = bf16[128,7168]{1,0:T(8,128)(2,1)} collective-permute-done((bf16[128,7168]{1,0:T(8,128)(2,1)}, bf16[128,7168]{1,0:T(8,128)(2,1)}, u32[]{:S(2)}, u32[]{:S(2)}) %collective-permute-start.6) | collective-permute-done | bytes 1835040 | tf_op jit(solution)/shard_map/ppermute | solution.py:165
  94.8 8.6 %collective-permute-done.7 = bf16[4,128,1792]{2,1,0:T(8,128)(2,1)S(1)} collective-permute-done((bf16[4,128,1792]{2,1,0:T(8,128)(2,1)}, bf16[4,128,1792]{2,1,0:T(8,128)(2,1)S(1)}, u32[]{:S(2)}, u32[]{:S(2)}) %collective-permute-start.7) | collective-permute-done | bytes 1835040 | tf_op jit(solution)/shard_map/ppermute | solution.py:173
  104.8 25.1 %collective-permute-done.8 = bf16[2,256,1792]{2,1,0:T(8,128)(2,1)S(1)} collective-permute-done((bf16[2,256,1792]{2,1,0:T(8,128)(2,1)}, bf16[2,256,1792]{2,1,0:T(8,128)(2,1)S(1)}, u32[]{:S(2)}, u32[]{:S(2)}) %collective-permute-start.8) | collective-permute-done | bytes 1835040 | tf_op jit(solution)/shard_map/ppermute | solution.py:165
  137.8 9.2 %collective-permute-done.9 = bf16[128,1792]{1,0:T(8,128)(2,1)} collective-permute-done((bf16[128,1792]{1,0:T(8,128)(2,1)}, bf16[128,1792]{1,0:T(8,128)(2,1)}, u32[]{:S(2)}, u32[]{:S(2)}) %collective-permute-start.9) | collective-permute-done | bytes 458784 | tf_op jit(solution)/shard_map/ppermute | solution.py:169
  148.7 17.3 %collective-permute-done.10 = bf16[128,1792]{1,0:T(8,128)(2,1)} collective-permute-done((bf16[128,1792]{1,0:T(8,128)(2,1)S(1)}, bf16[128,1792]{1,0:T(8,128)(2,1)}, u32[]{:S(2)}, u32[]{:S(2)}) %collective-permute-start.10) | collective-permute-done | bytes 458784 | tf_op jit(solution)/shard_map/ppermute | solution.py:169
  168.9 15.2 %collective-permute-done.13 = bf16[2,320,1792]{2,1,0:T(8,128)(2,1)} collective-permute-done((bf16[2,320,1792]{2,1,0:T(8,128)(2,1)}, bf16[2,320,1792]{2,1,0:T(8,128)(2,1)}, u32[]{:S(2)}, u32[]{:S(2)}) %collective-permute-start.13) | collective-permute-done | bytes 2293792 | tf_op jit(solution)/shard_map/ppermute | solution.py:165
  197.7 32.5 %collective-permute-done.17 = bf16[4,128,1792]{2,1,0:T(8,128)(2,1)} collective-permute-done((bf16[4,128,1792]{2,1,0:T(8,128)(2,1)}, bf16[4,128,1792]{2,1,0:T(8,128)(2,1)}, u32[]{:S(2)}, u32[]{:S(2)}) %collective-permute-start.17) | collective-permute-done | bytes 1835040 | tf_op jit(solution)/shard_map/ppermute | solution.py:173
  243.6 3.2 fusion.3
  247.2 20.5 %collective-permute-done.21.refs_6_ = bf16[8,576,128]{2,1,0:T(8,128)(2,1)S(1)} collective-permute-done((bf16[8,576,128]{2,1,0:T(8,128)(2,1)S(1)}, bf16[8,576,128]{2,1,0:T(8,128)(2,1)S(1)}, u32[]{:S(2)}, u32[]{:S(2)}) %collective-permute-start.21) | collective-permute-done | bytes 1179680 | tf_op jit(solution)/shard_map/ppermute | solution.py:181
  269.1 18.7 %shard_map.46.refs_0_ = bf16[576,1792]{1,0:T(8,128)(2,1)} custom-call(s32[3]{0:T(128)} %pad_add_fusion.1.place_ref, s32[4]{0:T(128)} %and_select_fusion.slot_ref, bf16[8,1040,128]{2,1,0:T(8,128)(2,1)} %copy-done.2, bf16[8,1040,128]{2,1,0:T(8,128)(2,1)} %collective-permute-done.5.refs_1_, bf16[8,1040,128]{2,1,0:T(8,128)(2,1)} %collective-permute-done.14.refs_2_, ...), custom_call_target="tpu_custom_call" | custom-call | flops 8455716864 | bytes 14680064 | tf_op jit(solution)/shard_map/pallas_call | solution.py:84
  298.7 19.5 %collective-permute-done.24.refs_6_ = bf16[8,448,128]{2,1,0:T(8,128)(2,1)S(1)} collective-permute-done((bf16[8,448,128]{2,1,0:T(8,128)(2,1)S(1)}, bf16[8,448,128]{2,1,0:T(8,128)(2,1)S(1)}, u32[]{:S(2)}, u32[]{:S(2)}) %collective-permute-start.24) | collective-permute-done | bytes 917536 | tf_op jit(solution)/shard_map/ppermute | solution.py:181
  319.9 16.6 %shard_map.47.refs_0_ = bf16[448,1792]{1,0:T(8,128)(2,1)} custom-call(s32[3]{0:T(128)} %pad_add_fusion.1.place_ref, s32[4]{0:T(128)} %and_select_fusion.slot_ref, bf16[8,1040,128]{2,1,0:T(8,128)(2,1)} %copy-done.2, bf16[8,1040,128]{2,1,0:T(8,128)(2,1)} %collective-permute-done.5.refs_1_, bf16[8,1040,128]{2,1,0:T(8,128)(2,1)} %collective-permute-done.14.refs_2_, ...), custom_call_target="tpu_custom_call" | custom-call | flops 6576668672 | bytes 14680064 | tf_op jit(solution)/shard_map/pallas_call | solution.py:84
  338.9 4.0 %collective-permute-done.30.refs_1_ = bf16[576,1792]{1,0:T(8,128)(2,1)} collective-permute-done((bf16[576,1792]{1,0:T(8,128)(2,1)S(1)}, bf16[576,1792]{1,0:T(8,128)(2,1)}, u32[]{:S(2)}, u32[]{:S(2)}) %collective-permute-start.30) | collective-permute-done | bytes 2064416 | tf_op jit(solution)/shard_map/ppermute | solution.py:165
  344.0 6.7 %shard_map.48.refs_4_ = bf16[4096,1792]{1,0:T(8,128)(2,1)} custom-call(s32[4]{0:T(128)S(1)} %pad_add_fusion.2.where_ref, bf16[576,1792]{1,0:T(8,128)(2,1)S(1)} %copy-done, bf16[576,1792]{1,0:T(8,128)(2,1)} %collective-permute-done.30.refs_1_, bf16[576,1792]{1,0:T(8,128)(2,1)} %collective-permute-done.31.refs_2_, ...), custom_call_target="tpu_custom_call" | custom-call | bytes 16515072 | tf_op jit(solution)/shard_map/pallas_call | solution.py:126
  350.8 23.8 %collective-permute-done.29.refs_2_ = bf16[448,1792]{1,0:T(8,128)(2,1)} collective-permute-done((bf16[448,1792]{1,0:T(8,128)(2,1)}, bf16[448,1792]{1,0:T(8,128)(2,1)}, u32[]{:S(2)}, u32[]{:S(2)}) %collective-permute-start.29) | collective-permute-done | bytes 1605664 | tf_op jit(solution)/shard_map/ppermute | solution.py:165
  374.6 3.6 collective-permute-done.33.refs_3_
  379.6 5.2 %shard_map.49 = bf16[4096,1792]{1,0:T(8,128)(2,1)} custom-call(s32[4]{0:T(128)S(1)} %pad_add_fusion.where_ref, bf16[448,1792]{1,0:T(8,128)(2,1)S(1)} %copy-done.1, bf16[448,1792]{1,0:T(8,128)(2,1)} %collective-permute-done.28.refs_1_, bf16[448,1792]{1,0:T(8,128)(2,1)} %collective-permute-done.29.refs_2_, ...), custom_call_target="tpu_custom_call", output_to_operand_aliasing={{}: (5, {})} | custom-call | bytes 12845056 | tf_op jit(solution)/shard_map/pallas_call | solution.py:126
  (122 shorter events, 95.2 us)
Async XLA Ops:
  6.6 45.1 %collective-permute-start.3 = (bf16[1024,1792]{1,0:T(8,128)(2,1)}, bf16[1024,1792]{1,0:T(8,128)(2,1)}, u32[]{:S(2)}, u32[]{:S(2)}) collective-permute-start(bf16[1024,1792]{1,0:T(8,128)(2,1)} %dynamic-slice_bitcast_fusion), channel_id=1, source_target_pairs={{0,8},{8,0},{16,24},{24,16},{1,9},{9,1},{17,25},{25,17},{2,10},{10... | collective-permute-start | bytes 11010056 | tf_op jit(solution)/shard_map/ppermute | solution.py:165
  7.1 35.5 %collective-permute-start = (bf16[128,1792]{1,0:T(8,128)(2,1)}, bf16[128,1792]{1,0:T(8,128)(2,1)}, u32[]{:S(2)}, u32[]{:S(2)}) collective-permute-start(bf16[128,1792]{1,0:T(8,128)(2,1)} %get-tuple-element.85), channel_id=1, source_target_pairs={{0,2},{1,3},{2,4},{3,5},{4,6},{5,7},{6,0},{7,1},{8,10},{9,11},{10,... | collective-permute-start | bytes 1376264 | tf_op jit(solution)/shard_map/ppermute | solution.py:169
  9.6 33.3 %collective-permute-start.1 = (bf16[128,1792]{1,0:T(8,128)(2,1)S(1)}, bf16[128,1792]{1,0:T(8,128)(2,1)}, u32[]{:S(2)}, u32[]{:S(2)}) collective-permute-start(bf16[128,1792]{1,0:T(8,128)(2,1)S(1)} %get-tuple-element.84), channel_id=1, source_target_pairs={{0,4},{1,5},{2,6},{3,7},{4,0},{5,1},{6,2},{7,3},{8,12},{9,13},{10,... | collective-permute-start | bytes 1376264 | tf_op jit(solution)/shard_map/ppermute | solution.py:169
  12.2 30.7 %collective-permute-start.2 = (bf16[128,1792]{1,0:T(8,128)(2,1)S(1)}, bf16[128,1792]{1,0:T(8,128)(2,1)}, u32[]{:S(2)}, u32[]{:S(2)}) collective-permute-start(bf16[128,1792]{1,0:T(8,128)(2,1)S(1)} %get-tuple-element.83), channel_id=1, source_target_pairs={{0,6},{1,7},{2,0},{3,1},{4,2},{5,3},{6,4},{7,5},{8,14},{9,15},{10,... | collective-permute-start | bytes 1376264 | tf_op jit(solution)/shard_map/ppermute | solution.py:169
  25.1 66.0 %collective-permute-start.6 = (bf16[128,7168]{1,0:T(8,128)(2,1)}, bf16[128,7168]{1,0:T(8,128)(2,1)}, u32[]{:S(2)}, u32[]{:S(2)}) collective-permute-start(bf16[128,7168]{1,0:T(8,128)(2,1)} %bitcast.66), channel_id=1, source_target_pairs={{0,16},{8,24},{16,0},{24,8},{1,17},{9,25},{17,1},{25,9},{2,18},{10... | collective-permute-start | bytes 5505032 | tf_op jit(solution)/shard_map/ppermute | solution.py:165
  51.7 78.2 %collective-permute-start.4 = (bf16[8,1040,128]{2,1,0:T(8,128)(2,1)S(1)}, bf16[8,1040,128]{2,1,0:T(8,128)(2,1)}, u32[]{:S(2)}, u32[]{:S(2)}) collective-permute-start(bf16[8,1040,128]{2,1,0:T(8,128)(2,1)S(1)} %all-to-all-done.refs_0_), channel_id=1, source_target_pairs={{2,0},{3,1},{4,2},{5,3},{6,4},{7,5},{10,8},{11,9},{12,10},{13,11},... | collective-permute-start | bytes 6389768 | tf_op jit(solution)/shard_map/ppermute | solution.py:181
  53.2 76.6 %collective-permute-start.5 = (bf16[8,1040,128]{2,1,0:T(8,128)(2,1)S(1)}, bf16[8,1040,128]{2,1,0:T(8,128)(2,1)}, u32[]{:S(2)}, u32[]{:S(2)}) collective-permute-start(bf16[8,1040,128]{2,1,0:T(8,128)(2,1)S(1)} %all-to-all-done.refs_0_), channel_id=1, source_target_pairs={{0,2},{1,3},{2,4},{3,5},{4,6},{5,7},{8,10},{9,11},{10,12},{11,13},... | collective-permute-start | bytes 6389768 | tf_op jit(solution)/shard_map/ppermute | solution.py:181
  61.5 41.9 %collective-permute-start.7 = (bf16[4,128,1792]{2,1,0:T(8,128)(2,1)}, bf16[4,128,1792]{2,1,0:T(8,128)(2,1)S(1)}, u32[]{:S(2)}, u32[]{:S(2)}) collective-permute-start(bf16[4,128,1792]{2,1,0:T(8,128)(2,1)} %pad_maximum_fusion.3), channel_id=1, source_target_pairs={{0,1},{1,0},{2,3},{3,2},{4,5},{5,4},{6,7},{7,6},{8,9},{9,8},{10,11... | collective-permute-start | bytes 5505032 | tf_op jit(solution)/shard_map/ppermute | solution.py:173
  63.1 66.8 %collective-permute-start.8 = (bf16[2,256,1792]{2,1,0:T(8,128)(2,1)}, bf16[2,256,1792]{2,1,0:T(8,128)(2,1)S(1)}, u32[]{:S(2)}, u32[]{:S(2)}) collective-permute-start(bf16[2,256,1792]{2,1,0:T(8,128)(2,1)} %pad_maximum_fusion.4), channel_id=1, source_target_pairs={{0,16},{8,24},{16,0},{24,8},{1,17},{9,25},{17,1},{25,9},{2,18},{10... | collective-permute-start | bytes 5505032 | tf_op jit(solution)/shard_map/ppermute | solution.py:165
  131.1 53.0 %collective-permute-start.12 = (bf16[4,256,1792]{2,1,0:T(8,128)(2,1)}, bf16[4,256,1792]{2,1,0:T(8,128)(2,1)}, u32[]{:S(2)}, u32[]{:S(2)}) collective-permute-start(bf16[4,256,1792]{2,1,0:T(8,128)(2,1)} %constant_dynamic-update-slice_fusion.refs_7_), channel_id=1, source_target_pairs={{0,8},{8,0},{16,24},{24,16},{1,9},{9,1},{17,25},{25,17},{2,10},{10... | collective-permute-start | bytes 11010056 | tf_op jit(solution)/shard_map/ppermute | solution.py:165
  131.1 53.0 %collective-permute-start.13 = (bf16[2,320,1792]{2,1,0:T(8,128)(2,1)}, bf16[2,320,1792]{2,1,0:T(8,128)(2,1)}, u32[]{:S(2)}, u32[]{:S(2)}) collective-permute-start(bf16[2,320,1792]{2,1,0:T(8,128)(2,1)} %pad_maximum_fusion), channel_id=1, source_target_pairs={{0,16},{8,24},{16,0},{24,8},{1,17},{9,25},{17,1},{25,9},{2,18},{10... | collective-permute-start | bytes 6881288 | tf_op jit(solution)/shard_map/ppermute | solution.py:165
  132.1 33.9 %collective-permute-start.10 = (bf16[128,1792]{1,0:T(8,128)(2,1)S(1)}, bf16[128,1792]{1,0:T(8,128)(2,1)}, u32[]{:S(2)}, u32[]{:S(2)}) collective-permute-start(bf16[128,1792]{1,0:T(8,128)(2,1)S(1)} %get-tuple-element.39), channel_id=1, source_target_pairs={{0,4},{1,5},{2,6},{3,7},{4,0},{5,1},{6,2},{7,3},{8,12},{9,13},{10,... | collective-permute-start | bytes 1376264 | tf_op jit(solution)/shard_map/ppermute | solution.py:169
  132.4 33.6 %collective-permute-start.11 = (bf16[128,1792]{1,0:T(8,128)(2,1)S(1)}, bf16[128,1792]{1,0:T(8,128)(2,1)}, u32[]{:S(2)}, u32[]{:S(2)}) collective-permute-start(bf16[128,1792]{1,0:T(8,128)(2,1)S(1)} %get-tuple-element.40), channel_id=1, source_target_pairs={{0,6},{1,7},{2,0},{3,1},{4,2},{5,3},{6,4},{7,5},{8,14},{9,15},{10,... | collective-permute-start | bytes 1376264 | tf_op jit(solution)/shard_map/ppermute | solution.py:169
  147.0 86.0 %collective-permute-start.16 = (bf16[2,320,1792]{2,1,0:T(8,128)(2,1)}, bf16[2,320,1792]{2,1,0:T(8,128)(2,1)}, u32[]{:S(2)}, u32[]{:S(2)}) collective-permute-start(bf16[2,320,1792]{2,1,0:T(8,128)(2,1)} %pad_maximum_fusion.1), channel_id=1, source_target_pairs={{0,16},{8,24},{16,0},{24,8},{1,17},{9,25},{17,1},{25,9},{2,18},{10... | collective-permute-start | bytes 6881288 | tf_op jit(solution)/shard_map/ppermute | solution.py:165
  184.0 50.9 %collective-permute-start.15 = (bf16[8,1040,128]{2,1,0:T(8,128)(2,1)}, bf16[8,1040,128]{2,1,0:T(8,128)(2,1)}, u32[]{:S(2)}, u32[]{:S(2)}) collective-permute-start(bf16[8,1040,128]{2,1,0:T(8,128)(2,1)} %collective-permute-done.4.refs_4_), channel_id=1, source_target_pairs={{2,0},{3,1},{4,2},{5,3},{10,8},{11,9},{12,10},{13,11},{18,16},{19,... | collective-permute-start | bytes 6389768 | tf_op jit(solution)/shard_map/ppermute | solution.py:181
  185.3 49.7 %collective-permute-start.14 = (bf16[8,1040,128]{2,1,0:T(8,128)(2,1)}, bf16[8,1040,128]{2,1,0:T(8,128)(2,1)}, u32[]{:S(2)}, u32[]{:S(2)}) collective-permute-start(bf16[8,1040,128]{2,1,0:T(8,128)(2,1)} %collective-permute-done.5.refs_1_), channel_id=1, source_target_pairs={{2,4},{3,5},{4,6},{5,7},{10,12},{11,13},{12,14},{13,15},{18,20},{1... | collective-permute-start | bytes 6389768 | tf_op jit(solution)/shard_map/ppermute | solution.py:181
  187.4 42.7 %collective-permute-start.17 = (bf16[4,128,1792]{2,1,0:T(8,128)(2,1)}, bf16[4,128,1792]{2,1,0:T(8,128)(2,1)}, u32[]{:S(2)}, u32[]{:S(2)}) collective-permute-start(bf16[4,128,1792]{2,1,0:T(8,128)(2,1)} %pad_maximum_fusion.5), channel_id=1, source_target_pairs={{0,1},{1,0},{2,3},{3,2},{4,5},{5,4},{6,7},{7,6},{8,9},{9,8},{10,11... | collective-permute-start | bytes 5505032 | tf_op jit(solution)/shard_map/ppermute | solution.py:173
  191.7 41.4 %collective-permute-start.19 = (bf16[320,1792]{1,0:T(8,128)(2,1)S(1)}, bf16[320,1792]{1,0:T(8,128)(2,1)}, u32[]{:S(2)}, u32[]{:S(2)}) collective-permute-start(bf16[320,1792]{1,0:T(8,128)(2,1)S(1)} %get-tuple-element.48), channel_id=1, source_target_pairs={{0,8},{8,0},{16,24},{24,16},{1,9},{9,1},{17,25},{25,17},{2,10},{10... | collective-permute-start | bytes 3440648 | tf_op jit(solution)/shard_map/ppermute | solution.py:165
  235.0 32.7 %collective-permute-start.22 = (bf16[4,256,1792]{2,1,0:T(8,128)(2,1)}, bf16[4,256,1792]{2,1,0:T(8,128)(2,1)}, u32[]{:S(2)}, u32[]{:S(2)}) collective-permute-start(bf16[4,256,1792]{2,1,0:T(8,128)(2,1)} %constant_dynamic-update-slice_fusion.2.refs_9_), channel_id=1, source_target_pairs={{0,8},{8,0},{16,24},{24,16},{1,9},{9,1},{17,25},{25,17},{2,10},{10... | collective-permute-start | bytes 11010056 | tf_op jit(solution)/shard_map/ppermute | solution.py:165
  236.3 31.4 %collective-permute-start.21 = (bf16[8,576,128]{2,1,0:T(8,128)(2,1)S(1)}, bf16[8,576,128]{2,1,0:T(8,128)(2,1)S(1)}, u32[]{:S(2)}, u32[]{:S(2)}) collective-permute-start(bf16[8,576,128]{2,1,0:T(8,128)(2,1)S(1)} %slice.41), channel_id=1, source_target_pairs={{2,0},{3,1},{10,8},{11,9},{18,16},{19,17},{26,24},{27,25}} | collective-permute-start | bytes 3538952 | tf_op jit(solution)/shard_map/ppermute | solution.py:181
  246.8 48.8 %collective-permute-start.26 = (bf16[2,128,1792]{2,1,0:T(8,128)(2,1)S(1)}, bf16[2,128,1792]{2,1,0:T(8,128)(2,1)S(1)}, u32[]{:S(2)}, u32[]{:S(2)}) collective-permute-start(bf16[2,128,1792]{2,1,0:T(8,128)(2,1)S(1)} %copy-done.9), channel_id=1, source_target_pairs={{0,16},{8,24},{16,0},{24,8},{1,17},{9,25},{17,1},{25,9},{2,18},{10... | collective-permute-start | bytes 2752520 | tf_op jit(solution)/shard_map/ppermute | solution.py:165
  287.8 48.8 %collective-permute-start.31 = (bf16[576,1792]{1,0:T(8,128)(2,1)}, bf16[576,1792]{1,0:T(8,128)(2,1)}, u32[]{:S(2)}, u32[]{:S(2)}) collective-permute-start(bf16[576,1792]{1,0:T(8,128)(2,1)} %shard_map.46.refs_0_), channel_id=1, source_target_pairs={{0,16},{8,24},{16,0},{24,8},{1,17},{9,25},{17,1},{25,9},{2,18},{10... | collective-permute-start | bytes 6193160 | tf_op jit(solution)/shard_map/ppermute | solution.py:165
  337.1 37.4 %collective-permute-start.29 = (bf16[448,1792]{1,0:T(8,128)(2,1)}, bf16[448,1792]{1,0:T(8,128)(2,1)}, u32[]{:S(2)}, u32[]{:S(2)}) collective-permute-start(bf16[448,1792]{1,0:T(8,128)(2,1)} %shard_map.47.refs_0_), channel_id=1, source_target_pairs={{0,16},{8,24},{16,0},{24,8},{1,17},{9,25},{17,1},{25,9},{2,18},{10... | collective-permute-start | bytes 4816904 | tf_op jit(solution)/shard_map/ppermute | solution.py:165
  338.9 35.7 %collective-permute-start.28 = (bf16[448,1792]{1,0:T(8,128)(2,1)}, bf16[448,1792]{1,0:T(8,128)(2,1)}, u32[]{:S(2)}, u32[]{:S(2)}) collective-permute-start(bf16[448,1792]{1,0:T(8,128)(2,1)} %shard_map.47.refs_0_), channel_id=1, source_target_pairs={{0,8},{8,0},{16,24},{24,16},{1,9},{9,1},{17,25},{25,17},{2,10},{10... | collective-permute-start | bytes 4816904 | tf_op jit(solution)/shard_map/ppermute | solution.py:165
  (26 other events, 422.4 us)

commit v6 on v5

--- a/solution.py
+++ b/solution.py
@@ -9,7 +9,7 @@
 
 F = 7168
 SEQS = 2
-CHUNKS = (16, 20, 20, 8)
+CHUNKS = (3, 5, 4, 4)
 FLAG_ROWS = 16
 COL_TILE = 256
 
@@ -195,19 +195,19 @@
     def mate(value, *others):
         return to_copy(after(value, *others), 1)
 
-    grad_far = to_copy(out_grads[0], 2)
     cut = cut_blocks(out_grads[0])
     grad_near = spread_blocks(cut)
     acts = after(activations[0], *cut).T.reshape(spread, copies, share, tok).transpose(1, 0, 2, 3)
     named = jnp.broadcast_to(seq_ids[0].astype(acts.dtype), acts.shape[:2] + (FLAG_ROWS, tok))
     acts = jnp.concatenate([acts, named], axis=2).reshape(copies * spread, share + FLAG_ROWS, tok)
+    grad_far = to_copy(after(out_grads[0], acts), 2)
     planes = [
         [c * devices + block * spread + s for c in range(copies) for s in range(spread)] for block in range(blocks)
     ]
     own = lax.all_to_all(acts, ("mp", "fsdp"), 0, 0, axis_index_groups=planes, tiled=True)
     leaving = [jnp.stack([weight_rows((1 - chip) * 2 + c, k) for c in range(2)]) for k in range(len(sizes))]
-    mate_rows = lax.dynamic_slice_in_dim(weights[0], (chip * 2 + 1 - core) * share, share, 0)
-    mate_rows = mate(mate_rows, *cut)
+    owner = after(chip * 2 + 1 - core, acts)
+    mate_rows = to_copy(lax.dynamic_slice_in_dim(weights[0], owner * share, share, 0), 1)
 
     weight_far = [None] * len(sizes)
     weight_mate = [None] * len(sizes)
@@ -216,23 +216,24 @@
         weight_far[k] = to_copy(after(leaving[k], *others), 2)
 
     def cores(k, *others):
-        weight_mate[k] = mate(lax.dynamic_index_in_dim(weight_far[k], 1 - core, 0, keepdims=False), *others)
+        other = after(1 - core, *others)
+        weight_mate[k] = to_copy(lax.dynamic_index_in_dim(weight_far[k], other, 0, keepdims=False), 1)
 
     grads = [None] * copies
-    stage = (own, grad_near, mate_rows, *leaving)
+    stage = (own, grad_near, *leaving)
     early = stage
     low, high = [along(after(own, *stage), 1, 1)], [along(after(own, *stage), 1, -1)]
-    send_weights(0, *stage)
+    send_weights(0, *stage, grad_far)
     grads[0] = over_halves(after(grad_near, *stage))
 
     send_weights(1, *early)
     cut = cut_blocks(grad_far)
-    stage = (low[0], high[0], grads[0], weight_far[0], *cut)
+    stage = (low[0], high[0], grads[0], mate_rows, weight_far[0], *cut)
     early = stage
     grad_far = spread_blocks([after(block, *stage) for block in cut])
     grads[1] = mate(grads[0], *stage)
 
-    stage = (grad_far, grads[1], weight_far[1])
+    stage = (grad_far, grads[1])
     low.append(along(after(low[0], *stage), 2, 1))
     high.append(along(after(high[0], *stage), 2, -1))
     send_weights(2, *early)
@@ -254,30 +255,31 @@
     high_last.append(along(after(high[1], *stage)[:, half:share], 3, -1))
     cores(2, *stage, grads[3])
     send_weights(3, *early)
-    cores(3, low_last[0], high_last[0])
-
-    merged = []
-    for part in range(2):
+
+    def sums(part, pieces, place, *others):
         held = []
-        for k in (2 * part, 2 * part + 1):
-            mine = lax.dynamic_index_in_dim(weight_far[k], core, 0, keepdims=False)
+        for k in pieces:
+            mine = lax.dynamic_index_in_dim(weight_far[k], after(core, *others), 0, keepdims=False)
             held += [weight_rows(m, k), mate_rows[starts[k]:starts[k] + sizes[k]], mine, weight_mate[k]]
         sources = [own, low[0], low[1], low_last[part], high[0], high[1], high_last[part]]
         begin = [part * half] * len(sources)
         begin[3] = begin[6] = 0
-        merged.append(merge_rows(place, slots, sources, begin, grads, held))
-        place = after(place, merged[-1])
-    far = [to_copy(mine, 2) for mine in merged]
-    near = after(merged[0], merged[1])
-    came = after(far[0], merged[1])
-    whole = None
-    for part in range(2):
-        if part == 1:
-            near, came = merged[1], after(far[1], whole)
-        pieces = [merged[part], to_copy(near, 1), far[part], to_copy(came, 1)]
-        where = [(m ^ flip) * share + part * half for flip in range(copies)]
-        whole = place_rows(rows, pieces, where, whole)
-    return whole
+        return merge_rows(place, slots, sources, begin, grads, held)
+
+    where = [[(m ^ flip) * share + part * half for flip in range(copies)] for part in range(2)]
+    first = sums(0, (0, 1), place)
+    far_first = to_copy(first, 2)
+    cores(3, first)
+    second = sums(1, (2, 3), after(place, first), first)
+    far_second = to_copy(second, 2)
+    near_first = to_copy(after(first, second), 1)
+    near_second = to_copy(second, 1)
+    mate_first = to_copy(after(far_first, second), 1)
+    pieces = [first, near_first, far_first, mate_first, second, near_second]
+    whole = place_rows(rows, pieces, where[0] + where[1][:2], None)
+    mate_second = to_copy(after(far_second, whole), 1)
+    whole = place_rows(rows, [far_second], where[1][2:3], whole)
+    return place_rows(rows, [mate_second], where[1][3:], whole)
 
 
 def solution(mesh):

time: 389 us -> 366 us (0.941)
  waiting for transfers between devices: 215 us -> 199 us
    ppermute x8, waiting for transfers between devices: 42 us -> 28.8 us  [along(): return lax.ppermute(value, 'fsdp', pairs)]
    ppermute x2, waiting for transfers between devices: 41.1 us -> 32.3 us  [to_half(): return lax.ppermute(value, 'fsdp', pairs)]
    ppermute x6, waiting for transfers between devices: 26.9 us -> 35.2 us  [to_block(): return lax.ppermute(value, 'fsdp', pairs)]
    all_to_all x1, waiting for transfers between devices: 5.92 us -> 0.01 us  [per_device(): lax.all_to_all(acts, ('mp', 'fsdp'), 0, 0, axis_index_groups=planes, tile...]
    slice x5 -> x3, local copies, waits for them, and re-layouts: 11 us -> 7.11 us  [sums(): mate_rows[starts[k]:starts[k] + sizes[k]]]
    unnamed x32 -> x22, local copies, waits for them, and re-layouts: 10.7 us -> 8.17 us
    pallas_call x2 -> x3, Pallas kernels: 12 us -> 11.9 us  [place_rows(): pl.pallas_call(functools.partial(place_kernel, count), out_shape=shape, g...]
  transfers between devices with their start and end apart: 35 -> 35, of which waited for: 16 -> 15; matrix products, arithmetic and copies ran while one was open for 17% -> 19% of each run, Pallas kernels for 11% -> 13%
where the time goes in v6:
time: 366 us; the launch traced here: 365 us
  waiting for transfers between devices  199 us (54%)
  local copies, waits for them, and re-layouts  61.9 us (17%)
  Pallas kernels  47.2 us (13%)
  starting transfers between devices  41.6 us (11%)
  other arithmetic  14.5 us (4%)
    ppermute x18, waiting for transfers between devices, to_copy(): return lax.ppermute(value, 'mp', [(s, s ^ flip) for s in range(copies)])  103 us
    pallas_call x2, Pallas kernels, merge_rows(): pl.pallas_call(functools.partial(merge_kernel, copies, shards, starts, si...  35.4 us
    ppermute x6, waiting for transfers between devices, to_block(): return lax.ppermute(value, 'fsdp', pairs)  35.2 us
    ppermute x2, waiting for transfers between devices, to_half(): return lax.ppermute(value, 'fsdp', pairs)  32.3 us
    ppermute x8, waiting for transfers between devices, along(): return lax.ppermute(value, 'fsdp', pairs)  28.8 us
    ppermute x8, starting transfers between devices, along(): return lax.ppermute(value, 'fsdp', pairs)  14.1 us
    pallas_call x3, Pallas kernels, place_rows(): pl.pallas_call(functools.partial(place_kernel, count), out_shape=shape, g...  11.9 us
    ppermute x6, starting transfers between devices, to_block(): return lax.ppermute(value, 'fsdp', pairs)  10.9 us
  transfers between devices with their start and end apart: 35, of which 15 were waited for; matrix products, arithmetic and copies ran while one was open for 19% of the time, Pallas kernels for 13%

profile of v6, /device:TPU:0, one launch (start us, length us, event | category | flops | bytes accessed | tf_op | source)
XLA Modules:
  0.0 364.7 jit_solution(12295536327238190559)
XLA Ops:
  2.6 5.0 %collective-permute-start.2 = (bf16[128,1792]{1,0:T(8,128)(2,1)}, bf16[128,1792]{1,0:T(8,128)(2,1)S(1)}, u32[]{:S(2)}, u32[]{:S(2)}) collective-permute-start(bf16[128,1792]{1,0:T(8,128)(2,1)} %get-tuple-element.92), channel_id=1, source_target_pairs={{0,6},{1,7},{2,0},{3,1},{4,2},{5,3},{6,4},{7,5},{8,14},{9,15},{10,... | collective-permute-start | bytes 1376264 | tf_op jit(solution)/shard_map/ppermute | solution.py:169
  11.5 3.4 copy.8
  16.4 3.7 %all-to-all-start = ((bf16[8,1040,128]{2,1,0:T(8,128)(2,1)}), bf16[8,1040,128]{2,1,0:T(8,128)(2,1)S(1)}, u32[]{:S(2)}, u32[]{:S(2)}) async-start(bf16[8,1040,128]{2,1,0:T(8,128)(2,1)} %bitcast.61), calls=%async_computation | async-start | bytes 4259840 | tf_op jit(solution)/shard_map/all_to_all | solution.py:207
  22.2 4.1 %dynamic-slice_bitcast_fusion = bf16[1024,1792]{1,0:T(8,128)(2,1)} fusion(bf16[1,4096,1792]{2,1,0:T(8,128)(2,1)} %param.7, s32[]{:T(128)S(6)} %select_n.186), kind=kLoop, calls=%fused_computation.1 | loop fusion | bytes 7340036 | tf_op jit(solution)/shard_map/dynamic_slice | solution.py:210
  26.2 4.2 %dynamic-slice_bitcast_fusion.6 = (bf16[256,1792]{1,0:T(8,128)(2,1)}, bf16[1,256,1792]{2,1,0:T(8,128)(2,1)S(1)}, bf16[1,256,1792]{2,1,0:T(8,128)(2,1)S(1)}, bf16...) fusion(bf16[1,4096,1792]{2,1,0:T(8,128)(2,1)} %param.7, ...), kind=kLoop, calls=%fused_computation.14 | loop fusion | bytes 11010072 | tf_op jit(solution)/shard_map/dynamic_slice | solution.py:193
  36.9 3.2 dynamic-slice_bitcast_fusion.2
  41.7 5.5 %collective-permute-done.1 = bf16[128,1792]{1,0:T(8,128)(2,1)} collective-permute-done((bf16[128,1792]{1,0:T(8,128)(2,1)}, bf16[128,1792]{1,0:T(8,128)(2,1)}, u32[]{:S(2)}, u32[]{:S(2)}) %collective-permute-start.1) | collective-permute-done | bytes 458784 | tf_op jit(solution)/shard_map/ppermute | solution.py:169
  49.8 4.3 %collective-permute-start.4 = (bf16[8,1040,128]{2,1,0:T(8,128)(2,1)S(1)}, bf16[8,1040,128]{2,1,0:T(8,128)(2,1)}, u32[]{:S(2)}, u32[]{:S(2)}) collective-permute-start(bf16[8,1040,128]{2,1,0:T(8,128)(2,1)S(1)} %all-to-all-done.refs_0_), channel_id=1, source_target_pairs={{0,2},{1,3},{2,4},{3,5},{4,6},{5,7},{8,10},{9,11},{10,12},{11,13},... | collective-permute-start | bytes 6389768 | tf_op jit(solution)/shard_map/ppermute | solution.py:181
  57.0 28.7 %collective-permute-done.5 = bf16[128,7168]{1,0:T(8,128)(2,1)} collective-permute-done((bf16[128,7168]{1,0:T(8,128)(2,1)}, bf16[128,7168]{1,0:T(8,128)(2,1)}, u32[]{:S(2)}, u32[]{:S(2)}) %collective-permute-start.5) | collective-permute-done | bytes 1835040 | tf_op jit(solution)/shard_map/ppermute | solution.py:165
  89.8 6.8 %collective-permute-done.6 = bf16[4,128,1792]{2,1,0:T(8,128)(2,1)S(1)} collective-permute-done((bf16[4,128,1792]{2,1,0:T(8,128)(2,1)}, bf16[4,128,1792]{2,1,0:T(8,128)(2,1)S(1)}, u32[]{:S(2)}, u32[]{:S(2)}) %collective-permute-start.6) | collective-permute-done | bytes 1835040 | tf_op jit(solution)/shard_map/ppermute | solution.py:173
  97.9 19.8 %collective-permute-done.8 = bf16[2,192,1792]{2,1,0:T(8,128)(2,1)S(1)} collective-permute-done((bf16[2,192,1792]{2,1,0:T(8,128)(2,1)}, bf16[2,192,1792]{2,1,0:T(8,128)(2,1)S(1)}, u32[]{:S(2)}, u32[]{:S(2)}) %collective-permute-start.8) | collective-permute-done | bytes 1376288 | tf_op jit(solution)/shard_map/ppermute | solution.py:165
  124.3 10.8 %collective-permute-done.9 = bf16[128,1792]{1,0:T(8,128)(2,1)} collective-permute-done((bf16[128,1792]{1,0:T(8,128)(2,1)}, bf16[128,1792]{1,0:T(8,128)(2,1)}, u32[]{:S(2)}, u32[]{:S(2)}) %collective-permute-start.9) | collective-permute-done | bytes 458784 | tf_op jit(solution)/shard_map/ppermute | solution.py:169
  135.1 19.0 %collective-permute-done.10 = bf16[128,1792]{1,0:T(8,128)(2,1)} collective-permute-done((bf16[128,1792]{1,0:T(8,128)(2,1)S(1)}, bf16[128,1792]{1,0:T(8,128)(2,1)}, u32[]{:S(2)}, u32[]{:S(2)}) %collective-permute-start.10) | collective-permute-done | bytes 458784 | tf_op jit(solution)/shard_map/ppermute | solution.py:169
  165.3 6.4 %collective-permute-done.17 = bf16[2,320,1792]{2,1,0:T(8,128)(2,1)} collective-permute-done((bf16[2,320,1792]{2,1,0:T(8,128)(2,1)}, bf16[2,320,1792]{2,1,0:T(8,128)(2,1)}, u32[]{:S(2)}, u32[]{:S(2)}) %collective-permute-start.17) | collective-permute-done | bytes 2293792 | tf_op jit(solution)/shard_map/ppermute | solution.py:165
  179.7 25.5 %collective-permute-done.16 = bf16[4,128,1792]{2,1,0:T(8,128)(2,1)} collective-permute-done((bf16[4,128,1792]{2,1,0:T(8,128)(2,1)}, bf16[4,128,1792]{2,1,0:T(8,128)(2,1)}, u32[]{:S(2)}, u32[]{:S(2)}) %collective-permute-start.16) | collective-permute-done | bytes 1835040 | tf_op jit(solution)/shard_map/ppermute | solution.py:173
  210.7 10.5 %collective-permute-done.14.refs_5_ = bf16[8,1040,128]{2,1,0:T(8,128)(2,1)} collective-permute-done((bf16[8,1040,128]{2,1,0:T(8,128)(2,1)}, bf16[8,1040,128]{2,1,0:T(8,128)(2,1)}, u32[]{:S(2)}, u32[]{:S(2)}) %collective-permute-start.14) | collective-permute-done | bytes 2129952 | tf_op jit(solution)/shard_map/ppermute | solution.py:181
  221.2 3.0 fusion.5
  226.1 3.1 fusion.4
  239.0 18.3 %collective-permute-done.21.refs_6_ = bf16[8,512,128]{2,1,0:T(8,128)(2,1)} collective-permute-done((bf16[8,512,128]{2,1,0:T(8,128)(2,1)}, bf16[8,512,128]{2,1,0:T(8,128)(2,1)}, u32[]{:S(2)}, u32[]{:S(2)}) %collective-permute-start.21) | collective-permute-done | bytes 1048608 | tf_op jit(solution)/shard_map/ppermute | solution.py:181
  257.3 17.7 %shard_map.46.refs_0_ = bf16[512,1792]{1,0:T(8,128)(2,1)} custom-call(s32[3]{0:T(128)} %pad_add_fusion.place_ref, s32[4]{0:T(128)} %and_select_fusion.slot_ref, bf16[8,1040,128]{2,1,0:T(8,128)(2,1)} %copy-done.2, bf16[8,1040,128]{2,1,0:T(8,128)(2,1)} %collective-permute-done.4.refs_1_, bf16[8,1040,128]{2,1,0:T(8,128)(2,1)} %collective-permute-done.13.refs_2_, ...), custom_call_target="tpu_custom_call" | custom-call | flops 7516192768 | bytes 14680064 | tf_op jit(solution)/shard_map/pallas_call | solution.py:84
  286.3 17.7 %shard_map.47.refs_4_ = bf16[512,1792]{1,0:T(8,128)(2,1)} custom-call(s32[3]{0:T(128)} %pad_add_fusion.place_ref, s32[4]{0:T(128)} %and_select_fusion.slot_ref, bf16[8,1040,128]{2,1,0:T(8,128)(2,1)} %copy-done.2, bf16[8,1040,128]{2,1,0:T(8,128)(2,1)} %collective-permute-done.4.refs_1_, bf16[8,1040,128]{2,1,0:T(8,128)(2,1)} %collective-permute-done.13.refs_2_, ...), custom_call_target="tpu_custom_call" | custom-call | flops 7516192768 | bytes 14680064 | tf_op jit(solution)/shard_map/pallas_call | solution.py:84
  304.6 12.0 %collective-permute-done.30.refs_2_ = bf16[512,1792]{1,0:T(8,128)(2,1)} collective-permute-done((bf16[512,1792]{1,0:T(8,128)(2,1)}, bf16[512,1792]{1,0:T(8,128)(2,1)}, u32[]{:S(2)}, u32[]{:S(2)}) %collective-permute-start.30) | collective-permute-done | bytes 1835040 | tf_op jit(solution)/shard_map/ppermute | solution.py:165
  322.2 7.9 %shard_map.48.refs_1_ = bf16[4096,1792]{1,0:T(8,128)(2,1)} custom-call(s32[6]{0:T(128)S(1)} %stack.111.where_ref, bf16[512,1792]{1,0:T(8,128)(2,1)S(1)} %copy-done, bf16[512,1792]{1,0:T(8,128)(2,1)} %collective-permute-done.29.refs_1_, bf16[512,1792]{1,0:T(8,128)(2,1)} %collective-permute-done.30.refs_2_, bf16[512,1792]{1,0:T(8,128)(2,1)} %collective-permute-done.31.refs_3_, ...), custom_call_target="tpu_custom_call" | custom-call | bytes 22020096 | tf_op jit(solution)/shard_map/pallas_call | solution.py:126
  330.1 29.2 %collective-permute-done.28.refs_0_ = bf16[512,1792]{1,0:T(8,128)(2,1)} collective-permute-done((bf16[512,1792]{1,0:T(8,128)(2,1)}, bf16[512,1792]{1,0:T(8,128)(2,1)}, u32[]{:S(2)}, u32[]{:S(2)}) %collective-permute-start.28) | collective-permute-done | bytes 1835040 | tf_op jit(solution)/shard_map/ppermute | solution.py:165
  (110 shorter events, 94.5 us)
Async XLA Ops:
  2.6 39.0 %collective-permute-start.2 = (bf16[128,1792]{1,0:T(8,128)(2,1)}, bf16[128,1792]{1,0:T(8,128)(2,1)S(1)}, u32[]{:S(2)}, u32[]{:S(2)}) collective-permute-start(bf16[128,1792]{1,0:T(8,128)(2,1)} %get-tuple-element.92), channel_id=1, source_target_pairs={{0,6},{1,7},{2,0},{3,1},{4,2},{5,3},{6,4},{7,5},{8,14},{9,15},{10,... | collective-permute-start | bytes 1376264 | tf_op jit(solution)/shard_map/ppermute | solution.py:169
  7.7 39.5 %collective-permute-start.1 = (bf16[128,1792]{1,0:T(8,128)(2,1)}, bf16[128,1792]{1,0:T(8,128)(2,1)}, u32[]{:S(2)}, u32[]{:S(2)}) collective-permute-start(bf16[128,1792]{1,0:T(8,128)(2,1)} %get-tuple-element.93), channel_id=1, source_target_pairs={{0,4},{1,5},{2,6},{3,7},{4,0},{5,1},{6,2},{7,3},{8,12},{9,13},{10,... | collective-permute-start | bytes 1376264 | tf_op jit(solution)/shard_map/ppermute | solution.py:169
  7.7 39.5 %collective-permute-start = (bf16[128,1792]{1,0:T(8,128)(2,1)S(1)}, bf16[128,1792]{1,0:T(8,128)(2,1)}, u32[]{:S(2)}, u32[]{:S(2)}) collective-permute-start(bf16[128,1792]{1,0:T(8,128)(2,1)S(1)} %get-tuple-element.94), channel_id=1, source_target_pairs={{0,2},{1,3},{2,4},{3,5},{4,6},{5,7},{6,0},{7,1},{8,10},{9,11},{10,... | collective-permute-start | bytes 1376264 | tf_op jit(solution)/shard_map/ppermute | solution.py:169
  16.4 33.4 %all-to-all-start = ((bf16[8,1040,128]{2,1,0:T(8,128)(2,1)}), bf16[8,1040,128]{2,1,0:T(8,128)(2,1)S(1)}, u32[]{:S(2)}, u32[]{:S(2)}) async-start(bf16[8,1040,128]{2,1,0:T(8,128)(2,1)} %bitcast.61), calls=%async_computation | async-start | bytes 4259840 | tf_op jit(solution)/shard_map/all_to_all | solution.py:207
  20.1 65.6 %collective-permute-start.5 = (bf16[128,7168]{1,0:T(8,128)(2,1)}, bf16[128,7168]{1,0:T(8,128)(2,1)}, u32[]{:S(2)}, u32[]{:S(2)}) collective-permute-start(bf16[128,7168]{1,0:T(8,128)(2,1)} %bitcast.65), channel_id=1, source_target_pairs={{0,16},{8,24},{16,0},{24,8},{1,17},{9,25},{17,1},{25,9},{2,18},{10... | collective-permute-start | bytes 5505032 | tf_op jit(solution)/shard_map/ppermute | solution.py:165
  26.2 91.4 %collective-permute-start.7 = (bf16[1024,1792]{1,0:T(8,128)(2,1)}, bf16[1024,1792]{1,0:T(8,128)(2,1)}, u32[]{:S(2)}, u32[]{:S(2)}) collective-permute-start(bf16[1024,1792]{1,0:T(8,128)(2,1)} %dynamic-slice_bitcast_fusion), channel_id=1, source_target_pairs={{0,8},{8,0},{16,24},{24,16},{1,9},{9,1},{17,25},{25,17},{2,10},{10... | collective-permute-start | bytes 11010056 | tf_op jit(solution)/shard_map/ppermute | solution.py:165
  49.8 67.8 %collective-permute-start.4 = (bf16[8,1040,128]{2,1,0:T(8,128)(2,1)S(1)}, bf16[8,1040,128]{2,1,0:T(8,128)(2,1)}, u32[]{:S(2)}, u32[]{:S(2)}) collective-permute-start(bf16[8,1040,128]{2,1,0:T(8,128)(2,1)S(1)} %all-to-all-done.refs_0_), channel_id=1, source_target_pairs={{0,2},{1,3},{2,4},{3,5},{4,6},{5,7},{8,10},{9,11},{10,12},{11,13},... | collective-permute-start | bytes 6389768 | tf_op jit(solution)/shard_map/ppermute | solution.py:181
  54.1 63.6 %collective-permute-start.3 = (bf16[8,1040,128]{2,1,0:T(8,128)(2,1)S(1)}, bf16[8,1040,128]{2,1,0:T(8,128)(2,1)}, u32[]{:S(2)}, u32[]{:S(2)}) collective-permute-start(bf16[8,1040,128]{2,1,0:T(8,128)(2,1)S(1)} %all-to-all-done.refs_0_), channel_id=1, source_target_pairs={{2,0},{3,1},{4,2},{5,3},{6,4},{7,5},{10,8},{11,9},{12,10},{13,11},... | collective-permute-start | bytes 6389768 | tf_op jit(solution)/shard_map/ppermute | solution.py:181
  55.4 41.1 %collective-permute-start.6 = (bf16[4,128,1792]{2,1,0:T(8,128)(2,1)}, bf16[4,128,1792]{2,1,0:T(8,128)(2,1)S(1)}, u32[]{:S(2)}, u32[]{:S(2)}) collective-permute-start(bf16[4,128,1792]{2,1,0:T(8,128)(2,1)} %pad_maximum_fusion.2), channel_id=1, source_target_pairs={{0,1},{1,0},{2,3},{3,2},{4,5},{5,4},{6,7},{7,6},{8,9},{9,8},{10,11... | collective-permute-start | bytes 5505032 | tf_op jit(solution)/shard_map/ppermute | solution.py:173
  85.7 31.9 %collective-permute-start.8 = (bf16[2,192,1792]{2,1,0:T(8,128)(2,1)}, bf16[2,192,1792]{2,1,0:T(8,128)(2,1)S(1)}, u32[]{:S(2)}, u32[]{:S(2)}) collective-permute-start(bf16[2,192,1792]{2,1,0:T(8,128)(2,1)} %pad_maximum_fusion.6), channel_id=1, source_target_pairs={{0,16},{8,24},{16,0},{24,8},{1,17},{9,25},{17,1},{25,9},{2,18},{10... | collective-permute-start | bytes 4128776 | tf_op jit(solution)/shard_map/ppermute | solution.py:165
  118.8 38.0 %collective-permute-start.12 = (bf16[4,256,1792]{2,1,0:T(8,128)(2,1)}, bf16[4,256,1792]{2,1,0:T(8,128)(2,1)}, u32[]{:S(2)}, u32[]{:S(2)}) collective-permute-start(bf16[4,256,1792]{2,1,0:T(8,128)(2,1)} %constant_dynamic-update-slice_fusion.refs_7_), channel_id=1, source_target_pairs={{0,8},{8,0},{16,24},{24,16},{1,9},{9,1},{17,25},{25,17},{2,10},{10... | collective-permute-start | bytes 11010056 | tf_op jit(solution)/shard_map/ppermute | solution.py:165
  118.8 53.0 %collective-permute-start.17 = (bf16[2,320,1792]{2,1,0:T(8,128)(2,1)}, bf16[2,320,1792]{2,1,0:T(8,128)(2,1)}, u32[]{:S(2)}, u32[]{:S(2)}) collective-permute-start(bf16[2,320,1792]{2,1,0:T(8,128)(2,1)} %pad_maximum_fusion), channel_id=1, source_target_pairs={{0,16},{8,24},{16,0},{24,8},{1,17},{9,25},{17,1},{25,9},{2,18},{10... | collective-permute-start | bytes 6881288 | tf_op jit(solution)/shard_map/ppermute | solution.py:165
  121.9 32.1 %collective-permute-start.10 = (bf16[128,1792]{1,0:T(8,128)(2,1)S(1)}, bf16[128,1792]{1,0:T(8,128)(2,1)}, u32[]{:S(2)}, u32[]{:S(2)}) collective-permute-start(bf16[128,1792]{1,0:T(8,128)(2,1)S(1)} %get-tuple-element.42), channel_id=1, source_target_pairs={{0,4},{1,5},{2,6},{3,7},{4,0},{5,1},{6,2},{7,3},{8,12},{9,13},{10,... | collective-permute-start | bytes 1376264 | tf_op jit(solution)/shard_map/ppermute | solution.py:169
  159.1 51.6 %collective-permute-start.13 = (bf16[8,1040,128]{2,1,0:T(8,128)(2,1)}, bf16[8,1040,128]{2,1,0:T(8,128)(2,1)}, u32[]{:S(2)}, u32[]{:S(2)}) collective-permute-start(bf16[8,1040,128]{2,1,0:T(8,128)(2,1)} %collective-permute-done.4.refs_1_), channel_id=1, source_target_pairs={{2,4},{3,5},{4,6},{5,7},{10,12},{11,13},{12,14},{13,15},{18,20},{1... | collective-permute-start | bytes 6389768 | tf_op jit(solution)/shard_map/ppermute | solution.py:181
  161.1 60.1 %collective-permute-start.14 = (bf16[8,1040,128]{2,1,0:T(8,128)(2,1)}, bf16[8,1040,128]{2,1,0:T(8,128)(2,1)}, u32[]{:S(2)}, u32[]{:S(2)}) collective-permute-start(bf16[8,1040,128]{2,1,0:T(8,128)(2,1)} %collective-permute-done.3.refs_4_), channel_id=1, source_target_pairs={{2,0},{3,1},{4,2},{5,3},{10,8},{11,9},{12,10},{13,11},{18,16},{19,... | collective-permute-start | bytes 6389768 | tf_op jit(solution)/shard_map/ppermute | solution.py:181
  162.4 42.8 %collective-permute-start.16 = (bf16[4,128,1792]{2,1,0:T(8,128)(2,1)}, bf16[4,128,1792]{2,1,0:T(8,128)(2,1)}, u32[]{:S(2)}, u32[]{:S(2)}) collective-permute-start(bf16[4,128,1792]{2,1,0:T(8,128)(2,1)} %pad_maximum_fusion.5), channel_id=1, source_target_pairs={{0,1},{1,0},{2,3},{3,2},{4,5},{5,4},{6,7},{7,6},{8,9},{9,8},{10,11... | collective-permute-start | bytes 5505032 | tf_op jit(solution)/shard_map/ppermute | solution.py:173
  163.8 46.9 %collective-permute-start.15 = (bf16[2,256,1792]{2,1,0:T(8,128)(2,1)}, bf16[2,256,1792]{2,1,0:T(8,128)(2,1)}, u32[]{:S(2)}, u32[]{:S(2)}) collective-permute-start(bf16[2,256,1792]{2,1,0:T(8,128)(2,1)} %pad_maximum_fusion.3), channel_id=1, source_target_pairs={{0,16},{8,24},{16,0},{24,8},{1,17},{9,25},{17,1},{25,9},{2,18},{10... | collective-permute-start | bytes 5505032 | tf_op jit(solution)/shard_map/ppermute | solution.py:165
  174.5 36.2 %collective-permute-start.19 = (bf16[320,1792]{1,0:T(8,128)(2,1)S(1)}, bf16[320,1792]{1,0:T(8,128)(2,1)}, u32[]{:S(2)}, u32[]{:S(2)}) collective-permute-start(bf16[320,1792]{1,0:T(8,128)(2,1)S(1)} %get-tuple-element.78), channel_id=1, source_target_pairs={{0,8},{8,0},{16,24},{24,16},{1,9},{9,1},{17,25},{25,17},{2,10},{10... | collective-permute-start | bytes 3440648 | tf_op jit(solution)/shard_map/ppermute | solution.py:165
  221.2 36.0 %collective-permute-start.22 = (bf16[4,256,1792]{2,1,0:T(8,128)(2,1)}, bf16[4,256,1792]{2,1,0:T(8,128)(2,1)}, u32[]{:S(2)}, u32[]{:S(2)}) collective-permute-start(bf16[4,256,1792]{2,1,0:T(8,128)(2,1)} %constant_dynamic-update-slice_fusion.2.refs_9_), channel_id=1, source_target_pairs={{0,8},{8,0},{16,24},{24,16},{1,9},{9,1},{17,25},{25,17},{2,10},{10... | collective-permute-start | bytes 11010056 | tf_op jit(solution)/shard_map/ppermute | solution.py:165
  230.4 48.8 %collective-permute-start.26 = (bf16[2,256,1792]{2,1,0:T(8,128)(2,1)S(1)}, bf16[2,256,1792]{2,1,0:T(8,128)(2,1)}, u32[]{:S(2)}, u32[]{:S(2)}) collective-permute-start(bf16[2,256,1792]{2,1,0:T(8,128)(2,1)S(1)} %copy-done.5), channel_id=1, source_target_pairs={{0,16},{8,24},{16,0},{24,8},{1,17},{9,25},{17,1},{25,9},{2,18},{10... | collective-permute-start | bytes 5505032 | tf_op jit(solution)/shard_map/ppermute | solution.py:165
  236.8 48.3 %collective-permute-start.23 = (bf16[8,512,128]{2,1,0:T(8,128)(2,1)}, bf16[8,512,128]{2,1,0:T(8,128)(2,1)S(1)}, u32[]{:S(2)}, u32[]{:S(2)}) collective-permute-start(bf16[8,512,128]{2,1,0:T(8,128)(2,1)} %get-tuple-element.81), channel_id=1, source_target_pairs={{4,6},{5,7},{12,14},{13,15},{20,22},{21,23},{28,30},{29,31}} | collective-permute-start | bytes 3145736 | tf_op jit(solution)/shard_map/ppermute | solution.py:181
  237.5 47.5 %collective-permute-start.24 = (bf16[8,512,128]{2,1,0:T(8,128)(2,1)}, bf16[8,512,128]{2,1,0:T(8,128)(2,1)}, u32[]{:S(2)}, u32[]{:S(2)}) collective-permute-start(bf16[8,512,128]{2,1,0:T(8,128)(2,1)} %get-tuple-element.79), channel_id=1, source_target_pairs={{2,0},{3,1},{10,8},{11,9},{18,16},{19,17},{26,24},{27,25}} | collective-permute-start | bytes 3145736 | tf_op jit(solution)/shard_map/ppermute | solution.py:181
  275.0 41.6 %collective-permute-start.30 = (bf16[512,1792]{1,0:T(8,128)(2,1)}, bf16[512,1792]{1,0:T(8,128)(2,1)}, u32[]{:S(2)}, u32[]{:S(2)}) collective-permute-start(bf16[512,1792]{1,0:T(8,128)(2,1)} %shard_map.46.refs_0_), channel_id=1, source_target_pairs={{0,16},{8,24},{16,0},{24,8},{1,17},{9,25},{17,1},{25,9},{2,18},{10... | collective-permute-start | bytes 5505032 | tf_op jit(solution)/shard_map/ppermute | solution.py:165
  316.6 42.7 %collective-permute-start.28 = (bf16[512,1792]{1,0:T(8,128)(2,1)}, bf16[512,1792]{1,0:T(8,128)(2,1)}, u32[]{:S(2)}, u32[]{:S(2)}) collective-permute-start(bf16[512,1792]{1,0:T(8,128)(2,1)} %shard_map.47.refs_4_), channel_id=1, source_target_pairs={{0,16},{8,24},{16,0},{24,8},{1,17},{9,25},{17,1},{25,9},{2,18},{10... | collective-permute-start | bytes 5505032 | tf_op jit(solution)/shard_map/ppermute | solution.py:165
  (21 other events, 347.8 us)

commit v7 on v6

--- a/solution.py
+++ b/solution.py
@@ -9,7 +9,7 @@
 
 F = 7168
 SEQS = 2
-CHUNKS = (3, 5, 4, 4)
+CHUNKS = (1, 5, 5, 5)
 FLAG_ROWS = 16
 COL_TILE = 256
 
@@ -142,6 +142,30 @@
     )(jnp.stack(where).astype(jnp.int32), *pieces, *more)
 
 
+def prepare_kernel(acts_ref, owner_ref, out_ref):
+    share = acts_ref.shape[1]
+    out_ref[0, :share, :] = acts_ref[...].T
+    named = owner_ref[...].astype(jnp.float32).astype(out_ref.dtype)
+    out_ref[0, share:, :] = jnp.broadcast_to(named, (FLAG_ROWS, named.shape[1]))
+
+
+def prepare(acts, owners, copies, spread):
+    tok, features = acts.shape
+    share = features // (copies * spread)
+    return pl.pallas_call(
+        prepare_kernel,
+        out_shape=jax.ShapeDtypeStruct((copies * spread, share + FLAG_ROWS, tok), acts.dtype),
+        grid=(copies * spread,),
+        in_specs=[
+            pl.BlockSpec((tok, share), lambda p: (0, p % spread * copies + p // spread)),
+            pl.BlockSpec((1, tok), lambda p: (0, 0)),
+        ],
+        out_specs=pl.BlockSpec((1, share + FLAG_ROWS, tok), lambda p: (p, 0, 0)),
+        compiler_params=pltpu.CompilerParams(vmem_limit_bytes=16 * 1024 * 1024),
+        cost_estimate=pl.CostEstimate(flops=0, bytes_accessed=4 * acts.size, transcendentals=0),
+    )(acts, owners)
+
+
 def after(value, *others):
     return lax.optimization_barrier((value, *others))[0]
 
@@ -197,9 +221,7 @@
 
     cut = cut_blocks(out_grads[0])
     grad_near = spread_blocks(cut)
-    acts = after(activations[0], *cut).T.reshape(spread, copies, share, tok).transpose(1, 0, 2, 3)
-    named = jnp.broadcast_to(seq_ids[0].astype(acts.dtype), acts.shape[:2] + (FLAG_ROWS, tok))
-    acts = jnp.concatenate([acts, named], axis=2).reshape(copies * spread, share + FLAG_ROWS, tok)
+    acts = prepare(after(activations[0], *cut), seq_ids, copies, spread)
     grad_far = to_copy(after(out_grads[0], acts), 2)
     planes = [
         [c * devices + block * spread + s for c in range(copies) for s in range(spread)] for block in range(blocks)
@@ -233,7 +255,7 @@
     grad_far = spread_blocks([after(block, *stage) for block in cut])
     grads[1] = mate(grads[0], *stage)
 
-    stage = (grad_far, grads[1])
+    stage = (grad_far, grads[1], weight_far[1])
     low.append(along(after(low[0], *stage), 2, 1))
     high.append(along(after(high[0], *stage), 2, -1))
     send_weights(2, *early)

time: 366 us -> 355 us (0.970)
  local copies, waits for them, and re-layouts: 61.9 us -> 52.5 us
  Pallas kernels: 47.2 us -> 51 us
    ppermute x8, waiting for transfers between devices: 28.8 us -> 17.9 us  [along(): return lax.ppermute(value, 'fsdp', pairs)]
    ppermute x2, waiting for transfers between devices: 32.3 us -> 42.8 us  [to_half(): return lax.ppermute(value, 'fsdp', pairs)]
    reshape x2 -> x0, local copies, waits for them, and re-layouts: 6.19 us -> none  [per_device(): after(activations[0], *cut).T.reshape(spread, copies, share, tok)]
    ppermute x18, waiting for transfers between devices: 103 us -> 97.4 us  [to_copy(): return lax.ppermute(value, 'mp', [(s, s ^ flip) for s in range(copies)])]
    ppermute x6, waiting for transfers between devices: 35.2 us -> 39.5 us  [to_block(): return lax.ppermute(value, 'fsdp', pairs)]
    dynamic_slice x3 -> x2, local copies, waits for them, and re-layouts: 9.93 us -> 9.46 us  [weight_rows(): lax.dynamic_slice_in_dim(weights[0], owner * share + starts[k], sizes[k], 0)]
    unnamed x22 -> x38, local copies, waits for them, and re-layouts: 8.17 us -> 8.38 us
  transfers between devices with their start and end apart: 35 -> 35, of which waited for: 15 -> 18; matrix products, arithmetic and copies ran while one was open for 19% -> 16% of each run, Pallas kernels for 13% -> 14%
where the time goes in v7:
time: 355 us; the launch traced here: 354 us
  waiting for transfers between devices  198 us (56%)
  local copies, waits for them, and re-layouts  52.5 us (15%)
  Pallas kernels  51 us (14%)
  starting transfers between devices  40.1 us (11%)
  other arithmetic  12.4 us (3%)
    ppermute x18, waiting for transfers between devices, to_copy(): return lax.ppermute(value, 'mp', [(s, s ^ flip) for s in range(copies)])  97.4 us
    ppermute x2, waiting for transfers between devices, to_half(): return lax.ppermute(value, 'fsdp', pairs)  42.8 us
    ppermute x6, waiting for transfers between devices, to_block(): return lax.ppermute(value, 'fsdp', pairs)  39.5 us
    pallas_call x2, Pallas kernels, merge_rows(): pl.pallas_call(functools.partial(merge_kernel, copies, shards, starts, si...  36.1 us
    ppermute x8, waiting for transfers between devices, along(): return lax.ppermute(value, 'fsdp', pairs)  17.9 us
    ppermute x8, starting transfers between devices, along(): return lax.ppermute(value, 'fsdp', pairs)  14 us
    pallas_call x3, Pallas kernels, place_rows(): pl.pallas_call(functools.partial(place_kernel, count), out_shape=shape, g...  11.4 us
    ppermute x6, starting transfers between devices, to_block(): return lax.ppermute(value, 'fsdp', pairs)  9.89 us
  transfers between devices with their start and end apart: 35, of which 18 were waited for; matrix products, arithmetic and copies ran while one was open for 16% of the time, Pallas kernels for 14%

profile of v7, /device:TPU:0, one launch (start us, length us, event | category | flops | bytes accessed | tf_op | source)
XLA Modules:
  0.0 354.0 jit_solution(11724852895135198751)
XLA Ops:
  2.9 5.0 %collective-permute-start.2 = (bf16[128,1792]{1,0:T(8,128)(2,1)}, bf16[128,1792]{1,0:T(8,128)(2,1)}, u32[]{:S(2)}, u32[]{:S(2)}) collective-permute-start(bf16[128,1792]{1,0:T(8,128)(2,1)} %get-tuple-element.89), channel_id=1, source_target_pairs={{0,6},{1,7},{2,0},{3,1},{4,2},{5,3},{6,4},{7,5},{8,14},{9,15},{10,... | collective-permute-start | bytes 1376264 | tf_op jit(solution)/shard_map/ppermute | solution.py:193
  9.0 3.6 %shard_map.46 = bf16[8,1040,128]{2,1,0:T(8,128)(2,1)} custom-call(bf16[128,8192]{1,0:T(8,128)(2,1)S(1)} %bitcast.54, s32[1,128]{1,0:T(1,128)S(1)} %copy-done.3), custom_call_target="tpu_custom_call" | custom-call | bytes 4194304 | tf_op jit(solution)/shard_map/pallas_call | solution.py:155
  12.6 3.7 %all-to-all-start = ((bf16[8,1040,128]{2,1,0:T(8,128)(2,1)}), bf16[8,1040,128]{2,1,0:T(8,128)(2,1)S(1)}, u32[]{:S(2)}, u32[]{:S(2)}) async-start(bf16[8,1040,128]{2,1,0:T(8,128)(2,1)} %shard_map.46), calls=%async_computation | async-start | bytes 4259840 | tf_op jit(solution)/shard_map/all_to_all | solution.py:229
  18.3 4.1 %dynamic-slice_bitcast_fusion = bf16[1024,1792]{1,0:T(8,128)(2,1)} fusion(bf16[1,4096,1792]{2,1,0:T(8,128)(2,1)} %param.7, s32[]{:T(128)S(6)} %select_n.185), kind=kLoop, calls=%fused_computation.1 | loop fusion | bytes 7340036 | tf_op jit(solution)/shard_map/dynamic_slice | solution.py:232
  22.4 7.5 %dynamic-slice_bitcast_fusion.3 = (bf16[320,1792]{1,0:T(8,128)(2,1)}, bf16[320,1792]{1,0:T(8,128)(2,1)}, bf16[1,320,1792]{2,1,0:T(8,128)(2,1)S(1)}, bf16[1,320,1...) fusion(bf16[1,4096,1792]{2,1,0:T(8,128)(2,1)} %param.7, ...), kind=kLoop, calls=%fused_computation.9 | loop fusion | bytes 20643876 | tf_op jit(solution)/shard_map/dynamic_slice | solution.py:217
  29.9 3.4 pad_maximum_fusion.1
  37.8 9.6 %collective-permute-done.1 = bf16[128,1792]{1,0:T(8,128)(2,1)} collective-permute-done((bf16[128,1792]{1,0:T(8,128)(2,1)}, bf16[128,1792]{1,0:T(8,128)(2,1)}, u32[]{:S(2)}, u32[]{:S(2)}) %collective-permute-start.1) | collective-permute-done | bytes 458784 | tf_op jit(solution)/shard_map/ppermute | solution.py:193
  50.2 4.4 %collective-permute-start.4 = (bf16[8,1040,128]{2,1,0:T(8,128)(2,1)S(1)}, bf16[8,1040,128]{2,1,0:T(8,128)(2,1)}, u32[]{:S(2)}, u32[]{:S(2)}) collective-permute-start(bf16[8,1040,128]{2,1,0:T(8,128)(2,1)S(1)} %all-to-all-done.refs_0_), channel_id=1, source_target_pairs={{0,2},{1,3},{2,4},{3,5},{4,6},{5,7},{8,10},{9,11},{10,12},{11,13},... | collective-permute-start | bytes 6389768 | tf_op jit(solution)/shard_map/ppermute | solution.py:205
  57.5 24.3 %collective-permute-done.5 = bf16[128,7168]{1,0:T(8,128)(2,1)} collective-permute-done((bf16[128,7168]{1,0:T(8,128)(2,1)}, bf16[128,7168]{1,0:T(8,128)(2,1)}, u32[]{:S(2)}, u32[]{:S(2)}) %collective-permute-start.5) | collective-permute-done | bytes 1835040 | tf_op jit(solution)/shard_map/ppermute | solution.py:189
  84.0 13.1 %collective-permute-done.6 = bf16[4,128,1792]{2,1,0:T(8,128)(2,1)S(1)} collective-permute-done((bf16[4,128,1792]{2,1,0:T(8,128)(2,1)}, bf16[4,128,1792]{2,1,0:T(8,128)(2,1)S(1)}, u32[]{:S(2)}, u32[]{:S(2)}) %collective-permute-start.6) | collective-permute-done | bytes 1835040 | tf_op jit(solution)/shard_map/ppermute | solution.py:197
  98.3 5.5 %collective-permute-done.3.refs_4_ = bf16[8,1040,128]{2,1,0:T(8,128)(2,1)} collective-permute-done((bf16[8,1040,128]{2,1,0:T(8,128)(2,1)S(1)}, bf16[8,1040,128]{2,1,0:T(8,128)(2,1)}, u32[]{:S(2)}, u32[]{:S(2)}) %collective-permute-start.3) | collective-permute-done | bytes 2129952 | tf_op jit(solution)/shard_map/ppermute | solution.py:205
  109.1 11.5 %collective-permute-done.9 = bf16[128,1792]{1,0:T(8,128)(2,1)S(1)} collective-permute-done((bf16[128,1792]{1,0:T(8,128)(2,1)S(1)}, bf16[128,1792]{1,0:T(8,128)(2,1)S(1)}, u32[]{:S(2)}, u32[]{:S(2)}) %collective-permute-start.9) | collective-permute-done | bytes 458784 | tf_op jit(solution)/shard_map/ppermute | solution.py:193
  121.1 18.4 %collective-permute-done.10 = bf16[128,1792]{1,0:T(8,128)(2,1)S(1)} collective-permute-done((bf16[128,1792]{1,0:T(8,128)(2,1)S(1)}, bf16[128,1792]{1,0:T(8,128)(2,1)S(1)}, u32[]{:S(2)}, u32[]{:S(2)}) %collective-permute-start.10) | collective-permute-done | bytes 458784 | tf_op jit(solution)/shard_map/ppermute | solution.py:193
  141.1 15.4 %collective-permute-done.13 = bf16[2,320,1792]{2,1,0:T(8,128)(2,1)S(1)} collective-permute-done((bf16[2,320,1792]{2,1,0:T(8,128)(2,1)S(1)}, bf16[2,320,1792]{2,1,0:T(8,128)(2,1)S(1)}, u32[]{:S(2)}, u32[]{:S(2)}) %collective-permute-start.13) | collective-permute-done | bytes 2293792 | tf_op jit(solution)/shard_map/ppermute | solution.py:189
  173.5 29.7 %collective-permute-done.17 = bf16[4,128,1792]{2,1,0:T(8,128)(2,1)} collective-permute-done((bf16[4,128,1792]{2,1,0:T(8,128)(2,1)}, bf16[4,128,1792]{2,1,0:T(8,128)(2,1)}, u32[]{:S(2)}, u32[]{:S(2)}) %collective-permute-start.17) | collective-permute-done | bytes 1835040 | tf_op jit(solution)/shard_map/ppermute | solution.py:197
  206.1 4.6 %collective-permute-done.15.refs_5_ = bf16[8,1040,128]{2,1,0:T(8,128)(2,1)} collective-permute-done((bf16[8,1040,128]{2,1,0:T(8,128)(2,1)}, bf16[8,1040,128]{2,1,0:T(8,128)(2,1)}, u32[]{:S(2)}, u32[]{:S(2)}) %collective-permute-start.15) | collective-permute-done | bytes 2129952 | tf_op jit(solution)/shard_map/ppermute | solution.py:205
  219.0 3.8 %fusion.3 = (bf16[320,1792]{1,0:T(8,128)(2,1)}, bf16[320,1792]{1,0:T(8,128)(2,1)}, bf16[320,1792]{1,0:T(8,128)(2,1)}) fusion(bf16[1024,1792]{1,0:T(8,128)(2,1)} %collective-permute-done.7), kind=kLoop, calls=%fused_computation.52 | loop fusion | bytes 6881280 | tf_op jit(solution)/shard_map/slice | solution.py:285
  229.1 6.7 %collective-permute-done.21.refs_6_ = bf16[8,384,128]{2,1,0:T(8,128)(2,1)S(1)} collective-permute-done((bf16[8,384,128]{2,1,0:T(8,128)(2,1)S(1)}, bf16[8,384,128]{2,1,0:T(8,128)(2,1)S(1)}, u32[]{:S(2)}, u32[]{:S(2)}) %collective-permute-start.21) | collective-permute-done | bytes 786464 | tf_op jit(solution)/shard_map/ppermute | solution.py:205
  238.4 16.4 %shard_map.47.refs_0_ = bf16[384,1792]{1,0:T(8,128)(2,1)} custom-call(s32[3]{0:T(128)} %pad_add_fusion.place_ref, s32[4]{0:T(128)} %and_select_fusion.slot_ref, bf16[8,1040,128]{2,1,0:T(8,128)(2,1)} %copy-done.5, bf16[8,1040,128]{2,1,0:T(8,128)(2,1)} %collective-permute-done.4.refs_1_, bf16[8,1040,128]{2,1,0:T(8,128)(2,1)} %collective-permute-done.14.refs_2_, ...), custom_call_target="tpu_custom_call" | custom-call | flops 5637144576 | bytes 14680064 | tf_op jit(solution)/shard_map/pallas_call | solution.py:84
  257.9 5.4 %collective-permute-done.26 = bf16[2,320,1792]{2,1,0:T(8,128)(2,1)} collective-permute-done((bf16[2,320,1792]{2,1,0:T(8,128)(2,1)}, bf16[2,320,1792]{2,1,0:T(8,128)(2,1)}, u32[]{:S(2)}, u32[]{:S(2)}) %collective-permute-start.26) | collective-permute-done | bytes 2293792 | tf_op jit(solution)/shard_map/ppermute | solution.py:189
  269.9 19.7 %shard_map.48.refs_4_ = bf16[640,1792]{1,0:T(8,128)(2,1)} custom-call(s32[3]{0:T(128)} %pad_add_fusion.place_ref, s32[4]{0:T(128)} %and_select_fusion.slot_ref, bf16[8,1040,128]{2,1,0:T(8,128)(2,1)} %copy-done.5, bf16[8,1040,128]{2,1,0:T(8,128)(2,1)} %collective-permute-done.4.refs_1_, bf16[8,1040,128]{2,1,0:T(8,128)(2,1)} %collective-permute-done.14.refs_2_, ...), custom_call_target="tpu_custom_call" | custom-call | flops 9395240960 | bytes 14680064 | tf_op jit(solution)/shard_map/pallas_call | solution.py:84
  291.4 7.7 %collective-permute-done.30.refs_2_ = bf16[384,1792]{1,0:T(8,128)(2,1)S(1)} collective-permute-done((bf16[384,1792]{1,0:T(8,128)(2,1)S(1)}, bf16[384,1792]{1,0:T(8,128)(2,1)S(1)}, u32[]{:S(2)}, u32[]{:S(2)}) %collective-permute-start.30) | collective-permute-done | bytes 1376288 | tf_op jit(solution)/shard_map/ppermute | solution.py:189
  304.0 7.0 %shard_map.49.refs_1_ = bf16[4096,1792]{1,0:T(8,128)(2,1)} custom-call(s32[6]{0:T(128)S(1)} %stack.111.where_ref, bf16[384,1792]{1,0:T(8,128)(2,1)S(1)} %copy-done.1, bf16[384,1792]{1,0:T(8,128)(2,1)} %collective-permute-done.29.refs_1_, bf16[384,1792]{1,0:T(8,128)(2,1)S(1)} %collective-permute-done.30.refs_2_, ...), custom_call_target="tpu_custom_call" | custom-call | bytes 20185088 | tf_op jit(solution)/shard_map/pallas_call | solution.py:126
  311.0 37.0 %collective-permute-done.28.refs_0_ = bf16[640,1792]{1,0:T(8,128)(2,1)} collective-permute-done((bf16[640,1792]{1,0:T(8,128)(2,1)}, bf16[640,1792]{1,0:T(8,128)(2,1)}, u32[]{:S(2)}, u32[]{:S(2)}) %collective-permute-start.28) | collective-permute-done | bytes 2293792 | tf_op jit(solution)/shard_map/ppermute | solution.py:189
  (121 shorter events, 86.1 us)
Async XLA Ops:
  2.9 34.9 %collective-permute-start.2 = (bf16[128,1792]{1,0:T(8,128)(2,1)}, bf16[128,1792]{1,0:T(8,128)(2,1)}, u32[]{:S(2)}, u32[]{:S(2)}) collective-permute-start(bf16[128,1792]{1,0:T(8,128)(2,1)} %get-tuple-element.89), channel_id=1, source_target_pairs={{0,6},{1,7},{2,0},{3,1},{4,2},{5,3},{6,4},{7,5},{8,14},{9,15},{10,... | collective-permute-start | bytes 1376264 | tf_op jit(solution)/shard_map/ppermute | solution.py:193
  8.0 39.5 %collective-permute-start.1 = (bf16[128,1792]{1,0:T(8,128)(2,1)}, bf16[128,1792]{1,0:T(8,128)(2,1)}, u32[]{:S(2)}, u32[]{:S(2)}) collective-permute-start(bf16[128,1792]{1,0:T(8,128)(2,1)} %get-tuple-element.90), channel_id=1, source_target_pairs={{0,4},{1,5},{2,6},{3,7},{4,0},{5,1},{6,2},{7,3},{8,12},{9,13},{10,... | collective-permute-start | bytes 1376264 | tf_op jit(solution)/shard_map/ppermute | solution.py:193
  8.0 39.5 %collective-permute-start = (bf16[128,1792]{1,0:T(8,128)(2,1)}, bf16[128,1792]{1,0:T(8,128)(2,1)}, u32[]{:S(2)}, u32[]{:S(2)}) collective-permute-start(bf16[128,1792]{1,0:T(8,128)(2,1)} %get-tuple-element.91), channel_id=1, source_target_pairs={{0,2},{1,3},{2,4},{3,5},{4,6},{5,7},{6,0},{7,1},{8,10},{9,11},{10,... | collective-permute-start | bytes 1376264 | tf_op jit(solution)/shard_map/ppermute | solution.py:193
  12.6 37.7 %all-to-all-start = ((bf16[8,1040,128]{2,1,0:T(8,128)(2,1)}), bf16[8,1040,128]{2,1,0:T(8,128)(2,1)S(1)}, u32[]{:S(2)}, u32[]{:S(2)}) async-start(bf16[8,1040,128]{2,1,0:T(8,128)(2,1)} %shard_map.46), calls=%async_computation | async-start | bytes 4259840 | tf_op jit(solution)/shard_map/all_to_all | solution.py:229
  16.3 65.6 %collective-permute-start.5 = (bf16[128,7168]{1,0:T(8,128)(2,1)}, bf16[128,7168]{1,0:T(8,128)(2,1)}, u32[]{:S(2)}, u32[]{:S(2)}) collective-permute-start(bf16[128,7168]{1,0:T(8,128)(2,1)} %bitcast.56), channel_id=1, source_target_pairs={{0,16},{8,24},{16,0},{24,8},{1,17},{9,25},{17,1},{25,9},{2,18},{10... | collective-permute-start | bytes 5505032 | tf_op jit(solution)/shard_map/ppermute | solution.py:189
  22.4 74.8 %collective-permute-start.7 = (bf16[1024,1792]{1,0:T(8,128)(2,1)}, bf16[1024,1792]{1,0:T(8,128)(2,1)}, u32[]{:S(2)}, u32[]{:S(2)}) collective-permute-start(bf16[1024,1792]{1,0:T(8,128)(2,1)} %dynamic-slice_bitcast_fusion), channel_id=1, source_target_pairs={{0,8},{8,0},{16,24},{24,16},{1,9},{9,1},{17,25},{25,17},{2,10},{10... | collective-permute-start | bytes 11010056 | tf_op jit(solution)/shard_map/ppermute | solution.py:189
  50.2 48.0 %collective-permute-start.4 = (bf16[8,1040,128]{2,1,0:T(8,128)(2,1)S(1)}, bf16[8,1040,128]{2,1,0:T(8,128)(2,1)}, u32[]{:S(2)}, u32[]{:S(2)}) collective-permute-start(bf16[8,1040,128]{2,1,0:T(8,128)(2,1)S(1)} %all-to-all-done.refs_0_), channel_id=1, source_target_pairs={{0,2},{1,3},{2,4},{3,5},{4,6},{5,7},{8,10},{9,11},{10,12},{11,13},... | collective-permute-start | bytes 6389768 | tf_op jit(solution)/shard_map/ppermute | solution.py:205
  54.6 49.2 %collective-permute-start.3 = (bf16[8,1040,128]{2,1,0:T(8,128)(2,1)S(1)}, bf16[8,1040,128]{2,1,0:T(8,128)(2,1)}, u32[]{:S(2)}, u32[]{:S(2)}) collective-permute-start(bf16[8,1040,128]{2,1,0:T(8,128)(2,1)S(1)} %all-to-all-done.refs_0_), channel_id=1, source_target_pairs={{2,0},{3,1},{4,2},{5,3},{6,4},{7,5},{10,8},{11,9},{12,10},{13,11},... | collective-permute-start | bytes 6389768 | tf_op jit(solution)/shard_map/ppermute | solution.py:205
  55.9 41.1 %collective-permute-start.6 = (bf16[4,128,1792]{2,1,0:T(8,128)(2,1)}, bf16[4,128,1792]{2,1,0:T(8,128)(2,1)S(1)}, u32[]{:S(2)}, u32[]{:S(2)}) collective-permute-start(bf16[4,128,1792]{2,1,0:T(8,128)(2,1)} %pad_maximum_fusion.3), channel_id=1, source_target_pairs={{0,1},{1,0},{2,3},{3,2},{4,5},{5,4},{6,7},{7,6},{8,9},{9,8},{10,11... | collective-permute-start | bytes 5505032 | tf_op jit(solution)/shard_map/ppermute | solution.py:197
  103.8 52.7 %collective-permute-start.12 = (bf16[4,256,1792]{2,1,0:T(8,128)(2,1)S(1)}, bf16[4,256,1792]{2,1,0:T(8,128)(2,1)S(1)}, u32[]{:S(2)}, u32[]{:S(2)}) collective-permute-start(bf16[4,256,1792]{2,1,0:T(8,128)(2,1)S(1)} %constant_dynamic-update-slice_fusion.refs_7_), channel_id=1, source_target_pairs={{0,8},{8,0},{16,24},{24,16},{1,9},{9,1},{17,25},{25,17},{2,10},{10... | collective-permute-start | bytes 11010056 | tf_op jit(solution)/shard_map/ppermute | solution.py:189
  103.8 52.6 %collective-permute-start.13 = (bf16[2,320,1792]{2,1,0:T(8,128)(2,1)S(1)}, bf16[2,320,1792]{2,1,0:T(8,128)(2,1)S(1)}, u32[]{:S(2)}, u32[]{:S(2)}) collective-permute-start(bf16[2,320,1792]{2,1,0:T(8,128)(2,1)S(1)} %copy-done.11), channel_id=1, source_target_pairs={{0,16},{8,24},{16,0},{24,8},{1,17},{9,25},{17,1},{25,9},{2,18},{10... | collective-permute-start | bytes 6881288 | tf_op jit(solution)/shard_map/ppermute | solution.py:189
  106.5 33.1 %collective-permute-start.10 = (bf16[128,1792]{1,0:T(8,128)(2,1)S(1)}, bf16[128,1792]{1,0:T(8,128)(2,1)S(1)}, u32[]{:S(2)}, u32[]{:S(2)}) collective-permute-start(bf16[128,1792]{1,0:T(8,128)(2,1)S(1)} %get-tuple-element.42), channel_id=1, source_target_pairs={{0,4},{1,5},{2,6},{3,7},{4,0},{5,1},{6,2},{7,3},{8,12},{9,13},{10,... | collective-permute-start | bytes 1376264 | tf_op jit(solution)/shard_map/ppermute | solution.py:193
  106.5 33.1 %collective-permute-start.11 = (bf16[128,1792]{1,0:T(8,128)(2,1)S(1)}, bf16[128,1792]{1,0:T(8,128)(2,1)S(1)}, u32[]{:S(2)}, u32[]{:S(2)}) collective-permute-start(bf16[128,1792]{1,0:T(8,128)(2,1)S(1)} %get-tuple-element.43), channel_id=1, source_target_pairs={{0,6},{1,7},{2,0},{3,1},{4,2},{5,3},{6,4},{7,5},{8,14},{9,15},{10,... | collective-permute-start | bytes 1376264 | tf_op jit(solution)/shard_map/ppermute | solution.py:193
  120.6 85.5 %collective-permute-start.16 = (bf16[2,320,1792]{2,1,0:T(8,128)(2,1)}, bf16[2,320,1792]{2,1,0:T(8,128)(2,1)}, u32[]{:S(2)}, u32[]{:S(2)}) collective-permute-start(bf16[2,320,1792]{2,1,0:T(8,128)(2,1)} %pad_maximum_fusion.1), channel_id=1, source_target_pairs={{0,16},{8,24},{16,0},{24,8},{1,17},{9,25},{17,1},{25,9},{2,18},{10... | collective-permute-start | bytes 6881288 | tf_op jit(solution)/shard_map/ppermute | solution.py:189
  158.3 47.8 %collective-permute-start.14 = (bf16[8,1040,128]{2,1,0:T(8,128)(2,1)}, bf16[8,1040,128]{2,1,0:T(8,128)(2,1)}, u32[]{:S(2)}, u32[]{:S(2)}) collective-permute-start(bf16[8,1040,128]{2,1,0:T(8,128)(2,1)} %collective-permute-done.4.refs_1_), channel_id=1, source_target_pairs={{2,4},{3,5},{4,6},{5,7},{10,12},{11,13},{12,14},{13,15},{18,20},{1... | collective-permute-start | bytes 6389768 | tf_op jit(solution)/shard_map/ppermute | solution.py:205
  160.3 50.5 %collective-permute-start.15 = (bf16[8,1040,128]{2,1,0:T(8,128)(2,1)}, bf16[8,1040,128]{2,1,0:T(8,128)(2,1)}, u32[]{:S(2)}, u32[]{:S(2)}) collective-permute-start(bf16[8,1040,128]{2,1,0:T(8,128)(2,1)} %collective-permute-done.3.refs_4_), channel_id=1, source_target_pairs={{2,0},{3,1},{4,2},{5,3},{10,8},{11,9},{12,10},{13,11},{18,16},{19,... | collective-permute-start | bytes 6389768 | tf_op jit(solution)/shard_map/ppermute | solution.py:205
  161.6 41.6 %collective-permute-start.17 = (bf16[4,128,1792]{2,1,0:T(8,128)(2,1)}, bf16[4,128,1792]{2,1,0:T(8,128)(2,1)}, u32[]{:S(2)}, u32[]{:S(2)}) collective-permute-start(bf16[4,128,1792]{2,1,0:T(8,128)(2,1)} %pad_maximum_fusion.4), channel_id=1, source_target_pairs={{0,1},{1,0},{2,3},{3,2},{4,5},{5,4},{6,7},{7,6},{8,9},{9,8},{10,11... | collective-permute-start | bytes 5505032 | tf_op jit(solution)/shard_map/ppermute | solution.py:197
  168.3 37.8 %collective-permute-start.19 = (bf16[320,1792]{1,0:T(8,128)(2,1)S(1)}, bf16[320,1792]{1,0:T(8,128)(2,1)}, u32[]{:S(2)}, u32[]{:S(2)}) collective-permute-start(bf16[320,1792]{1,0:T(8,128)(2,1)S(1)} %get-tuple-element.83), channel_id=1, source_target_pairs={{0,8},{8,0},{16,24},{24,16},{1,9},{9,1},{17,25},{25,17},{2,10},{10... | collective-permute-start | bytes 3440648 | tf_op jit(solution)/shard_map/ppermute | solution.py:189
  210.8 26.7 %collective-permute-start.22 = (bf16[4,256,1792]{2,1,0:T(8,128)(2,1)}, bf16[4,256,1792]{2,1,0:T(8,128)(2,1)}, u32[]{:S(2)}, u32[]{:S(2)}) collective-permute-start(bf16[4,256,1792]{2,1,0:T(8,128)(2,1)} %constant_dynamic-update-slice_fusion.2.refs_9_), channel_id=1, source_target_pairs={{0,8},{8,0},{16,24},{24,16},{1,9},{9,1},{17,25},{25,17},{2,10},{10... | collective-permute-start | bytes 11010056 | tf_op jit(solution)/shard_map/ppermute | solution.py:189
  210.8 52.6 %collective-permute-start.26 = (bf16[2,320,1792]{2,1,0:T(8,128)(2,1)}, bf16[2,320,1792]{2,1,0:T(8,128)(2,1)}, u32[]{:S(2)}, u32[]{:S(2)}) collective-permute-start(bf16[2,320,1792]{2,1,0:T(8,128)(2,1)} %get-tuple-element.58), channel_id=1, source_target_pairs={{0,16},{8,24},{16,0},{24,8},{1,17},{9,25},{17,1},{25,9},{2,18},{10... | collective-permute-start | bytes 6881288 | tf_op jit(solution)/shard_map/ppermute | solution.py:189
  227.8 39.9 %collective-permute-start.24 = (bf16[8,640,128]{2,1,0:T(8,128)(2,1)}, bf16[8,640,128]{2,1,0:T(8,128)(2,1)}, u32[]{:S(2)}, u32[]{:S(2)}) collective-permute-start(bf16[8,640,128]{2,1,0:T(8,128)(2,1)} %slice.45), channel_id=1, source_target_pairs={{2,0},{3,1},{10,8},{11,9},{18,16},{19,17},{26,24},{27,25}} | collective-permute-start | bytes 3932168 | tf_op jit(solution)/shard_map/ppermute | solution.py:205
  235.8 31.9 %collective-permute-start.23 = (bf16[8,640,128]{2,1,0:T(8,128)(2,1)}, bf16[8,640,128]{2,1,0:T(8,128)(2,1)}, u32[]{:S(2)}, u32[]{:S(2)}) collective-permute-start(bf16[8,640,128]{2,1,0:T(8,128)(2,1)} %slice.44), channel_id=1, source_target_pairs={{4,6},{5,7},{12,14},{13,15},{20,22},{21,23},{28,30},{29,31}} | collective-permute-start | bytes 3932168 | tf_op jit(solution)/shard_map/ppermute | solution.py:205
  266.1 33.0 %collective-permute-start.30 = (bf16[384,1792]{1,0:T(8,128)(2,1)S(1)}, bf16[384,1792]{1,0:T(8,128)(2,1)S(1)}, u32[]{:S(2)}, u32[]{:S(2)}) collective-permute-start(bf16[384,1792]{1,0:T(8,128)(2,1)S(1)} %copy-done.1), channel_id=1, source_target_pairs={{0,16},{8,24},{16,0},{24,8},{1,17},{9,25},{17,1},{25,9},{2,18},{10... | collective-permute-start | bytes 4128776 | tf_op jit(solution)/shard_map/ppermute | solution.py:189
  289.8 58.2 %collective-permute-start.28 = (bf16[640,1792]{1,0:T(8,128)(2,1)}, bf16[640,1792]{1,0:T(8,128)(2,1)}, u32[]{:S(2)}, u32[]{:S(2)}) collective-permute-start(bf16[640,1792]{1,0:T(8,128)(2,1)} %shard_map.48.refs_4_), channel_id=1, source_target_pairs={{0,16},{8,24},{16,0},{24,8},{1,17},{9,25},{17,1},{25,9},{2,18},{10... | collective-permute-start | bytes 6881288 | tf_op jit(solution)/shard_map/ppermute | solution.py:189
  (29 other events, 392.9 us)

commit v8 on v7

--- a/solution.py
+++ b/solution.py
@@ -9,7 +9,7 @@
 
 F = 7168
 SEQS = 2
-CHUNKS = (1, 5, 5, 5)
+CHUNKS = (2, 5, 5, 4)
 FLAG_ROWS = 16
 COL_TILE = 256
 
@@ -208,10 +208,10 @@
         return [lax.dynamic_slice_in_dim(value, (a + k) % blocks * width, width, 1) for k in range(blocks)]
 
     def spread_blocks(cut):
-        return jnp.stack([cut[0]] + [to_block(cut[k], k) for k in range(1, blocks)])
+        return [cut[0]] + [to_block(cut[k], k) for k in range(1, blocks)]
 
     def over_halves(value):
-        return jnp.concatenate([value] + [to_half(value, d) for d in range(1, spread)], axis=1)
+        return [value] + [to_half(value, d) for d in range(1, spread)]
 
     def weight_rows(owner, k):
         return lax.dynamic_slice_in_dim(weights[0], owner * share + starts[k], sizes[k], 0)
@@ -242,25 +242,27 @@
         weight_mate[k] = to_copy(lax.dynamic_index_in_dim(weight_far[k], other, 0, keepdims=False), 1)
 
     grads = [None] * copies
-    stage = (own, grad_near, *leaving)
+    stage = (own, *grad_near, *leaving)
     early = stage
     low, high = [along(after(own, *stage), 1, 1)], [along(after(own, *stage), 1, -1)]
     send_weights(0, *stage, grad_far)
-    grads[0] = over_halves(after(grad_near, *stage))
+    halves = over_halves(after(jnp.stack(grad_near), *stage))
+    grads[0] = jnp.concatenate(halves, axis=1)
 
     send_weights(1, *early)
     cut = cut_blocks(grad_far)
-    stage = (low[0], high[0], grads[0], mate_rows, weight_far[0], *cut)
+    stage = (low[0], high[0], *halves, mate_rows, weight_far[0], *cut)
     early = stage
     grad_far = spread_blocks([after(block, *stage) for block in cut])
     grads[1] = mate(grads[0], *stage)
 
-    stage = (grad_far, grads[1], weight_far[1])
+    stage = (*grad_far, grads[1], weight_far[1])
     low.append(along(after(low[0], *stage), 2, 1))
     high.append(along(after(high[0], *stage), 2, -1))
     send_weights(2, *early)
     early = stage
-    grads[2] = over_halves(after(grad_far, *stage))
+    halves = over_halves(after(jnp.stack(grad_far), *stage))
+    grads[2] = jnp.concatenate(halves, axis=1)
     cores(0, *stage)
     cores(1, weight_mate[0])
     named = jnp.where(a == 0, high[0][:, share, 0], jnp.where(a == blocks - 1, low[0][:, share, 0], own[:, share, 0]))
@@ -268,7 +270,7 @@
     slots = ((a - alone) % blocks).astype(jnp.int32)
     place = jnp.stack([a, m, h]).astype(jnp.int32)
 
-    stage = (low[1], high[1], weight_far[2], grads[1], grads[2], weight_mate[1], slots)
+    stage = (low[1], high[1], weight_far[2], grads[1], *halves, weight_mate[1], slots)
     half = starts[2]
     grads[3] = mate(grads[2], *stage)
     low_last = [along(after(low[1], *stage)[:, :half], 3, 1)]

time: 355 us -> 355 us (level)
  local copies, waits for them, and re-layouts: 52.5 us -> 58.8 us
  waiting for transfers between devices: 198 us -> 194 us
    ppermute x18, waiting for transfers between devices: 97.4 us -> 107 us  [to_copy(): return lax.ppermute(value, 'mp', [(s, s ^ flip) for s in range(copies)])]
    ppermute x2, waiting for transfers between devices: 42.8 us -> 33.5 us  [to_half(): return lax.ppermute(value, 'fsdp', pairs)]
    slice x2 -> x3, local copies, waits for them, and re-layouts: 5.42 us -> 7.15 us  [sums(): mate_rows[starts[k]:starts[k] + sizes[k]]]
    unnamed x38 -> x22, local copies, waits for them, and re-layouts: 8.38 us -> 9.46 us
    dynamic_slice x2 -> x3, local copies, waits for them, and re-layouts: 9.46 us -> 9.86 us  [weight_rows(): lax.dynamic_slice_in_dim(weights[0], owner * share + starts[k], sizes[k], 0)]
  transfers between devices with their start and end apart: 35 -> 35, of which waited for: 18 -> 16; matrix products, arithmetic and copies ran while one was open for 16% -> 18% of each run, Pallas kernels for 14% -> 14%
where the time goes in v8:
time: 355 us; the launch traced here: 354 us
  waiting for transfers between devices  194 us (55%)
  local copies, waits for them, and re-layouts  58.8 us (17%)
  Pallas kernels  50 us (14%)
  starting transfers between devices  39.1 us (11%)
  other arithmetic  11.9 us (3%)
    ppermute x18, waiting for transfers between devices, to_copy(): return lax.ppermute(value, 'mp', [(s, s ^ flip) for s in range(copies)])  107 us
    ppermute x6, waiting for transfers between devices, to_block(): return lax.ppermute(value, 'fsdp', pairs)  37.7 us
    pallas_call x2, Pallas kernels, merge_rows(): pl.pallas_call(functools.partial(merge_kernel, copies, shards, starts, si...  35.1 us
    ppermute x2, waiting for transfers between devices, to_half(): return lax.ppermute(value, 'fsdp', pairs)  33.5 us
    ppermute x8, waiting for transfers between devices, along(): return lax.ppermute(value, 'fsdp', pairs)  15.6 us
    ppermute x8, starting transfers between devices, along(): return lax.ppermute(value, 'fsdp', pairs)  13.5 us
    pallas_call x3, Pallas kernels, place_rows(): pl.pallas_call(functools.partial(place_kernel, count), out_shape=shape, g...  11.3 us
    ppermute x6, starting transfers between devices, to_block(): return lax.ppermute(value, 'fsdp', pairs)  10.9 us
  transfers between devices with their start and end apart: 35, of which 16 were waited for; matrix products, arithmetic and copies ran while one was open for 18% of the time, Pallas kernels for 14%

profile of v8, /device:TPU:0, one launch (start us, length us, event | category | flops | bytes accessed | tf_op | source)
XLA Modules:
  0.0 353.7 jit_solution(7744206762504486392)
XLA Ops:
  2.7 5.0 %collective-permute-start.2 = (bf16[128,1792]{1,0:T(8,128)(2,1)}, bf16[128,1792]{1,0:T(8,128)(2,1)S(1)}, u32[]{:S(2)}, u32[]{:S(2)}) collective-permute-start(bf16[128,1792]{1,0:T(8,128)(2,1)} %get-tuple-element.87), channel_id=1, source_target_pairs={{0,6},{1,7},{2,0},{3,1},{4,2},{5,3},{6,4},{7,5},{8,14},{9,15},{10,... | collective-permute-start | bytes 1376264 | tf_op jit(solution)/shard_map/ppermute | solution.py:193
  8.8 3.6 %shard_map.46 = bf16[8,1040,128]{2,1,0:T(8,128)(2,1)} custom-call(bf16[128,8192]{1,0:T(8,128)(2,1)S(1)} %bitcast.55, s32[1,128]{1,0:T(1,128)S(1)} %copy-done.3), custom_call_target="tpu_custom_call" | custom-call | bytes 4194304 | tf_op jit(solution)/shard_map/pallas_call | solution.py:155
  12.4 3.7 %all-to-all-start = ((bf16[8,1040,128]{2,1,0:T(8,128)(2,1)}), bf16[8,1040,128]{2,1,0:T(8,128)(2,1)S(1)}, u32[]{:S(2)}, u32[]{:S(2)}) async-start(bf16[8,1040,128]{2,1,0:T(8,128)(2,1)} %shard_map.46), calls=%async_computation | async-start | bytes 4259840 | tf_op jit(solution)/shard_map/all_to_all | solution.py:229
  18.1 4.1 %dynamic-slice_bitcast_fusion = bf16[1024,1792]{1,0:T(8,128)(2,1)} fusion(bf16[1,4096,1792]{2,1,0:T(8,128)(2,1)} %param.7, s32[]{:T(128)S(6)} %select_n.186), kind=kLoop, calls=%fused_computation.1 | loop fusion | bytes 7340036 | tf_op jit(solution)/shard_map/dynamic_slice | solution.py:232
  28.7 4.8 %dynamic-slice_bitcast_fusion.3 = (bf16[320,1792]{1,0:T(8,128)(2,1)}, bf16[320,1792]{1,0:T(8,128)(2,1)}, bf16[1,320,1792]{2,1,0:T(8,128)(2,1)S(1)}, bf16[1,320,1...) fusion(bf16[1,4096,1792]{2,1,0:T(8,128)(2,1)} %param.7, ...), kind=kLoop, calls=%fused_computation.9 | loop fusion | bytes 13762584 | tf_op jit(solution)/shard_map/dynamic_slice | solution.py:217
  37.8 9.4 %collective-permute-done.1 = bf16[128,1792]{1,0:T(8,128)(2,1)S(1)} collective-permute-done((bf16[128,1792]{1,0:T(8,128)(2,1)}, bf16[128,1792]{1,0:T(8,128)(2,1)S(1)}, u32[]{:S(2)}, u32[]{:S(2)}) %collective-permute-start.1) | collective-permute-done | bytes 458784 | tf_op jit(solution)/shard_map/ppermute | solution.py:193
  54.4 27.3 %collective-permute-done.5 = bf16[128,7168]{1,0:T(8,128)(2,1)} collective-permute-done((bf16[128,7168]{1,0:T(8,128)(2,1)}, bf16[128,7168]{1,0:T(8,128)(2,1)}, u32[]{:S(2)}, u32[]{:S(2)}) %collective-permute-start.5) | collective-permute-done | bytes 1835040 | tf_op jit(solution)/shard_map/ppermute | solution.py:189
  85.9 7.9 %collective-permute-done.6 = bf16[4,128,1792]{2,1,0:T(8,128)(2,1)S(1)} collective-permute-done((bf16[4,128,1792]{2,1,0:T(8,128)(2,1)S(1)}, bf16[4,128,1792]{2,1,0:T(8,128)(2,1)S(1)}, u32[]{:S(2)}, u32[]{:S(2)}) %collective-permute-start.6) | collective-permute-done | bytes 1835040 | tf_op jit(solution)/shard_map/ppermute | solution.py:197
  95.1 8.4 %collective-permute-done.8 = bf16[2,128,1792]{2,1,0:T(8,128)(2,1)S(1)} collective-permute-done((bf16[2,128,1792]{2,1,0:T(8,128)(2,1)S(1)}, bf16[2,128,1792]{2,1,0:T(8,128)(2,1)S(1)}, u32[]{:S(2)}, u32[]{:S(2)}) %collective-permute-start.8) | collective-permute-done | bytes 917536 | tf_op jit(solution)/shard_map/ppermute | solution.py:189
  111.8 10.7 %collective-permute-done.9 = bf16[128,1792]{1,0:T(8,128)(2,1)} collective-permute-done((bf16[128,1792]{1,0:T(8,128)(2,1)}, bf16[128,1792]{1,0:T(8,128)(2,1)}, u32[]{:S(2)}, u32[]{:S(2)}) %collective-permute-start.9) | collective-permute-done | bytes 458784 | tf_op jit(solution)/shard_map/ppermute | solution.py:193
  123.9 17.6 %collective-permute-done.10 = bf16[128,1792]{1,0:T(8,128)(2,1)} collective-permute-done((bf16[128,1792]{1,0:T(8,128)(2,1)}, bf16[128,1792]{1,0:T(8,128)(2,1)}, u32[]{:S(2)}, u32[]{:S(2)}) %collective-permute-start.10) | collective-permute-done | bytes 458784 | tf_op jit(solution)/shard_map/ppermute | solution.py:193
  144.3 15.0 %collective-permute-done.13 = bf16[2,320,1792]{2,1,0:T(8,128)(2,1)} collective-permute-done((bf16[2,320,1792]{2,1,0:T(8,128)(2,1)}, bf16[2,320,1792]{2,1,0:T(8,128)(2,1)}, u32[]{:S(2)}, u32[]{:S(2)}) %collective-permute-start.13) | collective-permute-done | bytes 2293792 | tf_op jit(solution)/shard_map/ppermute | solution.py:189
  175.2 25.6 %collective-permute-done.17 = bf16[4,128,1792]{2,1,0:T(8,128)(2,1)} collective-permute-done((bf16[4,128,1792]{2,1,0:T(8,128)(2,1)}, bf16[4,128,1792]{2,1,0:T(8,128)(2,1)}, u32[]{:S(2)}, u32[]{:S(2)}) %collective-permute-start.17) | collective-permute-done | bytes 1835040 | tf_op jit(solution)/shard_map/ppermute | solution.py:197
  203.7 4.3 %collective-permute-done.16 = bf16[2,320,1792]{2,1,0:T(8,128)(2,1)} collective-permute-done((bf16[2,320,1792]{2,1,0:T(8,128)(2,1)}, bf16[2,320,1792]{2,1,0:T(8,128)(2,1)}, u32[]{:S(2)}, u32[]{:S(2)}) %collective-permute-start.16) | collective-permute-done | bytes 2293792 | tf_op jit(solution)/shard_map/ppermute | solution.py:189
  208.0 6.0 %collective-permute-done.15.refs_5_ = bf16[8,1040,128]{2,1,0:T(8,128)(2,1)} collective-permute-done((bf16[8,1040,128]{2,1,0:T(8,128)(2,1)}, bf16[8,1040,128]{2,1,0:T(8,128)(2,1)}, u32[]{:S(2)}, u32[]{:S(2)}) %collective-permute-start.15) | collective-permute-done | bytes 2129952 | tf_op jit(solution)/shard_map/ppermute | solution.py:205
  223.4 3.1 fusion.3
  232.6 9.6 %collective-permute-done.21.refs_6_ = bf16[8,448,128]{2,1,0:T(8,128)(2,1)} collective-permute-done((bf16[8,448,128]{2,1,0:T(8,128)(2,1)}, bf16[8,448,128]{2,1,0:T(8,128)(2,1)}, u32[]{:S(2)}, u32[]{:S(2)}) %collective-permute-start.21) | collective-permute-done | bytes 917536 | tf_op jit(solution)/shard_map/ppermute | solution.py:205
  243.9 16.5 %shard_map.47.refs_0_ = bf16[448,1792]{1,0:T(8,128)(2,1)} custom-call(s32[3]{0:T(128)} %pad_add_fusion.place_ref, s32[4]{0:T(128)} %and_select_fusion.slot_ref, bf16[8,1040,128]{2,1,0:T(8,128)(2,1)} %copy-done.4, bf16[8,1040,128]{2,1,0:T(8,128)(2,1)} %copy-done.5, bf16[8,1040,128]{2,1,0:T(8,128)(2,1)} %collective-permute-done.14.refs_2_, ...), custom_call_target="tpu_custom_call" | custom-call | flops 6576668672 | bytes 14680064 | tf_op jit(solution)/shard_map/pallas_call | solution.py:84
  260.4 3.2 dynamic-slice_bitcast_fusion.1
  271.3 18.6 %shard_map.48.refs_4_ = bf16[576,1792]{1,0:T(8,128)(2,1)} custom-call(s32[3]{0:T(128)} %pad_add_fusion.place_ref, s32[4]{0:T(128)} %and_select_fusion.slot_ref, bf16[8,1040,128]{2,1,0:T(8,128)(2,1)} %copy-done.4, bf16[8,1040,128]{2,1,0:T(8,128)(2,1)} %copy-done.5, bf16[8,1040,128]{2,1,0:T(8,128)(2,1)} %collective-permute-done.14.refs_2_, ...), custom_call_target="tpu_custom_call" | custom-call | flops 8455716864 | bytes 14680064 | tf_op jit(solution)/shard_map/pallas_call | solution.py:84
  290.8 13.9 %collective-permute-done.30.refs_2_ = bf16[448,1792]{1,0:T(8,128)(2,1)S(1)} collective-permute-done((bf16[448,1792]{1,0:T(8,128)(2,1)S(1)}, bf16[448,1792]{1,0:T(8,128)(2,1)S(1)}, u32[]{:S(2)}, u32[]{:S(2)}) %collective-permute-start.30) | collective-permute-done | bytes 1605664 | tf_op jit(solution)/shard_map/ppermute | solution.py:189
  304.8 3.5 collective-permute-done.31.refs_3_
  309.9 7.1 %shard_map.49.refs_1_ = bf16[4096,1792]{1,0:T(8,128)(2,1)} custom-call(s32[6]{0:T(128)S(1)} %stack.111.where_ref, bf16[448,1792]{1,0:T(8,128)(2,1)S(1)} %copy-done.1, bf16[448,1792]{1,0:T(8,128)(2,1)} %collective-permute-done.29.refs_1_, bf16[448,1792]{1,0:T(8,128)(2,1)S(1)} %collective-permute-done.30.refs_2_, ...), custom_call_target="tpu_custom_call" | custom-call | bytes 21102592 | tf_op jit(solution)/shard_map/pallas_call | solution.py:126
  317.0 31.1 %collective-permute-done.28.refs_0_ = bf16[576,1792]{1,0:T(8,128)(2,1)} collective-permute-done((bf16[576,1792]{1,0:T(8,128)(2,1)}, bf16[576,1792]{1,0:T(8,128)(2,1)}, u32[]{:S(2)}, u32[]{:S(2)}) %collective-permute-start.28) | collective-permute-done | bytes 2064416 | tf_op jit(solution)/shard_map/ppermute | solution.py:189
  (108 shorter events, 93.4 us)
Async XLA Ops:
  2.7 35.1 %collective-permute-start.2 = (bf16[128,1792]{1,0:T(8,128)(2,1)}, bf16[128,1792]{1,0:T(8,128)(2,1)S(1)}, u32[]{:S(2)}, u32[]{:S(2)}) collective-permute-start(bf16[128,1792]{1,0:T(8,128)(2,1)} %get-tuple-element.87), channel_id=1, source_target_pairs={{0,6},{1,7},{2,0},{3,1},{4,2},{5,3},{6,4},{7,5},{8,14},{9,15},{10,... | collective-permute-start | bytes 1376264 | tf_op jit(solution)/shard_map/ppermute | solution.py:193
  7.8 39.4 %collective-permute-start.1 = (bf16[128,1792]{1,0:T(8,128)(2,1)}, bf16[128,1792]{1,0:T(8,128)(2,1)S(1)}, u32[]{:S(2)}, u32[]{:S(2)}) collective-permute-start(bf16[128,1792]{1,0:T(8,128)(2,1)} %get-tuple-element.88), channel_id=1, source_target_pairs={{0,4},{1,5},{2,6},{3,7},{4,0},{5,1},{6,2},{7,3},{8,12},{9,13},{10,... | collective-permute-start | bytes 1376264 | tf_op jit(solution)/shard_map/ppermute | solution.py:193
  7.8 39.4 %collective-permute-start = (bf16[128,1792]{1,0:T(8,128)(2,1)}, bf16[128,1792]{1,0:T(8,128)(2,1)}, u32[]{:S(2)}, u32[]{:S(2)}) collective-permute-start(bf16[128,1792]{1,0:T(8,128)(2,1)} %get-tuple-element.89), channel_id=1, source_target_pairs={{0,2},{1,3},{2,4},{3,5},{4,6},{5,7},{6,0},{7,1},{8,10},{9,11},{10,... | collective-permute-start | bytes 1376264 | tf_op jit(solution)/shard_map/ppermute | solution.py:193
  12.4 34.8 %all-to-all-start = ((bf16[8,1040,128]{2,1,0:T(8,128)(2,1)}), bf16[8,1040,128]{2,1,0:T(8,128)(2,1)S(1)}, u32[]{:S(2)}, u32[]{:S(2)}) async-start(bf16[8,1040,128]{2,1,0:T(8,128)(2,1)} %shard_map.46), calls=%async_computation | async-start | bytes 4259840 | tf_op jit(solution)/shard_map/all_to_all | solution.py:229
  16.1 65.6 %collective-permute-start.5 = (bf16[128,7168]{1,0:T(8,128)(2,1)}, bf16[128,7168]{1,0:T(8,128)(2,1)}, u32[]{:S(2)}, u32[]{:S(2)}) collective-permute-start(bf16[128,7168]{1,0:T(8,128)(2,1)} %bitcast.57), channel_id=1, source_target_pairs={{0,16},{8,24},{16,0},{24,8},{1,17},{9,25},{17,1},{25,9},{2,18},{10... | collective-permute-start | bytes 5505032 | tf_op jit(solution)/shard_map/ppermute | solution.py:189
  22.2 81.4 %collective-permute-start.7 = (bf16[1024,1792]{1,0:T(8,128)(2,1)}, bf16[1024,1792]{1,0:T(8,128)(2,1)}, u32[]{:S(2)}, u32[]{:S(2)}) collective-permute-start(bf16[1024,1792]{1,0:T(8,128)(2,1)} %dynamic-slice_bitcast_fusion), channel_id=1, source_target_pairs={{0,8},{8,0},{16,24},{24,16},{1,9},{9,1},{17,25},{25,17},{2,10},{10... | collective-permute-start | bytes 11010056 | tf_op jit(solution)/shard_map/ppermute | solution.py:189
  47.2 56.4 %collective-permute-start.4 = (bf16[8,1040,128]{2,1,0:T(8,128)(2,1)S(1)}, bf16[8,1040,128]{2,1,0:T(8,128)(2,1)S(1)}, u32[]{:S(2)}, u32[]{:S(2)}) collective-permute-start(bf16[8,1040,128]{2,1,0:T(8,128)(2,1)S(1)} %all-to-all-done.refs_0_), channel_id=1, source_target_pairs={{0,2},{1,3},{2,4},{3,5},{4,6},{5,7},{8,10},{9,11},{10,12},{11,13},... | collective-permute-start | bytes 6389768 | tf_op jit(solution)/shard_map/ppermute | solution.py:205
  50.2 53.4 %collective-permute-start.3 = (bf16[8,1040,128]{2,1,0:T(8,128)(2,1)S(1)}, bf16[8,1040,128]{2,1,0:T(8,128)(2,1)S(1)}, u32[]{:S(2)}, u32[]{:S(2)}) collective-permute-start(bf16[8,1040,128]{2,1,0:T(8,128)(2,1)S(1)} %all-to-all-done.refs_0_), channel_id=1, source_target_pairs={{2,0},{3,1},{4,2},{5,3},{6,4},{7,5},{10,8},{11,9},{12,10},{13,11},... | collective-permute-start | bytes 6389768 | tf_op jit(solution)/shard_map/ppermute | solution.py:205
  52.8 40.9 %collective-permute-start.6 = (bf16[4,128,1792]{2,1,0:T(8,128)(2,1)S(1)}, bf16[4,128,1792]{2,1,0:T(8,128)(2,1)S(1)}, u32[]{:S(2)}, u32[]{:S(2)}) collective-permute-start(bf16[4,128,1792]{2,1,0:T(8,128)(2,1)S(1)} %pad_maximum_fusion.3), channel_id=1, source_target_pairs={{0,1},{1,0},{2,3},{3,2},{4,5},{5,4},{6,7},{7,6},{8,9},{9,8},{10,11... | collective-permute-start | bytes 5505032 | tf_op jit(solution)/shard_map/ppermute | solution.py:197
  106.3 53.0 %collective-permute-start.12 = (bf16[4,256,1792]{2,1,0:T(8,128)(2,1)}, bf16[4,256,1792]{2,1,0:T(8,128)(2,1)}, u32[]{:S(2)}, u32[]{:S(2)}) collective-permute-start(bf16[4,256,1792]{2,1,0:T(8,128)(2,1)} %constant_dynamic-update-slice_fusion.refs_7_), channel_id=1, source_target_pairs={{0,8},{8,0},{16,24},{24,16},{1,9},{9,1},{17,25},{25,17},{2,10},{10... | collective-permute-start | bytes 11010056 | tf_op jit(solution)/shard_map/ppermute | solution.py:189
  106.3 53.0 %collective-permute-start.13 = (bf16[2,320,1792]{2,1,0:T(8,128)(2,1)}, bf16[2,320,1792]{2,1,0:T(8,128)(2,1)}, u32[]{:S(2)}, u32[]{:S(2)}) collective-permute-start(bf16[2,320,1792]{2,1,0:T(8,128)(2,1)} %pad_maximum_fusion), channel_id=1, source_target_pairs={{0,16},{8,24},{16,0},{24,8},{1,17},{9,25},{17,1},{25,9},{2,18},{10... | collective-permute-start | bytes 6881288 | tf_op jit(solution)/shard_map/ppermute | solution.py:189
  109.4 32.1 %collective-permute-start.10 = (bf16[128,1792]{1,0:T(8,128)(2,1)}, bf16[128,1792]{1,0:T(8,128)(2,1)}, u32[]{:S(2)}, u32[]{:S(2)}) collective-permute-start(bf16[128,1792]{1,0:T(8,128)(2,1)} %get-tuple-element.42), channel_id=1, source_target_pairs={{0,4},{1,5},{2,6},{3,7},{4,0},{5,1},{6,2},{7,3},{8,12},{9,13},{10,... | collective-permute-start | bytes 1376264 | tf_op jit(solution)/shard_map/ppermute | solution.py:193
  110.3 31.2 %collective-permute-start.11 = (bf16[128,1792]{1,0:T(8,128)(2,1)}, bf16[128,1792]{1,0:T(8,128)(2,1)}, u32[]{:S(2)}, u32[]{:S(2)}) collective-permute-start(bf16[128,1792]{1,0:T(8,128)(2,1)} %get-tuple-element.43), channel_id=1, source_target_pairs={{0,6},{1,7},{2,0},{3,1},{4,2},{5,3},{6,4},{7,5},{8,14},{9,15},{10,... | collective-permute-start | bytes 1376264 | tf_op jit(solution)/shard_map/ppermute | solution.py:193
  122.6 85.5 %collective-permute-start.16 = (bf16[2,320,1792]{2,1,0:T(8,128)(2,1)}, bf16[2,320,1792]{2,1,0:T(8,128)(2,1)}, u32[]{:S(2)}, u32[]{:S(2)}) collective-permute-start(bf16[2,320,1792]{2,1,0:T(8,128)(2,1)} %pad_maximum_fusion.1), channel_id=1, source_target_pairs={{0,16},{8,24},{16,0},{24,8},{1,17},{9,25},{17,1},{25,9},{2,18},{10... | collective-permute-start | bytes 6881288 | tf_op jit(solution)/shard_map/ppermute | solution.py:189
  159.3 41.6 %collective-permute-start.17 = (bf16[4,128,1792]{2,1,0:T(8,128)(2,1)}, bf16[4,128,1792]{2,1,0:T(8,128)(2,1)}, u32[]{:S(2)}, u32[]{:S(2)}) collective-permute-start(bf16[4,128,1792]{2,1,0:T(8,128)(2,1)} %pad_maximum_fusion.4), channel_id=1, source_target_pairs={{0,1},{1,0},{2,3},{3,2},{4,5},{5,4},{6,7},{7,6},{8,9},{9,8},{10,11... | collective-permute-start | bytes 5505032 | tf_op jit(solution)/shard_map/ppermute | solution.py:197
  160.7 47.3 %collective-permute-start.14 = (bf16[8,1040,128]{2,1,0:T(8,128)(2,1)}, bf16[8,1040,128]{2,1,0:T(8,128)(2,1)}, u32[]{:S(2)}, u32[]{:S(2)}) collective-permute-start(bf16[8,1040,128]{2,1,0:T(8,128)(2,1)} %copy-done.5), channel_id=1, source_target_pairs={{2,4},{3,5},{4,6},{5,7},{10,12},{11,13},{12,14},{13,15},{18,20},{1... | collective-permute-start | bytes 6389768 | tf_op jit(solution)/shard_map/ppermute | solution.py:205
  162.8 51.2 %collective-permute-start.15 = (bf16[8,1040,128]{2,1,0:T(8,128)(2,1)}, bf16[8,1040,128]{2,1,0:T(8,128)(2,1)}, u32[]{:S(2)}, u32[]{:S(2)}) collective-permute-start(bf16[8,1040,128]{2,1,0:T(8,128)(2,1)} %copy-done.6), channel_id=1, source_target_pairs={{2,0},{3,1},{4,2},{5,3},{10,8},{11,9},{12,10},{13,11},{18,16},{19,... | collective-permute-start | bytes 6389768 | tf_op jit(solution)/shard_map/ppermute | solution.py:205
  170.0 38.1 %collective-permute-start.19 = (bf16[320,1792]{1,0:T(8,128)(2,1)}, bf16[320,1792]{1,0:T(8,128)(2,1)}, u32[]{:S(2)}, u32[]{:S(2)}) collective-permute-start(bf16[320,1792]{1,0:T(8,128)(2,1)} %get-tuple-element.80), channel_id=1, source_target_pairs={{0,8},{8,0},{16,24},{24,16},{1,9},{9,1},{17,25},{25,17},{2,10},{10... | collective-permute-start | bytes 3440648 | tf_op jit(solution)/shard_map/ppermute | solution.py:189
  214.0 29.9 %collective-permute-start.22 = (bf16[4,256,1792]{2,1,0:T(8,128)(2,1)}, bf16[4,256,1792]{2,1,0:T(8,128)(2,1)}, u32[]{:S(2)}, u32[]{:S(2)}) collective-permute-start(bf16[4,256,1792]{2,1,0:T(8,128)(2,1)} %constant_dynamic-update-slice_fusion.2.refs_9_), channel_id=1, source_target_pairs={{0,8},{8,0},{16,24},{24,16},{1,9},{9,1},{17,25},{25,17},{2,10},{10... | collective-permute-start | bytes 11010056 | tf_op jit(solution)/shard_map/ppermute | solution.py:189
  214.0 49.6 %collective-permute-start.26 = (bf16[2,256,1792]{2,1,0:T(8,128)(2,1)S(1)}, bf16[2,256,1792]{2,1,0:T(8,128)(2,1)}, u32[]{:S(2)}, u32[]{:S(2)}) collective-permute-start(bf16[2,256,1792]{2,1,0:T(8,128)(2,1)S(1)} %copy-done.7), channel_id=1, source_target_pairs={{0,16},{8,24},{16,0},{24,8},{1,17},{9,25},{17,1},{25,9},{2,18},{10... | collective-permute-start | bytes 5505032 | tf_op jit(solution)/shard_map/ppermute | solution.py:189
  231.3 39.1 %collective-permute-start.24 = (bf16[8,576,128]{2,1,0:T(8,128)(2,1)}, bf16[8,576,128]{2,1,0:T(8,128)(2,1)}, u32[]{:S(2)}, u32[]{:S(2)}) collective-permute-start(bf16[8,576,128]{2,1,0:T(8,128)(2,1)} %slice.45), channel_id=1, source_target_pairs={{2,0},{3,1},{10,8},{11,9},{18,16},{19,17},{26,24},{27,25}} | collective-permute-start | bytes 3538952 | tf_op jit(solution)/shard_map/ppermute | solution.py:205
  242.2 28.2 %collective-permute-start.23 = (bf16[8,576,128]{2,1,0:T(8,128)(2,1)}, bf16[8,576,128]{2,1,0:T(8,128)(2,1)}, u32[]{:S(2)}, u32[]{:S(2)}) collective-permute-start(bf16[8,576,128]{2,1,0:T(8,128)(2,1)} %slice.44), channel_id=1, source_target_pairs={{4,6},{5,7},{12,14},{13,15},{20,22},{21,23},{28,30},{29,31}} | collective-permute-start | bytes 3538952 | tf_op jit(solution)/shard_map/ppermute | solution.py:205
  266.8 38.0 %collective-permute-start.30 = (bf16[448,1792]{1,0:T(8,128)(2,1)S(1)}, bf16[448,1792]{1,0:T(8,128)(2,1)S(1)}, u32[]{:S(2)}, u32[]{:S(2)}) collective-permute-start(bf16[448,1792]{1,0:T(8,128)(2,1)S(1)} %copy-done.1), channel_id=1, source_target_pairs={{0,16},{8,24},{16,0},{24,8},{1,17},{9,25},{17,1},{25,9},{2,18},{10... | collective-permute-start | bytes 4816904 | tf_op jit(solution)/shard_map/ppermute | solution.py:189
  290.0 58.1 %collective-permute-start.28 = (bf16[576,1792]{1,0:T(8,128)(2,1)}, bf16[576,1792]{1,0:T(8,128)(2,1)}, u32[]{:S(2)}, u32[]{:S(2)}) collective-permute-start(bf16[576,1792]{1,0:T(8,128)(2,1)} %shard_map.48.refs_4_), channel_id=1, source_target_pairs={{0,16},{8,24},{16,0},{24,8},{1,17},{9,25},{17,1},{25,9},{2,18},{10... | collective-permute-start | bytes 6193160 | tf_op jit(solution)/shard_map/ppermute | solution.py:189
  (21 other events, 355.3 us)

commit v9 on v8

--- a/solution.py
+++ b/solution.py
@@ -9,7 +9,7 @@
 
 F = 7168
 SEQS = 2
-CHUNKS = (2, 5, 5, 4)
+CHUNKS = (2, 4, 6, 4)
 FLAG_ROWS = 16
 COL_TILE = 256
 
@@ -76,10 +76,17 @@
         first += size
 
 
+def weight_block(piece):
+    rows = piece.shape[-2]
+    if piece.ndim == 2:
+        return pl.BlockSpec((rows, COL_TILE), lambda j, *_: (0, j))
+    return pl.BlockSpec((None, rows, COL_TILE), lambda j, place, slots: (place[3], 0, j))
+
+
 def merge_rows(place, slots, sources, starts, grads, weights):
     copies, shards = len(grads), grads[0].shape[0]
     tok, width = grads[0].shape[1:]
-    sizes = [piece.shape[0] for piece in weights[::copies]]
+    sizes = [piece.shape[-2] for piece in weights[::copies]]
     rows = sum(sizes)
     return pl.pallas_call(
         functools.partial(merge_kernel, copies, shards, starts, sizes),
@@ -89,7 +96,7 @@
             grid=(width // COL_TILE,),
             in_specs=[pl.BlockSpec(memory_space=pl.ANY)] * len(sources)
             + [pl.BlockSpec((shards, tok, COL_TILE), lambda j, *_: (0, 0, j))] * copies
-            + [pl.BlockSpec((piece.shape[0], COL_TILE), lambda j, *_: (0, j)) for piece in weights],
+            + [weight_block(piece) for piece in weights],
             out_specs=pl.BlockSpec((rows, COL_TILE), lambda j, *_: (0, j)),
             scratch_shapes=[
                 pltpu.VMEM((copies, shards, rows, tok), jnp.bfloat16),
@@ -268,7 +275,7 @@
     named = jnp.where(a == 0, high[0][:, share, 0], jnp.where(a == blocks - 1, low[0][:, share, 0], own[:, share, 0]))
     alone = jnp.where(named[::spread] > 0.5, 0, blocks - 1)[m ^ jnp.arange(copies)]
     slots = ((a - alone) % blocks).astype(jnp.int32)
-    place = jnp.stack([a, m, h]).astype(jnp.int32)
+    place = jnp.stack([a, m, h, core]).astype(jnp.int32)
 
     stage = (low[1], high[1], weight_far[2], grads[1], *halves, weight_mate[1], slots)
     half = starts[2]
@@ -280,21 +287,21 @@
     cores(2, *stage, grads[3])
     send_weights(3, *early)
 
-    def sums(part, pieces, place, *others):
+    def sums(part, pieces, place):
         held = []
         for k in pieces:
-            mine = lax.dynamic_index_in_dim(weight_far[k], after(core, *others), 0, keepdims=False)
-            held += [weight_rows(m, k), mate_rows[starts[k]:starts[k] + sizes[k]], mine, weight_mate[k]]
+            held += [*ready[k], weight_far[k], weight_mate[k]]
         sources = [own, low[0], low[1], low_last[part], high[0], high[1], high_last[part]]
         begin = [part * half] * len(sources)
         begin[3] = begin[6] = 0
         return merge_rows(place, slots, sources, begin, grads, held)
 
     where = [[(m ^ flip) * share + part * half for flip in range(copies)] for part in range(2)]
-    first = sums(0, (0, 1), place)
+    ready = {k: (weight_rows(m, k), mate_rows[starts[k]:starts[k] + sizes[k]]) for k in range(len(sizes))}
+    first = sums(0, (0, 1), after(place, *ready[2], *ready[3]))
     far_first = to_copy(first, 2)
     cores(3, first)
-    second = sums(1, (2, 3), after(place, first), first)
+    second = sums(1, (2, 3), after(place, first))
     far_second = to_copy(second, 2)
     near_first = to_copy(after(first, second), 1)
     near_second = to_copy(second, 1)

time: 355 us -> 345 us (0.972)
  local copies, waits for them, and re-layouts: 58.8 us -> 52.7 us
  waiting for transfers between devices: 194 us -> 190 us
    ppermute x6, waiting for transfers between devices: 37.7 us -> 8.43 us  [to_block(): return lax.ppermute(value, 'fsdp', pairs)]
    ppermute x18, waiting for transfers between devices: 107 us -> 125 us  [to_copy(): return lax.ppermute(value, 'mp', [(s, s ^ flip) for s in range(copies)])]
    ppermute x2, waiting for transfers between devices: 33.5 us -> 43.3 us  [to_half(): return lax.ppermute(value, 'fsdp', pairs)]
    squeeze x2 -> x0, local copies, waits for them, and re-layouts: 3.94 us -> none  [sums(): lax.dynamic_index_in_dim(weight_far[k], after(core, *others), 0, keepdims...]
    unnamed x22 -> x42, local copies, waits for them, and re-layouts: 9.46 us -> 10.6 us
  transfers between devices with their start and end apart: 35 -> 35, of which waited for: 16 -> 15; matrix products, arithmetic and copies ran while one was open for 18% -> 15% of each run, Pallas kernels for 14% -> 14%
where the time goes in v9:
time: 345 us; the launch traced here: 344 us
  waiting for transfers between devices  190 us (55%)
  local copies, waits for them, and re-layouts  52.7 us (15%)
  Pallas kernels  50.2 us (15%)
  starting transfers between devices  40.7 us (12%)
  other arithmetic  10.3 us (3%)
    ppermute x18, waiting for transfers between devices, to_copy(): return lax.ppermute(value, 'mp', [(s, s ^ flip) for s in range(copies)])  125 us
    ppermute x2, waiting for transfers between devices, to_half(): return lax.ppermute(value, 'fsdp', pairs)  43.3 us
    pallas_call x2, Pallas kernels, merge_rows(): pl.pallas_call(functools.partial(merge_kernel, copies, shards, starts, si...  35.2 us
    ppermute x8, starting transfers between devices, along(): return lax.ppermute(value, 'fsdp', pairs)  14.6 us
    ppermute x8, waiting for transfers between devices, along(): return lax.ppermute(value, 'fsdp', pairs)  13 us
    pallas_call x3, Pallas kernels, place_rows(): pl.pallas_call(functools.partial(place_kernel, count), out_shape=shape, g...  11.4 us
    ppermute x6, starting transfers between devices, to_block(): return lax.ppermute(value, 'fsdp', pairs)  10.9 us
    dynamic_slice x3, local copies, waits for them, and re-layouts, weight_rows(): lax.dynamic_slice_in_dim(weights[0], owner * share + starts[k], sizes[k], 0)  10.7 us
  transfers between devices with their start and end apart: 35, of which 15 were waited for; matrix products, arithmetic and copies ran while one was open for 15% of the time, Pallas kernels for 14%

profile of v9, /device:TPU:0, one launch (start us, length us, event | category | flops | bytes accessed | tf_op | source)
XLA Modules:
  0.0 344.1 jit_solution(7732001843726516407)
XLA Ops:
  2.7 5.0 %collective-permute-start.3 = (bf16[128,1792]{1,0:T(8,128)(2,1)}, bf16[128,1792]{1,0:T(8,128)(2,1)}, u32[]{:S(2)}, u32[]{:S(2)}) collective-permute-start(bf16[128,1792]{1,0:T(8,128)(2,1)} %get-tuple-element.81), channel_id=1, source_target_pairs={{0,6},{1,7},{2,0},{3,1},{4,2},{5,3},{6,4},{7,5},{8,14},{9,15},{10,... | collective-permute-start | bytes 1376264 | tf_op jit(solution)/shard_map/ppermute | solution.py:200
  8.8 3.6 %shard_map.46 = bf16[8,1040,128]{2,1,0:T(8,128)(2,1)} custom-call(bf16[128,8192]{1,0:T(8,128)(2,1)S(1)} %bitcast.48, s32[1,128]{1,0:T(1,128)S(1)} %copy-done.3), custom_call_target="tpu_custom_call" | custom-call | bytes 4194304 | tf_op jit(solution)/shard_map/pallas_call | solution.py:162
  12.4 3.7 %all-to-all-start = ((bf16[8,1040,128]{2,1,0:T(8,128)(2,1)}), bf16[8,1040,128]{2,1,0:T(8,128)(2,1)S(1)}, u32[]{:S(2)}, u32[]{:S(2)}) async-start(bf16[8,1040,128]{2,1,0:T(8,128)(2,1)} %shard_map.46), calls=%async_computation | async-start | bytes 4259840 | tf_op jit(solution)/shard_map/all_to_all | solution.py:236
  18.1 4.1 %dynamic-slice_bitcast_fusion = bf16[1024,1792]{1,0:T(8,128)(2,1)} fusion(bf16[1,4096,1792]{2,1,0:T(8,128)(2,1)} %param.7, s32[]{:T(128)S(6)} %select_n.163), kind=kLoop, calls=%fused_computation.1 | loop fusion | bytes 7340036 | tf_op jit(solution)/shard_map/dynamic_slice | solution.py:239
  22.2 4.7 %dynamic-slice_bitcast_fusion.4 = (bf16[256,1792]{1,0:T(8,128)(2,1)}, bf16[1,256,1792]{2,1,0:T(8,128)(2,1)S(1)}, bf16[1,256,1792]{2,1,0:T(8,128)(2,1)}, bf16[1,2...) fusion(bf16[1,4096,1792]{2,1,0:T(8,128)(2,1)} %param.7, s32[]{:T(128)S(6)} %select_n.184, ...), kind=kLoop, calls=%fused_computation.11 | loop fusion | bytes 11010072 | tf_op jit(solution)/shard_map/dynamic_slice | solution.py:224
  29.3 3.6 %constant_dynamic-slice_fusion.7 = (bf16[1,384,1792]{2,1,0:T(8,128)(2,1)S(1)}, bf16[1,384,1792]{2,1,0:T(8,128)(2,1)S(1)}, bf16[384,1792]{1,0:T(8,128)(2,1)}) fusion(bf16[1,4096,1792]{2,1,0:T(8,128)(2,1)} %param.7, s32[]{:T(128)S(6)} %select_n.170, s32[]{:T(128)S(6)} %select_n.171, s32[]{:T(128)S(6)} %select_n.153), kind=kLoop, calls=%fused_computation.32 | loop fusion | bytes 8257548 | tf_op jit(solution)/shard_map/dynamic_slice | solution.py:224
  38.8 8.4 %collective-permute-done.2 = bf16[128,1792]{1,0:T(8,128)(2,1)} collective-permute-done((bf16[128,1792]{1,0:T(8,128)(2,1)}, bf16[128,1792]{1,0:T(8,128)(2,1)}, u32[]{:S(2)}, u32[]{:S(2)}) %collective-permute-start.2) | collective-permute-done | bytes 458784 | tf_op jit(solution)/shard_map/ppermute | solution.py:200
  47.3 4.1 %collective-permute-start.5 = (bf16[8,1040,128]{2,1,0:T(8,128)(2,1)S(1)}, bf16[8,1040,128]{2,1,0:T(8,128)(2,1)}, u32[]{:S(2)}, u32[]{:S(2)}) collective-permute-start(bf16[8,1040,128]{2,1,0:T(8,128)(2,1)S(1)} %all-to-all-done.refs_0_), channel_id=1, source_target_pairs={{0,2},{1,3},{2,4},{3,5},{4,6},{5,7},{8,10},{9,11},{10,12},{11,13},... | collective-permute-start | bytes 6389768 | tf_op jit(solution)/shard_map/ppermute | solution.py:212
  55.9 25.8 %collective-permute-done.6 = bf16[128,7168]{1,0:T(8,128)(2,1)} collective-permute-done((bf16[128,7168]{1,0:T(8,128)(2,1)}, bf16[128,7168]{1,0:T(8,128)(2,1)}, u32[]{:S(2)}, u32[]{:S(2)}) %collective-permute-start.6) | collective-permute-done | bytes 1835040 | tf_op jit(solution)/shard_map/ppermute | solution.py:196
  83.7 11.5 %collective-permute-done.7 = bf16[4,128,1792]{2,1,0:T(8,128)(2,1)S(1)} collective-permute-done((bf16[4,128,1792]{2,1,0:T(8,128)(2,1)S(1)}, bf16[4,128,1792]{2,1,0:T(8,128)(2,1)S(1)}, u32[]{:S(2)}, u32[]{:S(2)}) %collective-permute-start.7) | collective-permute-done | bytes 1835040 | tf_op jit(solution)/shard_map/ppermute | solution.py:204
  95.3 8.2 %collective-permute-done.8.refs_13_ = bf16[2,128,1792]{2,1,0:T(8,128)(2,1)S(1)} collective-permute-done((bf16[2,128,1792]{2,1,0:T(8,128)(2,1)S(1)}, bf16[2,128,1792]{2,1,0:T(8,128)(2,1)S(1)}, u32[]{:S(2)}, u32[]{:S(2)}) %collective-permute-start.8) | collective-permute-done | bytes 917536 | tf_op jit(solution)/shard_map/ppermute | solution.py:196
  109.2 36.8 %collective-permute-done.13.refs_17_ = bf16[2,256,1792]{2,1,0:T(8,128)(2,1)S(1)} collective-permute-done((bf16[2,256,1792]{2,1,0:T(8,128)(2,1)S(1)}, bf16[2,256,1792]{2,1,0:T(8,128)(2,1)S(1)}, u32[]{:S(2)}, u32[]{:S(2)}) %collective-permute-start.13) | collective-permute-done | bytes 1835040 | tf_op jit(solution)/shard_map/ppermute | solution.py:196
  160.4 2.9 constant_dynamic-update-slice_fusion.3
  163.3 31.9 %collective-permute-done.17 = bf16[4,128,1792]{2,1,0:T(8,128)(2,1)} collective-permute-done((bf16[4,128,1792]{2,1,0:T(8,128)(2,1)}, bf16[4,128,1792]{2,1,0:T(8,128)(2,1)}, u32[]{:S(2)}, u32[]{:S(2)}) %collective-permute-start.17) | collective-permute-done | bytes 1835040 | tf_op jit(solution)/shard_map/ppermute | solution.py:204
  195.1 2.9 constant_dynamic-update-slice_fusion.2.refs_9_
  198.0 9.6 %collective-permute-done.16.refs_13_ = bf16[2,384,1792]{2,1,0:T(8,128)(2,1)} collective-permute-done((bf16[2,384,1792]{2,1,0:T(8,128)(2,1)}, bf16[2,384,1792]{2,1,0:T(8,128)(2,1)}, u32[]{:S(2)}, u32[]{:S(2)}) %collective-permute-start.16) | collective-permute-done | bytes 2752544 | tf_op jit(solution)/shard_map/ppermute | solution.py:196
  232.8 4.3 %collective-permute-done.21.refs_6_ = bf16[8,384,128]{2,1,0:T(8,128)(2,1)} collective-permute-done((bf16[8,384,128]{2,1,0:T(8,128)(2,1)S(1)}, bf16[8,384,128]{2,1,0:T(8,128)(2,1)}, u32[]{:S(2)}, u32[]{:S(2)}) %collective-permute-start.21) | collective-permute-done | bytes 786464 | tf_op jit(solution)/shard_map/ppermute | solution.py:212
  237.2 15.4 %shard_map.47.refs_0_ = bf16[384,1792]{1,0:T(8,128)(2,1)} custom-call(s32[4]{0:T(128)} %pad_add_fusion.place_ref, s32[4]{0:T(128)} %and_select_fusion.slot_ref, bf16[8,1040,128]{2,1,0:T(8,128)(2,1)} %copy-done.5, bf16[8,1040,128]{2,1,0:T(8,128)(2,1)} %collective-permute-done.5.refs_1_, bf16[8,1040,128]{2,1,0:T(8,128)(2,1)} %collective-permute-done.14.refs_2_, ...), custom_call_target="tpu_custom_call" | custom-call | flops 5637144576 | bytes 14680064 | tf_op jit(solution)/shard_map/pallas_call | solution.py:91
  256.0 8.7 %collective-permute-done.24.refs_6_ = bf16[8,640,128]{2,1,0:T(8,128)(2,1)} collective-permute-done((bf16[8,640,128]{2,1,0:T(8,128)(2,1)}, bf16[8,640,128]{2,1,0:T(8,128)(2,1)}, u32[]{:S(2)}, u32[]{:S(2)}) %collective-permute-start.24) | collective-permute-done | bytes 1310752 | tf_op jit(solution)/shard_map/ppermute | solution.py:212
  265.6 19.8 %shard_map.48.refs_4_ = bf16[640,1792]{1,0:T(8,128)(2,1)} custom-call(s32[4]{0:T(128)} %pad_add_fusion.place_ref, s32[4]{0:T(128)} %and_select_fusion.slot_ref, bf16[8,1040,128]{2,1,0:T(8,128)(2,1)} %copy-done.5, bf16[8,1040,128]{2,1,0:T(8,128)(2,1)} %collective-permute-done.5.refs_1_, bf16[8,1040,128]{2,1,0:T(8,128)(2,1)} %collective-permute-done.14.refs_2_, ...), custom_call_target="tpu_custom_call" | custom-call | flops 9395240960 | bytes 14680064 | tf_op jit(solution)/shard_map/pallas_call | solution.py:91
  287.6 4.5 %collective-permute-done.29.refs_1_ = bf16[384,1792]{1,0:T(8,128)(2,1)} collective-permute-done((bf16[384,1792]{1,0:T(8,128)(2,1)S(1)}, bf16[384,1792]{1,0:T(8,128)(2,1)}, u32[]{:S(2)}, u32[]{:S(2)}) %collective-permute-start.29) | collective-permute-done | bytes 1376288 | tf_op jit(solution)/shard_map/ppermute | solution.py:196
  295.7 7.0 %shard_map.49.refs_1_ = bf16[4096,1792]{1,0:T(8,128)(2,1)} custom-call(s32[6]{0:T(128)S(1)} %stack.115.where_ref, bf16[384,1792]{1,0:T(8,128)(2,1)S(1)} %copy-done.1, bf16[384,1792]{1,0:T(8,128)(2,1)} %collective-permute-done.29.refs_1_, bf16[384,1792]{1,0:T(8,128)(2,1)S(1)} %collective-permute-done.30.refs_2_, ...), custom_call_target="tpu_custom_call" | custom-call | bytes 20185088 | tf_op jit(solution)/shard_map/pallas_call | solution.py:133
  302.6 35.5 %collective-permute-done.28.refs_0_ = bf16[640,1792]{1,0:T(8,128)(2,1)} collective-permute-done((bf16[640,1792]{1,0:T(8,128)(2,1)}, bf16[640,1792]{1,0:T(8,128)(2,1)}, u32[]{:S(2)}, u32[]{:S(2)}) %collective-permute-start.28) | collective-permute-done | bytes 2293792 | tf_op jit(solution)/shard_map/ppermute | solution.py:196
  338.1 3.0 shard_map.50.refs_1_
  (127 shorter events, 78.9 us)
Async XLA Ops:
  2.7 36.1 %collective-permute-start.3 = (bf16[128,1792]{1,0:T(8,128)(2,1)}, bf16[128,1792]{1,0:T(8,128)(2,1)}, u32[]{:S(2)}, u32[]{:S(2)}) collective-permute-start(bf16[128,1792]{1,0:T(8,128)(2,1)} %get-tuple-element.81), channel_id=1, source_target_pairs={{0,6},{1,7},{2,0},{3,1},{4,2},{5,3},{6,4},{7,5},{8,14},{9,15},{10,... | collective-permute-start | bytes 1376264 | tf_op jit(solution)/shard_map/ppermute | solution.py:200
  7.8 39.5 %collective-permute-start.2 = (bf16[128,1792]{1,0:T(8,128)(2,1)}, bf16[128,1792]{1,0:T(8,128)(2,1)}, u32[]{:S(2)}, u32[]{:S(2)}) collective-permute-start(bf16[128,1792]{1,0:T(8,128)(2,1)} %get-tuple-element.82), channel_id=1, source_target_pairs={{0,4},{1,5},{2,6},{3,7},{4,0},{5,1},{6,2},{7,3},{8,12},{9,13},{10,... | collective-permute-start | bytes 1376264 | tf_op jit(solution)/shard_map/ppermute | solution.py:200
  7.8 39.5 %collective-permute-start.1 = (bf16[128,1792]{1,0:T(8,128)(2,1)}, bf16[128,1792]{1,0:T(8,128)(2,1)}, u32[]{:S(2)}, u32[]{:S(2)}) collective-permute-start(bf16[128,1792]{1,0:T(8,128)(2,1)} %get-tuple-element.83), channel_id=1, source_target_pairs={{0,2},{1,3},{2,4},{3,5},{4,6},{5,7},{6,0},{7,1},{8,10},{9,11},{10,... | collective-permute-start | bytes 1376264 | tf_op jit(solution)/shard_map/ppermute | solution.py:200
  12.4 34.9 %all-to-all-start = ((bf16[8,1040,128]{2,1,0:T(8,128)(2,1)}), bf16[8,1040,128]{2,1,0:T(8,128)(2,1)S(1)}, u32[]{:S(2)}, u32[]{:S(2)}) async-start(bf16[8,1040,128]{2,1,0:T(8,128)(2,1)} %shard_map.46), calls=%async_computation | async-start | bytes 4259840 | tf_op jit(solution)/shard_map/all_to_all | solution.py:236
  16.1 65.6 %collective-permute-start.6 = (bf16[128,7168]{1,0:T(8,128)(2,1)}, bf16[128,7168]{1,0:T(8,128)(2,1)}, u32[]{:S(2)}, u32[]{:S(2)}) collective-permute-start(bf16[128,7168]{1,0:T(8,128)(2,1)} %bitcast.50), channel_id=1, source_target_pairs={{0,16},{8,24},{16,0},{24,8},{1,17},{9,25},{17,1},{25,9},{2,18},{10... | collective-permute-start | bytes 5505032 | tf_op jit(solution)/shard_map/ppermute | solution.py:196
  22.2 81.4 %collective-permute-start = (bf16[1024,1792]{1,0:T(8,128)(2,1)}, bf16[1024,1792]{1,0:T(8,128)(2,1)}, u32[]{:S(2)}, u32[]{:S(2)}) collective-permute-start(bf16[1024,1792]{1,0:T(8,128)(2,1)} %dynamic-slice_bitcast_fusion), channel_id=1, source_target_pairs={{0,8},{8,0},{16,24},{24,16},{1,9},{9,1},{17,25},{25,17},{2,10},{10... | collective-permute-start | bytes 11010056 | tf_op jit(solution)/shard_map/ppermute | solution.py:196
  47.3 56.3 %collective-permute-start.5 = (bf16[8,1040,128]{2,1,0:T(8,128)(2,1)S(1)}, bf16[8,1040,128]{2,1,0:T(8,128)(2,1)}, u32[]{:S(2)}, u32[]{:S(2)}) collective-permute-start(bf16[8,1040,128]{2,1,0:T(8,128)(2,1)S(1)} %all-to-all-done.refs_0_), channel_id=1, source_target_pairs={{0,2},{1,3},{2,4},{3,5},{4,6},{5,7},{8,10},{9,11},{10,12},{11,13},... | collective-permute-start | bytes 6389768 | tf_op jit(solution)/shard_map/ppermute | solution.py:212
  51.4 52.2 %collective-permute-start.4 = (bf16[8,1040,128]{2,1,0:T(8,128)(2,1)S(1)}, bf16[8,1040,128]{2,1,0:T(8,128)(2,1)}, u32[]{:S(2)}, u32[]{:S(2)}) collective-permute-start(bf16[8,1040,128]{2,1,0:T(8,128)(2,1)S(1)} %all-to-all-done.refs_0_), channel_id=1, source_target_pairs={{2,0},{3,1},{4,2},{5,3},{6,4},{7,5},{10,8},{11,9},{12,10},{13,11},... | collective-permute-start | bytes 6389768 | tf_op jit(solution)/shard_map/ppermute | solution.py:212
  54.3 40.9 %collective-permute-start.7 = (bf16[4,128,1792]{2,1,0:T(8,128)(2,1)S(1)}, bf16[4,128,1792]{2,1,0:T(8,128)(2,1)S(1)}, u32[]{:S(2)}, u32[]{:S(2)}) collective-permute-start(bf16[4,128,1792]{2,1,0:T(8,128)(2,1)S(1)} %pad_maximum_fusion.3), channel_id=1, source_target_pairs={{0,1},{1,0},{2,3},{3,2},{4,5},{5,4},{6,7},{7,6},{8,9},{9,8},{10,11... | collective-permute-start | bytes 5505032 | tf_op jit(solution)/shard_map/ppermute | solution.py:204
  103.6 43.2 %collective-permute-start.12 = (bf16[4,256,1792]{2,1,0:T(8,128)(2,1)S(1)}, bf16[4,256,1792]{2,1,0:T(8,128)(2,1)S(1)}, u32[]{:S(2)}, u32[]{:S(2)}) collective-permute-start(bf16[4,256,1792]{2,1,0:T(8,128)(2,1)S(1)} %constant_dynamic-update-slice_fusion.refs_7_), channel_id=1, source_target_pairs={{0,8},{8,0},{16,24},{24,16},{1,9},{9,1},{17,25},{25,17},{2,10},{10... | collective-permute-start | bytes 11010056 | tf_op jit(solution)/shard_map/ppermute | solution.py:196
  103.7 42.4 %collective-permute-start.13 = (bf16[2,256,1792]{2,1,0:T(8,128)(2,1)S(1)}, bf16[2,256,1792]{2,1,0:T(8,128)(2,1)S(1)}, u32[]{:S(2)}, u32[]{:S(2)}) collective-permute-start(bf16[2,256,1792]{2,1,0:T(8,128)(2,1)S(1)} %copy-done.13), channel_id=1, source_target_pairs={{0,16},{8,24},{16,0},{24,8},{1,17},{9,25},{17,1},{25,9},{2,18},{10... | collective-permute-start | bytes 5505032 | tf_op jit(solution)/shard_map/ppermute | solution.py:196
  104.4 42.4 %collective-permute-start.9 = (bf16[128,1792]{1,0:T(8,128)(2,1)S(1)}, bf16[128,1792]{1,0:T(8,128)(2,1)S(1)}, u32[]{:S(2)}, u32[]{:S(2)}) collective-permute-start(bf16[128,1792]{1,0:T(8,128)(2,1)S(1)} %get-tuple-element.42), channel_id=1, source_target_pairs={{0,2},{1,3},{2,4},{3,5},{4,6},{5,7},{6,0},{7,1},{8,10},{9,11},{10,... | collective-permute-start | bytes 1376264 | tf_op jit(solution)/shard_map/ppermute | solution.py:200
  106.8 39.9 %collective-permute-start.10 = (bf16[128,1792]{1,0:T(8,128)(2,1)S(1)}, bf16[128,1792]{1,0:T(8,128)(2,1)S(1)}, u32[]{:S(2)}, u32[]{:S(2)}) collective-permute-start(bf16[128,1792]{1,0:T(8,128)(2,1)S(1)} %get-tuple-element.43), channel_id=1, source_target_pairs={{0,4},{1,5},{2,6},{3,7},{4,0},{5,1},{6,2},{7,3},{8,12},{9,13},{10,... | collective-permute-start | bytes 1376264 | tf_op jit(solution)/shard_map/ppermute | solution.py:200
  107.7 39.0 %collective-permute-start.11 = (bf16[128,1792]{1,0:T(8,128)(2,1)S(1)}, bf16[128,1792]{1,0:T(8,128)(2,1)S(1)}, u32[]{:S(2)}, u32[]{:S(2)}) collective-permute-start(bf16[128,1792]{1,0:T(8,128)(2,1)S(1)} %get-tuple-element.44), channel_id=1, source_target_pairs={{0,6},{1,7},{2,0},{3,1},{4,2},{5,3},{6,4},{7,5},{8,14},{9,15},{10,... | collective-permute-start | bytes 1376264 | tf_op jit(solution)/shard_map/ppermute | solution.py:200
  146.1 61.5 %collective-permute-start.16 = (bf16[2,384,1792]{2,1,0:T(8,128)(2,1)}, bf16[2,384,1792]{2,1,0:T(8,128)(2,1)}, u32[]{:S(2)}, u32[]{:S(2)}) collective-permute-start(bf16[2,384,1792]{2,1,0:T(8,128)(2,1)} %pad_maximum_fusion), channel_id=1, source_target_pairs={{0,16},{8,24},{16,0},{24,8},{1,17},{9,25},{17,1},{25,9},{2,18},{10... | collective-permute-start | bytes 8257544 | tf_op jit(solution)/shard_map/ppermute | solution.py:196
  148.6 59.1 %collective-permute-start.14 = (bf16[8,1040,128]{2,1,0:T(8,128)(2,1)}, bf16[8,1040,128]{2,1,0:T(8,128)(2,1)}, u32[]{:S(2)}, u32[]{:S(2)}) collective-permute-start(bf16[8,1040,128]{2,1,0:T(8,128)(2,1)} %collective-permute-done.5.refs_1_), channel_id=1, source_target_pairs={{2,4},{3,5},{4,6},{5,7},{10,12},{11,13},{12,14},{13,15},{18,20},{1... | collective-permute-start | bytes 6389768 | tf_op jit(solution)/shard_map/ppermute | solution.py:212
  150.6 57.0 %collective-permute-start.15 = (bf16[8,1040,128]{2,1,0:T(8,128)(2,1)}, bf16[8,1040,128]{2,1,0:T(8,128)(2,1)}, u32[]{:S(2)}, u32[]{:S(2)}) collective-permute-start(bf16[8,1040,128]{2,1,0:T(8,128)(2,1)} %collective-permute-done.4.refs_4_), channel_id=1, source_target_pairs={{2,0},{3,1},{4,2},{5,3},{10,8},{11,9},{12,10},{13,11},{18,16},{19,... | collective-permute-start | bytes 6389768 | tf_op jit(solution)/shard_map/ppermute | solution.py:212
  153.4 41.8 %collective-permute-start.17 = (bf16[4,128,1792]{2,1,0:T(8,128)(2,1)}, bf16[4,128,1792]{2,1,0:T(8,128)(2,1)}, u32[]{:S(2)}, u32[]{:S(2)}) collective-permute-start(bf16[4,128,1792]{2,1,0:T(8,128)(2,1)} %pad_maximum_fusion.4), channel_id=1, source_target_pairs={{0,1},{1,0},{2,3},{3,2},{4,5},{5,4},{6,7},{7,6},{8,9},{9,8},{10,11... | collective-permute-start | bytes 5505032 | tf_op jit(solution)/shard_map/ppermute | solution.py:204
  159.0 48.6 %collective-permute-start.19 = (bf16[256,1792]{1,0:T(8,128)(2,1)S(1)}, bf16[256,1792]{1,0:T(8,128)(2,1)S(1)}, u32[]{:S(2)}, u32[]{:S(2)}) collective-permute-start(bf16[256,1792]{1,0:T(8,128)(2,1)S(1)} %dynamic-slice_bitcast_fusion.5), channel_id=1, source_target_pairs={{0,8},{8,0},{16,24},{24,16},{1,9},{9,1},{17,25},{25,17},{2,10},{10... | collective-permute-start | bytes 2752520 | tf_op jit(solution)/shard_map/ppermute | solution.py:196
  208.6 44.0 %collective-permute-start.26 = (bf16[2,256,1792]{2,1,0:T(8,128)(2,1)}, bf16[2,256,1792]{2,1,0:T(8,128)(2,1)S(1)}, u32[]{:S(2)}, u32[]{:S(2)}) collective-permute-start(bf16[2,256,1792]{2,1,0:T(8,128)(2,1)} %get-tuple-element.58), channel_id=1, source_target_pairs={{0,16},{8,24},{16,0},{24,8},{1,17},{9,25},{17,1},{25,9},{2,18},{10... | collective-permute-start | bytes 5505032 | tf_op jit(solution)/shard_map/ppermute | solution.py:196
  227.2 37.4 %collective-permute-start.24 = (bf16[8,640,128]{2,1,0:T(8,128)(2,1)}, bf16[8,640,128]{2,1,0:T(8,128)(2,1)}, u32[]{:S(2)}, u32[]{:S(2)}) collective-permute-start(bf16[8,640,128]{2,1,0:T(8,128)(2,1)} %slice.47), channel_id=1, source_target_pairs={{2,0},{3,1},{10,8},{11,9},{18,16},{19,17},{26,24},{27,25}} | collective-permute-start | bytes 3932168 | tf_op jit(solution)/shard_map/ppermute | solution.py:212
  228.5 36.2 %collective-permute-start.23 = (bf16[8,640,128]{2,1,0:T(8,128)(2,1)}, bf16[8,640,128]{2,1,0:T(8,128)(2,1)}, u32[]{:S(2)}, u32[]{:S(2)}) collective-permute-start(bf16[8,640,128]{2,1,0:T(8,128)(2,1)} %slice.46), channel_id=1, source_target_pairs={{4,6},{5,7},{12,14},{13,15},{20,22},{21,23},{28,30},{29,31}} | collective-permute-start | bytes 3932168 | tf_op jit(solution)/shard_map/ppermute | solution.py:212
  254.6 32.6 %collective-permute-start.30 = (bf16[384,1792]{1,0:T(8,128)(2,1)S(1)}, bf16[384,1792]{1,0:T(8,128)(2,1)S(1)}, u32[]{:S(2)}, u32[]{:S(2)}) collective-permute-start(bf16[384,1792]{1,0:T(8,128)(2,1)S(1)} %copy-done.1), channel_id=1, source_target_pairs={{0,16},{8,24},{16,0},{24,8},{1,17},{9,25},{17,1},{25,9},{2,18},{10... | collective-permute-start | bytes 4128776 | tf_op jit(solution)/shard_map/ppermute | solution.py:196
  285.5 52.6 %collective-permute-start.28 = (bf16[640,1792]{1,0:T(8,128)(2,1)}, bf16[640,1792]{1,0:T(8,128)(2,1)}, u32[]{:S(2)}, u32[]{:S(2)}) collective-permute-start(bf16[640,1792]{1,0:T(8,128)(2,1)} %shard_map.48.refs_4_), channel_id=1, source_target_pairs={{0,16},{8,24},{16,0},{24,8},{1,17},{9,25},{17,1},{25,9},{2,18},{10... | collective-permute-start | bytes 6881288 | tf_op jit(solution)/shard_map/ppermute | solution.py:196
  (31 other events, 507.1 us)
